TPU v7x, 32 devices: a whole 2x2x4 slice. The times are simulated.
32 devices in a mesh: det: 4 (over x, core), pix: 8 (over z, y).
Axes of the slice: x: 2, y: 2, z: 4, core: 2. Of those that a mesh axis runs over, the one named last changes fastest.
Arguments:
- timestream: float32 [32, 256, 128], P(('det', 'pix')), may hold values from -48 to 48
- weights: bfloat16 [32, 256, 128, 256], P(('det', 'pix')), may hold values from 0.0004 to 1
- block_owner: int32 [32, 256, 1], P(('det', 'pix')), may hold values from 0 to 7; in each aligned block of 256 rows (0 to 255, 256 to 511, ..., all dimensions but the last counted through in order) at most 64 rows name the same one
- block_local: int32 [32, 256], P(('det', 'pix')), may hold values from 0 to 63
- baseline_of: int32 [32, 256], P(('det', 'pix')), may hold values from 0 to 127, never falling along the last dimension, each value on 1 to 3 neighbouring positions
Outputs:
- offset_levels: float32 [32, 128], P(('det', 'pix'))
- leftover_error: float32 [32, 128], P(('det', 'pix'))
Inputs may be any that keep to these rules, and one draw needn't show every extreme that they name: `block_owner`: among the 256 blocks of one timestream row at most 64 name the same owner, and in every row some owner is named by exactly 64. `baseline_of`: along each row the baseline index never falls; each of the 128 baselines covers 1 to 3 blocks, and some covers exactly 3.
All inputs are finite; a program needn't handle non-finite values.
Results may differ from a plain program's by a relative error of at most 0.013.
Values may be sent and summed in bfloat16 or wider, within the bound.
No kernel may reach another device: no remote copies, remote signals or barrier semaphores. Data moves between devices by JAX's collectives and lax.ppermute only.
A program may use at most 64 MiB of HBM per device.

v0:
```python
import jax
import jax.numpy as jnp
from jax import lax
from jax.sharding import PartitionSpec as P

PB_DEV = 64
ITERS = 2
NBASE_DEV = 128


def squares_total(leftover_error):
    return lax.psum(jnp.sum(leftover_error * leftover_error), ("det", "pix"))


def body(timestream, weights, block_owner, block_local, baseline_of):
    series_data = timestream[0]
    weight_rows = weights[0]
    owners = block_owner[0, :, 0]
    local_idx = block_local[0]
    segments_row = baseline_of[0]
    blocks = weight_rows.shape[0]
    samples = weight_rows.shape[1]
    pixels = weight_rows.shape[2]
    pix_count = lax.axis_size("pix")
    capacity = blocks // 4
    slot_count = pix_count * capacity
    highest = lax.Precision.HIGHEST
    base_hot = (segments_row[:, None] == jnp.arange(NBASE_DEV)[None, :]).astype(jnp.float32)
    owner_hot = (owners[:, None] == jnp.arange(pix_count)[None, :]).astype(jnp.int32)
    before = jnp.cumsum(owner_hot, axis=0) - owner_hot
    slot_position = jnp.sum(before * owner_hot, axis=1)
    slot_ids = owners * capacity + slot_position
    slot_match = slot_ids[None, :] == jnp.arange(slot_count)[:, None]
    slot_hot = slot_match.astype(jnp.float32)
    send_idx = jnp.sum(jnp.where(slot_match, local_idx[None, :] + 1, 0), axis=1) - 1
    incoming_idx = lax.all_to_all(send_idx, "pix", split_axis=0, concat_axis=0, tiled=True)
    received_onehot = (incoming_idx[None, :] == jnp.arange(PB_DEV)[:, None]).astype(jnp.float32)

    def bin_terms(terms):
        outgoing = jnp.einsum("cb,kbp->kcp", slot_hot, terms, precision=highest)
        arrived = lax.all_to_all(
            outgoing.astype(jnp.bfloat16), "pix", split_axis=1, concat_axis=1, tiled=True
        ).astype(outgoing.dtype)
        owned = jnp.einsum("qc,kcp->kqp", received_onehot, arrived, precision=highest)
        return lax.psum(owned.astype(jnp.bfloat16), "det").astype(jnp.float32)

    incoming_indicator_transposed = (incoming_idx[:, None] == jnp.arange(PB_DEV)[None, :]).astype(
        jnp.bfloat16
    )
    slot_hot_t = (slot_ids[:, None] == jnp.arange(slot_count)[None, :]).astype(jnp.bfloat16)

    def distribute_skymap(map_b):
        gathered_result = jnp.dot(
            incoming_indicator_transposed, map_b, preferred_element_type=jnp.float32
        ).astype(jnp.bfloat16)
        arrived = lax.all_to_all(gathered_result, "pix", split_axis=0, concat_axis=0, tiled=True)
        return jnp.dot(slot_hot_t, arrived, preferred_element_type=jnp.float32).astype(jnp.bfloat16)

    def project_map(map_b):
        per_block = distribute_skymap(map_b)
        return jnp.einsum("bsp,bp->bs", weight_rows, per_block, preferred_element_type=jnp.float32)

    def collapse(series):
        return jnp.dot(jnp.sum(series, axis=1), base_hot, precision=highest)

    unit_row_vector = jnp.ones((pixels,), jnp.bfloat16)
    row_sums = jnp.einsum(
        "bsp,p->bs", weight_rows, unit_row_vector, preferred_element_type=jnp.float32
    ).astype(jnp.bfloat16)
    stacked = jnp.stack([row_sums, series_data.astype(jnp.bfloat16)])
    first_terms = jnp.einsum(
        "kbs,bsp->kbp", stacked, weight_rows, preferred_element_type=jnp.float32
    )
    totals = bin_terms(first_terms)
    hit_sums = totals[0]
    sky_map = totals[1] / (hit_sums + 1.0)
    projected = project_map(sky_map.astype(jnp.bfloat16))
    equation_target = collapse(series_data - projected) / samples
    offset_levels = jnp.zeros_like(equation_target)
    leftover_error = equation_target
    descent_heading = equation_target
    current_norm = squares_total(leftover_error)
    for iteration in range(ITERS):
        expand_per_block = jnp.dot(base_hot, descent_heading, precision=highest)
        normal_series = jnp.broadcast_to(expand_per_block[:, None], (blocks, samples))
        normal_terms = jnp.einsum(
            "bs,bsp->bp",
            normal_series.astype(jnp.bfloat16),
            weight_rows,
            preferred_element_type=jnp.float32,
        )
        binned = bin_terms(normal_terms[None])[0]
        sky = binned / (hit_sums + 1.0)
        proj = project_map(sky.astype(jnp.bfloat16))
        image = collapse(normal_series - proj) / samples + descent_heading
        descent_factor = current_norm / lax.psum(jnp.sum(descent_heading * image), ("det", "pix"))
        offset_levels = offset_levels + descent_factor * descent_heading
        leftover_error = leftover_error - descent_factor * image
        norm_next = squares_total(leftover_error)
        descent_heading = leftover_error + norm_next / current_norm * descent_heading
        current_norm = norm_next
    return (offset_levels[None], leftover_error[None])


def solution(mesh):
    placed = (
        P(("det", "pix"), None, None),
        P(("det", "pix"), None, None, None),
        P(("det", "pix"), None, None),
        P(("det", "pix"), None),
        P(("det", "pix"), None),
    )
    return jax.shard_map(
        body,
        mesh=mesh,
        in_specs=placed,
        out_specs=(P(("det", "pix"), None), P(("det", "pix"), None)),
        check_vma=False,
    )
```

profile of v0, /device:TPU:0, one launch (start us, length us, event | category | flops | bytes accessed | tf_op | source)
XLA Modules:
  0.0 359.6 jit_solution(8274988202841696218)
XLA Ops:
  11.7 7.3 %all-to-all-start = ((s32[8,64,1]{1,2,0:T(1,128)}), s32[8,64,1]{1,2,0:T(1,128)S(1)}, u32[]{:S(2)}, u32[]{:S(2)}) async-start(s32[8,64,1]{1,2,0:T(1,128)} %bitcast.6), calls=%async_computation | async-start | bytes 8192 | tf_op jit(solution)/shard_map/all_to_all | solution.py:36
  19.0 8.2 %fusion.12 = f32[1,256,128]{2,0,1:T(1,128)S(1)} fusion(bf16[1,256,128,256]{3,2,1,0:T(8,128)(2,1)} %param.6), kind=kOutput, calls=%fused_computation.12 | convolution fusion | flops 16777216 | bytes 16908288 | tf_op jit(solution)/shard_map/bsp,p->bs/dot_general | solution.py:67
  29.5 2.3 fusion.15
  33.9 6.0 %all-to-all-start.1 = ((bf16[2,512,256]{2,0,1:T(2,128)(2,1)}), bf16[2,512,256]{2,0,1:T(2,128)(2,1)S(1)}, u32[]{:S(2)}, u32[]{:S(2)}) async-start(bf16[2,512,256]{2,0,1:T(2,128)(2,1)} %copy.26), calls=%async_computation.1 | async-start | bytes 1048576 | tf_op jit(solution)/shard_map/all_to_all | solution.py:41
  41.2 12.7 %all-to-all-done.1 = bf16[2,512,256]{2,0,1:T(2,128)(2,1)S(1)} async-done(((bf16[2,512,256]{2,0,1:T(2,128)(2,1)}), bf16[2,512,256]{2,0,1:T(2,128)(2,1)S(1)}, u32[]{:S(2)}, u32[]{:S(2)}) %all-to-all-start.1) | async-done | bytes 524320 | tf_op jit(solution)/shard_map/all_to_all | solution.py:41
  54.8 30.2 %all-reduce.3.cloned.1.call-done = bf16[2,64,256]{2,1,0:T(8,128)(2,1)} async-done(((bf16[2,64,256]{2,1,0:T(8,128)(2,1)}), bf16[2,64,256]{2,1,0:T(8,128)(2,1)}) %all-reduce.3.cloned.1.call-update) | async-done | bytes 65552 | tf_op jit(solution)/shard_map/psum | solution.py:45
  86.1 13.5 %all_to_all.57 = bf16[8,64,256]{2,1,0:T(8,128)(2,1)S(1)} all-to-all(bf16[8,64,256]{2,1,0:T(8,128)(2,1)S(1)} %bitcast.157), channel_id=1, replica_groups=mesh['det'=4,'pix'=8] {'pix'}, dimensions={0} | all-to-all | bytes 524288 | tf_op jit(solution)/shard_map/all_to_all | solution.py:56
  100.0 10.2 %fusion.8 = f32[256,1,128]{2,1,0:T(1,128)S(1)} fusion(bf16[1,256,128,256]{3,2,1,0:T(8,128)(2,1)} %param.6, bf16[256,256,1]{1,0,2:T(8,128)(2,1)S(1)} %fusion.20), kind=kOutput, calls=%fused_computation.8 | convolution fusion | flops 16777216 | bytes 17039360 | tf_op jit(solution)/shard_map/bsp,bp->bs/dot_general | solution.py:61
  110.7 8.2 %fusion.6 = f32[256,1,256]{2,1,0:T(1,128)S(1)} fusion(bf16[1,256,128,256]{3,2,1,0:T(8,128)(2,1)} %param.6, bf16[256]{0:T(256)(128)(2,1)S(1)} %convert_element_type.136), kind=kOutput, calls=%fused_computation.6 | convolution fusion | flops 16777216 | bytes 17039872 | tf_op jit(solution)/shard_map/bs,bsp->bp/dot_general | solution.py:86
  120.5 2.2 reduce.6
  122.8 11.3 %all_to_all.58 = bf16[8,2,8192]{2,1,0:T(2,128)(2,1)S(1)} all-to-all(bf16[8,2,8192]{2,1,0:T(2,128)(2,1)S(1)} %reshape.131), channel_id=1, replica_groups=mesh['det'=4,'pix'=8] {'pix'}, dimensions={0} | all-to-all | bytes 524288 | tf_op jit(solution)/shard_map/all_to_all | solution.py:41
  134.6 10.3 %psum.51 = bf16[1,64,256]{2,1,0:T(8,128)(2,1)S(1)} all-reduce(bf16[1,64,256]{2,1,0:T(8,128)(2,1)S(1)} %fusion.24), channel_id=1, replica_groups=mesh['det'=4,'pix'=8] {'det'}, use_global_device_ids=true, to_apply=%region_8.9 | all-reduce | flops 16384 | bytes 65536 | tf_op jit(solution)/shard_map/psum | solution.py:45
  145.1 12.0 %all_to_all.59 = bf16[8,64,256]{2,1,0:T(8,128)(2,1)S(1)} all-to-all(bf16[8,64,256]{2,1,0:T(8,128)(2,1)S(1)} %bitcast.155), channel_id=1, replica_groups=mesh['det'=4,'pix'=8] {'pix'}, dimensions={0} | all-to-all | bytes 524288 | tf_op jit(solution)/shard_map/all_to_all | solution.py:56
  157.4 10.2 %fusion.4 = f32[256,1,128]{2,1,0:T(1,128)S(1)} fusion(bf16[1,256,128,256]{3,2,1,0:T(8,128)(2,1)} %param.6, bf16[256,256,1]{1,0,2:T(8,128)(2,1)S(1)} %fusion.21), kind=kOutput, calls=%fused_computation.4 | convolution fusion | flops 16777216 | bytes 17039360 | tf_op jit(solution)/shard_map/bsp,bp->bs/dot_general | solution.py:61
  168.7 39.0 %all-reduce = (f32[]{:T(128)}, f32[]{:T(128)}) all-reduce(f32[]{:T(128)} %get-tuple-element.3, f32[]{:T(128)} %get-tuple-element.2), channel_id=1, replica_groups=mesh['det'=4,'pix'=8] {'det','pix'}, use_global_device_ids=true, to_apply=%region_7.8 | all-reduce | flops 2 | bytes 16 | tf_op jit(solution)/shard_map/psum | solution.py:12
  209.6 40.9 %psum.53 = f32[]{:T(128)} all-reduce(f32[]{:T(128)} %get-tuple-element.6), channel_id=1, replica_groups=mesh['det'=4,'pix'=8] {'det','pix'}, use_global_device_ids=true, to_apply=%region_13.14 | all-reduce | flops 1 | bytes 8 | tf_op jit(solution)/shard_map/psum | solution.py:12
  252.0 8.2 %fusion.2 = f32[256,1,256]{2,1,0:T(1,128)S(1)} fusion(bf16[1,256,128,256]{3,2,1,0:T(8,128)(2,1)} %param.6, bf16[256]{0:T(256)(128)(2,1)S(1)} %convert_element_type.148), kind=kOutput, calls=%fused_computation.2 | convolution fusion | flops 16777216 | bytes 17039872 | tf_op jit(solution)/shard_map/bs,bsp->bp/dot_general | solution.py:86
  261.3 2.2 reduce.7
  263.6 12.8 %all_to_all.60 = bf16[8,2,8192]{2,1,0:T(2,128)(2,1)S(1)} all-to-all(bf16[8,2,8192]{2,1,0:T(2,128)(2,1)S(1)} %reshape.133), channel_id=1, replica_groups=mesh['det'=4,'pix'=8] {'pix'}, dimensions={0} | all-to-all | bytes 524288 | tf_op jit(solution)/shard_map/all_to_all | solution.py:41
  276.8 10.3 %psum.54 = bf16[1,64,256]{2,1,0:T(8,128)(2,1)S(1)} all-reduce(bf16[1,64,256]{2,1,0:T(8,128)(2,1)S(1)} %fusion.25), channel_id=1, replica_groups=mesh['det'=4,'pix'=8] {'det'}, use_global_device_ids=true, to_apply=%region_14.15 | all-reduce | flops 16384 | bytes 65536 | tf_op jit(solution)/shard_map/psum | solution.py:45
  288.0 3.4 all-to-all-start.6
  291.4 9.0 %all-to-all-done.6 = bf16[8,64,256]{2,1,0:T(8,128)(2,1)S(1)} async-done(((bf16[8,64,256]{2,1,0:T(8,128)(2,1)}), bf16[8,64,256]{2,1,0:T(8,128)(2,1)S(1)}, u32[]{:S(2)}, u32[]{:S(2)}) %all-to-all-start.6) | async-done | bytes 262176 | tf_op jit(solution)/shard_map/all_to_all | solution.py:56
  300.7 10.2 %fusion = f32[256,1,128]{2,1,0:T(1,128)S(1)} fusion(bf16[1,256,128,256]{3,2,1,0:T(8,128)(2,1)} %param.6, bf16[256,256,1]{1,0,2:T(8,128)(2,1)S(1)} %fusion.22), kind=kOutput, calls=%fused_computation | convolution fusion | flops 16777216 | bytes 17039360 | tf_op jit(solution)/shard_map/bsp,bp->bs/dot_general | solution.py:61
  312.0 38.9 %psum.55 = f32[]{:T(128)} all-reduce(f32[]{:T(128)} %get-tuple-element.9), channel_id=1, replica_groups=mesh['det'=4,'pix'=8] {'det','pix'}, use_global_device_ids=true, to_apply=%region_17.18 | all-reduce | flops 1 | bytes 8 | tf_op jit(solution)/shard_map/psum | solution.py:96
  (61 shorter events, 22.0 us)
Async XLA Ops:
  7.2 20.2 %copy-start.1 = (f32[1,256,128]{2,1,0:T(8,128)S(1)}, f32[1,256,128]{2,1,0:T(8,128)}, u32[]{:S(2)}) copy-start(f32[1,256,128]{2,1,0:T(8,128)} %param.5) | copy-start | bytes 393220
  11.7 22.3 %all-to-all-start = ((s32[8,64,1]{1,2,0:T(1,128)}), s32[8,64,1]{1,2,0:T(1,128)S(1)}, u32[]{:S(2)}, u32[]{:S(2)}) async-start(s32[8,64,1]{1,2,0:T(1,128)} %bitcast.6), calls=%async_computation | async-start | bytes 8192 | tf_op jit(solution)/shard_map/all_to_all | solution.py:36
  19.0 10.5 %copy-start = (bf16[1,256,128,256]{3,2,1,0:T(8,128)(2,1)S(1)}, bf16[1,256,128,256]{3,2,1,0:T(8,128)(2,1)}, u32[]{:S(2)}) copy-start(bf16[1,256,128,256]{3,2,1,0:T(8,128)(2,1)} %param.6) | copy-start | bytes 50331652
  31.8 78.5 %copy-start.2 = (s32[1,256]{1,0:T(1,128)S(1)}, s32[1,256]{1,0:T(1,128)}, u32[]{:S(2)}) copy-start(s32[1,256]{1,0:T(1,128)} %param.9) | copy-start | bytes 3076
  33.9 20.0 %all-to-all-start.1 = ((bf16[2,512,256]{2,0,1:T(2,128)(2,1)}), bf16[2,512,256]{2,0,1:T(2,128)(2,1)S(1)}, u32[]{:S(2)}, u32[]{:S(2)}) async-start(bf16[2,512,256]{2,0,1:T(2,128)(2,1)} %copy.26), calls=%async_computation.1 | async-start | bytes 1048576 | tf_op jit(solution)/shard_map/all_to_all | solution.py:41
  39.9 45.1 %all-reduce.3.cloned.1.call-start = ((), (), s32[]{:S(2)}) async-start(), calls=%async_computation.7 | async-start | bytes 131072 | tf_op jit(solution)/shard_map/psum | solution.py:45
  288.0 12.4 %all-to-all-start.6 = ((bf16[8,64,256]{2,1,0:T(8,128)(2,1)}), bf16[8,64,256]{2,1,0:T(8,128)(2,1)S(1)}, u32[]{:S(2)}, u32[]{:S(2)}) async-start(bf16[8,64,256]{2,1,0:T(8,128)(2,1)} %bitcast.48), calls=%async_computation.6 | async-start | bytes 524288 | tf_op jit(solution)/shard_map/all_to_all | solution.py:56
Sparse Core Ops, SparseCore 0:
  54.9 30.0 all-reduce.2
where the time goes:
time: 361 us; the launch traced here: 360 us
  blocking collectives  189 us (52%)
  matrix products  65.7 us (18%)
  waiting for transfers between devices  52 us (14%)
  between operations  18.1 us (5%)
  starting transfers between devices  16.7 us (5%)
  other arithmetic  11.2 us (3%)
  local copies, waits for them, and re-layouts  6.85 us (2%)
    psum x2, blocking collectives, squares_total(): return lax.psum(jnp.sum(leftover_error * leftover_error), ('det', 'pix'))  80 us
    psum x1, blocking collectives, body(): lax.psum(jnp.sum(descent_heading * image), ('det', 'pix'))  38.9 us
    dot_general x3, matrix products, project_map(): jnp.einsum('bsp,bp->bs', weight_rows, per_block, preferred_element_type=j...  30.6 us
    psum x1, waiting for transfers between devices, bin_terms(): return lax.psum(owned.astype(jnp.bfloat16), 'det').astype(jnp.float32)  30.2 us
    all_to_all x2, blocking collectives, distribute_skymap(): lax.all_to_all(gathered_result, 'pix', split_axis=0, concat_axis=0, tiled...  25.6 us
    all_to_all x2, blocking collectives, bin_terms(): lax.all_to_all(outgoing.astype(jnp.bfloat16), 'pix', split_axis=1, concat...  24.1 us
    psum x2, blocking collectives, bin_terms(): return lax.psum(owned.astype(jnp.bfloat16), 'det').astype(jnp.float32)  20.5 us
    dot_general x2, matrix products, body(): jnp.einsum('bs,bsp->bp', normal_series.astype(jnp.bfloat16), weight_rows,...  16.3 us
  transfers between devices with their start and end apart: 4, of which 3 were waited for; matrix products, arithmetic and copies ran while one was open for 4% of the time, Pallas kernels for 0%

commit v1 on v0

v1 whole, which is shorter than its diff:
```python
import functools

import jax
import jax.numpy as jnp
from jax import lax
from jax.experimental import pallas as pl
from jax.experimental.pallas import tpu as pltpu
from jax.sharding import PartitionSpec as P

PB_DEV = 64
NBASE_DEV = 128
CAP = 64
LANES = 128
AXES = ("det", "pix")
BF = jnp.bfloat16
F32 = jnp.float32
VMEM_LIMIT = 48 * 1024 * 1024


def dot_nn(a, b):
    return lax.dot_general(a, b, (((1,), (0,)), ((), ())), preferred_element_type=F32)


def dot_nt(a, b):
    return lax.dot_general(a, b, (((1,), (1,)), ((), ())), preferred_element_type=F32)


def split3(v):
    a = v.astype(BF)
    left = v - a.astype(F32)
    b = left.astype(BF)
    c = (left - b.astype(F32)).astype(BF)
    return a, b, c


def iota(shape, dim):
    return lax.broadcasted_iota(jnp.int32, shape, dim)


def bin_kernel(n_det, n_pix, group, ts_ref, w_ref, own_ref, loc_ref, base_ref, out_ref, col_s, hit_s, dat_s):
    step = pl.program_id(0)
    blocks, samples = ts_ref.shape[1], ts_ref.shape[2]
    pixels = w_ref.shape[3]
    row = iota((8, samples), 0)
    ones = jnp.ones((8, pixels), BF)
    lhs = []
    for j in range(group):
        r = dot_nt(ones, w_ref[0, j])
        u = jnp.broadcast_to(ts_ref[0, pl.ds(step * group + j, 1), :], (8, samples))
        lhs.append(jnp.where(row == 0, r, jnp.where(row == 1, u, 1.0)).astype(BF))
    for j in range(group):
        t = dot_nn(lhs[j], w_ref[0, j])
        where = pl.ds(step * group + j, 1)
        hit_s[where, :] = t[0:1]
        dat_s[where, :] = t[1:2]
        col_s[where, :] = t[2:3]

    @pl.when(step == pl.num_programs(0) - 1)
    def _():
        pch = pixels // n_det
        half = pch // 2
        wide = n_pix * LANES
        own = own_ref[0]
        loc_row = loc_ref[...].astype(F32).astype(BF)
        base_row = base_ref[...].astype(F32).astype(BF)
        eye = (iota((blocks, blocks), 0) == iota((blocks, blocks), 1)).astype(F32).astype(BF)
        loc = dot_nt(eye, jnp.broadcast_to(loc_row, (8, blocks)))[:, 0:1].astype(jnp.int32)
        tri = (iota((blocks, blocks), 1) < iota((blocks, blocks), 0)).astype(F32).astype(BF)
        own_hot = (own == iota((blocks, LANES), 1)).astype(F32)
        before = dot_nn(tri, own_hot.astype(BF))
        pos = jnp.sum(before * own_hot, axis=1, keepdims=True).astype(jnp.int32)
        lane = iota((blocks, wide), 1)

        def hot(target):
            return (lane == target).astype(F32).astype(BF)

        slot_lo, slot_hi = hot(own * LANES + pos), hot(own * LANES + PB_DEV + pos)
        pb_lo, pb_hi = hot(own * LANES + loc), hot(own * LANES + PB_DEV + loc)
        col_t = col_s[...].T.astype(BF)
        hit_t = hit_s[...].T.astype(BF)
        dat_t = dat_s[...].T.astype(BF)
        both = (dot_nn(col_t, slot_lo) + dot_nn(hit_t, pb_hi)).astype(BF)
        first = jnp.concatenate([dat_t[d * pch : d * pch + half] for d in range(n_det)], axis=0)
        second = jnp.concatenate([dat_t[d * pch + half : (d + 1) * pch] for d in range(n_det)], axis=0)
        data = (dot_nn(first, pb_lo) + dot_nn(second, pb_hi)).astype(BF)
        where = dot_nn(jnp.broadcast_to(loc_row, (8, blocks)), slot_lo) + dot_nn(jnp.broadcast_to(base_row, (8, blocks)), slot_hi)

        base_t = iota((NBASE_DEV, blocks), 0) == base_ref[...]
        base_hot = base_t.astype(F32).astype(BF)
        t0, t1, t2 = split3(ts_ref[0])
        per_base = dot_nn(base_hot, t0) + dot_nn(base_hot, t1) + dot_nn(base_hot, t2)
        b0, b1, b2 = split3(per_base)
        one = jnp.ones((8, samples), BF)
        total = dot_nt(one, b0) + dot_nt(one, b1) + dot_nt(one, b2)
        s0, s1, s2 = split3(total)
        count = dot_nt(jnp.ones((8, blocks), BF), base_hot)
        r16 = iota((16, LANES), 0)

        def rep(v):
            v = v.astype(F32)
            return jnp.concatenate([v, v], axis=0)

        own_rows = jnp.where(r16 == 1, rep(s0), jnp.where(r16 == 2, rep(s1), jnp.where(r16 == 3, rep(s2), rep(count))))
        for o in range(n_pix):
            cols = slice(o * LANES, (o + 1) * LANES)
            tile = jnp.where(r16 == 0, rep(where[:, cols]), own_rows).astype(BF)
            for d in range(n_det):
                to = d * n_pix + o
                out_ref[to, 0:pch, :] = both[d * pch : (d + 1) * pch, cols]
                out_ref[to, pch : pch + half, :] = data[d * half : (d + 1) * half, cols]
                out_ref[to, pch + half :, :] = tile


def project(col_t, sky_t, pb_hot, base_hot, row_hot):
    spread = dot_nn(sky_t.astype(BF), pb_hot)
    per_slot = jnp.sum(col_t.astype(F32) * spread, axis=0, keepdims=True)
    parts = [jnp.where(row_hot, p.astype(F32), 0.0).astype(BF) for p in split3(per_slot)]
    return dot_nt(parts[0], base_hot) + dot_nt(parts[1], base_hot) + dot_nt(parts[2], base_hot)


def bin_amps(amps, col_t, pb_hot, base_hot, row_hot):
    a0, a1, a2 = split3(amps)
    spread = dot_nn(a0, base_hot) + dot_nn(a1, base_hot) + dot_nn(a2, base_hot)
    per_slot = jnp.sum(jnp.where(row_hot, spread, 0.0), axis=0, keepdims=True)
    terms = col_t.astype(F32) * per_slot
    high = terms.astype(BF)
    low = (terms - high.astype(F32)).astype(BF)
    return dot_nt(high, pb_hot) + dot_nt(low, pb_hot)


def hots(idx_ref):
    slots = idx_ref.shape[1]
    pb_hot = (iota((PB_DEV, slots), 0).astype(F32) == idx_ref[0:1, :]).astype(F32).astype(BF)
    base_hot = (iota((NBASE_DEV, slots), 0).astype(F32) == idx_ref[1:2, :]).astype(F32).astype(BF)
    return pb_hot, base_hot


def row_mask(rows, slots):
    return iota((rows, slots), 1) // CAP == iota((rows, slots), 0)


def owner_kernel(pch, got_ref, send_ref, col_ref, idx_ref, inv_ref, base_ref, count_ref):
    rows = got_ref.shape[0]
    half = pch // 2
    low = iota((pch, LANES), 1) < CAP
    low8 = iota((16, LANES), 1) < CAP
    hits = jnp.zeros((pch, LANES), F32)
    data = jnp.zeros((half, LANES), F32)
    for i in range(rows // 2):
        a, b = got_ref[2 * i, 0:pch, :].astype(F32), got_ref[2 * i + 1, 0:pch, :].astype(F32)
        hits = hits + a + b
        data = data + got_ref[2 * i, pch : pch + half, :].astype(F32) + got_ref[2 * i + 1, pch : pch + half, :].astype(F32)
        cols = slice(i * LANES, (i + 1) * LANES)
        col_ref[:, cols] = jnp.where(low, a, pltpu.roll(b, CAP, 1)).astype(BF)
        ta, tb = got_ref[2 * i, pch + half :, :].astype(F32), got_ref[2 * i + 1, pch + half :, :].astype(F32)
        pb = jnp.where(low8, ta, pltpu.roll(tb, CAP, 1))
        base = jnp.where(low8, pltpu.roll(ta, CAP, 1), tb)
        idx_ref[0:1, cols] = pb[0:1]
        idx_ref[1:2, cols] = base[0:1]
        for g, t in ((2 * i, ta), (2 * i + 1, tb)):
            base_ref[g : g + 1, :] = t[1:2] + t[2:3] + t[3:4]
            count_ref[g : g + 1, :] = t[4:5]
    inv = 1.0 / (hits[:, CAP:] + 1.0)
    inv_ref[...] = inv
    sky = jnp.concatenate([data[:, :PB_DEV], data[:, PB_DEV:]], axis=0) * inv
    pb_hot, base_hot = hots(idx_ref)
    part = project(col_ref[...], sky, pb_hot, base_hot, row_mask(rows, col_ref.shape[1])).astype(BF)
    for g in range(rows):
        send_ref[g] = part


def total_of(got_ref):
    acc = got_ref[0].astype(F32)
    for g in range(1, got_ref.shape[0]):
        acc = acc + got_ref[g].astype(F32)
    return acc


def first_kernel(samples, got_ref, col_ref, idx_ref, inv_ref, base_ref, send_ref, rhs_ref):
    rhs = (base_ref[...] - total_of(got_ref)) * (1.0 / samples)
    rhs_ref[...] = rhs
    pb_hot, base_hot = hots(idx_ref)
    row_hot = row_mask(rhs.shape[0], col_ref.shape[1])
    binned = bin_amps(rhs, col_ref[...], pb_hot, base_hot, row_hot)
    part = project(col_ref[...], binned * inv_ref[...], pb_hot, base_hot, row_hot).astype(BF)
    for g in range(send_ref.shape[0]):
        send_ref[g] = part


def second_kernel(samples, got_ref, col_ref, idx_ref, inv_ref, rhs_ref, count_ref, send_ref, state_ref):
    rhs = rhs_ref[...]
    more = count_ref[...] + 1.0
    image = more * rhs - total_of(got_ref) * (1.0 / samples)
    rr = jnp.sum(rhs * rhs)
    alpha = rr / jnp.sum(rhs * image)
    levels = alpha * rhs
    error = rhs - alpha * image
    new = jnp.sum(error * error)
    heading = error + (new / rr) * rhs
    curve = jnp.sum(more * heading * heading)
    pb_hot, base_hot = hots(idx_ref)
    rows = rhs.shape[0]
    row_hot = row_mask(rows, col_ref.shape[1])
    binned = bin_amps(heading, col_ref[...], pb_hot, base_hot, row_hot)
    sky = binned * inv_ref[...]
    quad = jnp.sum(binned * sky)
    part = project(col_ref[...], sky, pb_hot, base_hot, row_hot)
    for g in range(rows):
        send_ref[g, 0:1, 0:LANES] = part[g : g + 1]
        send_ref[g, 0:1, LANES:] = jnp.full((1, LANES), quad, F32)
    state_ref[0] = levels
    state_ref[1] = error
    state_ref[2] = heading
    state_ref[3] = more * heading
    state_ref[4] = jnp.full((rows, LANES), new, F32)
    state_ref[5] = jnp.full((rows, LANES), curve, F32)


def last_kernel(samples, n_pix, got_ref, state_ref, levels_ref, error_ref):
    me = lax.axis_index("det") * n_pix + lax.axis_index("pix")
    acc = got_ref[0]
    for g in range(1, got_ref.shape[0]):
        acc = acc + got_ref[g]
    acc = acc * (1.0 / samples)
    mine = [state_ref[k, pl.ds(me, 1), :] for k in range(6)]
    levels, error, heading, scaled, new, curve = mine
    image = scaled - acc[:, 0:LANES]
    alpha = new / (curve - acc[:, LANES:])
    levels_ref[...] = levels + alpha * heading
    error_ref[...] = error - alpha * image


def call(kernel, outs, *args, **kw):
    vmem = pl.BlockSpec(memory_space=pltpu.VMEM)
    return pl.pallas_call(
        kernel,
        out_shape=outs,
        in_specs=[vmem] * len(args),
        out_specs=[vmem] * len(outs),
        compiler_params=pltpu.CompilerParams(vmem_limit_bytes=VMEM_LIMIT),
        **kw,
    )(*args)


def exchange(x):
    return lax.all_to_all(x, AXES, split_axis=0, concat_axis=0, tiled=True)


def body(timestream, weights, block_owner, block_local, baseline_of):
    n_det, n_pix = lax.axis_size("det"), lax.axis_size("pix")
    rows = n_det * n_pix
    _, blocks, samples, pixels = weights.shape
    pch = pixels // n_det
    slots = rows * CAP
    group = 16
    whole = lambda *shape: pl.BlockSpec(shape, lambda i: (0,) * len(shape))
    tall = pch + pch // 2 + 16
    sent = pl.pallas_call(
        functools.partial(bin_kernel, n_det, n_pix, group),
        grid=(blocks // group,),
        out_shape=jax.ShapeDtypeStruct((rows, tall, LANES), BF),
        in_specs=[
            whole(1, blocks, samples),
            pl.BlockSpec((1, group, samples, pixels), lambda i: (0, i, 0, 0)),
            whole(1, blocks, 1),
            whole(1, blocks),
            whole(1, blocks),
        ],
        out_specs=whole(rows, tall, LANES),
        scratch_shapes=[pltpu.VMEM((blocks, pixels), F32)] * 3,
        compiler_params=pltpu.CompilerParams(vmem_limit_bytes=VMEM_LIMIT, dimension_semantics=("arbitrary",)),
    )(timestream, weights, block_owner, block_local, baseline_of)
    got = exchange(sent)
    shape = jax.ShapeDtypeStruct
    everyone = shape((rows, rows, NBASE_DEV), BF)
    vector = shape((rows, NBASE_DEV), F32)
    part, col_t, idx, inv, base, count = call(
        functools.partial(owner_kernel, pch),
        [everyone, shape((pch, slots), BF), shape((8, slots), F32), shape((pch, PB_DEV), F32), vector, vector],
        got,
    )
    part, rhs = call(
        functools.partial(first_kernel, samples), [everyone, vector], exchange(part), col_t, idx, inv, base
    )
    part, state = call(
        functools.partial(second_kernel, samples),
        [shape((rows, 1, 2 * LANES), F32), shape((6, rows, NBASE_DEV), F32)],
        exchange(part), col_t, idx, inv, rhs, count,
    )
    own = shape((1, NBASE_DEV), F32)
    return tuple(call(functools.partial(last_kernel, samples, n_pix), [own, own], exchange(part), state))


def solution(mesh):
    placed = (
        P(AXES, None, None),
        P(AXES, None, None, None),
        P(AXES, None, None),
        P(AXES, None),
        P(AXES, None),
    )
    return jax.shard_map(
        body,
        mesh=mesh,
        in_specs=placed,
        out_specs=(P(AXES, None), P(AXES, None)),
        check_vma=False,
    )
```

time: 361 us -> 92.7 us (0.26)
  blocking collectives: 189 us -> 66.8 us
  matrix products: 65.7 us -> 0 us
  waiting for transfers between devices: 52 us -> 0 us
  Pallas kernels: 0 us -> 21.6 us
  between operations: 18.1 us -> 0.68 us
  starting transfers between devices: 16.7 us -> 0 us
  other arithmetic: 11.2 us -> 0 us
  local copies, waits for them, and re-layouts: 6.85 us -> 3.07 us
    psum x5 -> x0, blocking collectives: 139 us -> none  [the longest x2 80 us: squares_total(): return lax.psum(jnp.sum(leftover_error * leftover_error), ('det', 'pix'))]
    dot_general x24 -> x0, matrix products: 65.7 us -> none  [the longest x3 30.6 us: project_map(): jnp.einsum('bsp,bp->bs', weight_rows, per_block, preferred_element_type=j...]
    psum x1 -> x0, waiting for transfers between devices: 30.2 us -> none  [bin_terms(): return lax.psum(owned.astype(jnp.bfloat16), 'det').astype(jnp.float32)]
    all_to_all x3 -> x0, waiting for transfers between devices: 21.7 us -> none  [the longest x1 12.7 us: bin_terms(): lax.all_to_all(outgoing.astype(jnp.bfloat16), 'pix', split_axis=1, concat...]
    pallas_call x0 -> x5, Pallas kernels: none -> 21.6 us  [the longest x1 16.7 us: body(): pl.pallas_call(functools.partial(bin_kernel, n_det, n_pix, group), grid=(...]
    all_to_all x4, blocking collectives: 49.7 us -> 66.8 us  [exchange(): return lax.all_to_all(x, AXES, split_axis=0, concat_axis=0, tiled=True)]
    all_to_all x3 -> x0, starting transfers between devices: 16.7 us -> none  [the longest x1 7.28 us: body(): lax.all_to_all(send_idx, 'pix', split_axis=0, concat_axis=0, tiled=True)]
    unnamed x2 -> x0, other arithmetic: 4.42 us -> none
  transfers between devices with their start and end apart: 4 -> 0, of which waited for: 3 -> 0; matrix products, arithmetic and copies ran while one was open for 4% -> 0% of each run, Pallas kernels for 0% -> 0%
where the time goes in v1:
time: 92.7 us; the launch traced here: 92.1 us
  blocking collectives  66.8 us (72%)
  Pallas kernels  21.6 us (23%)
  local copies, waits for them, and re-layouts  3.07 us (3%)
    all_to_all x4, blocking collectives, exchange(): return lax.all_to_all(x, AXES, split_axis=0, concat_axis=0, tiled=True)  66.8 us
    pallas_call x1, Pallas kernels, body(): pl.pallas_call(functools.partial(bin_kernel, n_det, n_pix, group), grid=(...  16.7 us
    pallas_call x4, Pallas kernels, call(): pl.pallas_call(kernel, out_shape=outs, in_specs=[vmem] * len(args), out_s...  4.94 us
    unnamed x7, local copies, waits for them, and re-layouts  3.07 us

profile of v1, /device:TPU:0, one launch (start us, length us, event | category | flops | bytes accessed | tf_op | source)
XLA Modules:
  0.0 92.1 jit_solution(6669041900035536922)
XLA Ops:
  0.6 0.8 copy.7.own_ref
  1.4 0.0 copy-start
  1.5 0.9 copy-done
  2.4 0.0 copy-start.1
  2.4 0.7 copy-done.1
  3.0 0.0 copy-start.2
  3.0 0.7 copy-done.2
  3.7 16.7 %shard_map.68 = bf16[32,112,128]{2,1,0:T(8,128)(2,1)S(1)} custom-call(f32[1,256,128]{2,1,0:T(8,128)S(1)} %copy-done, bf16[1,256,128,256]{3,2,1,0:T(8,128)(2,1)} %w_ref.1, s32[1,256,1]{2,1,0:T(8,128)S(1)} %copy.7.own_ref, s32[1,256]{1,0:T(1,128)S(1)} %copy-done.1, s32[1,256]{1,0:T(1,128)S(1)} %copy-done.2), custom_call_target="tpu_custom_call" | custom-call | tf_op jit(solution)/shard_map/pallas_call | solution.py:258
  20.4 31.9 %all_to_all.20.got_ref = bf16[32,112,128]{2,1,0:T(8,128)(2,1)S(1)} all-to-all(bf16[32,112,128]{2,1,0:T(8,128)(2,1)S(1)} %shard_map.68), channel_id=1, replica_groups=mesh['det'=4,'pix'=8] {'det','pix'}, dimensions={0} | all-to-all | bytes 1835008 | tf_op jit(solution)/shard_map/all_to_all | solution.py:246
  52.3 1.0 %shard_map.69 = (bf16[32,32,128]{2,1,0:T(8,128)(2,1)S(1)}, bf16[64,2048]{1,0:T(8,128)(2,1)S(1)}, f32[8,2048]{1,0:T(8,128)S(1)}, f32[64,64]{1,0:T(8,128)S(1)}, f3...) custom-call(bf16[32,112,128]{2,1,0:T(8,128)(2,1)S(1)} %all_to_all.20.got_ref), custom_call_target="tpu_custom_call" | custom-call | tf_op jit(solution)/shard_map/pallas_call | solution.py:235
  53.3 12.7 %all_to_all.21.got_ref = bf16[32,32,128]{2,1,0:T(8,128)(2,1)S(1)} all-to-all(bf16[32,32,128]{2,1,0:T(8,128)(2,1)S(1)} %get-tuple-element.12), channel_id=1, replica_groups=mesh['det'=4,'pix'=8] {'det','pix'}, dimensions={0} | all-to-all | bytes 524288 | tf_op jit(solution)/shard_map/all_to_all | solution.py:246
  66.0 1.5 %shard_map.70 = (bf16[32,32,128]{2,1,0:T(8,128)(2,1)S(1)}, f32[32,128]{1,0:T(8,128)S(1)}) custom-call(bf16[32,32,128]{2,1,0:T(8,128)(2,1)S(1)} %all_to_all.21.got_ref, bf16[64,2048]{1,0:T(8,128)(2,1)S(1)} %get-tuple-element.13.col_ref, f32[8,2048]{1,0:T(8,128)S(1)} %get-tuple-element.14.idx_ref, f32[64,64]{1,0:T(8,128)S(1)} %get-tuple-element.15.inv_ref, ...), custom_call_target="tpu_custom_call" | custom-call | tf_op jit(solution)/shard_map/pallas_call | solution.py:235
  67.6 12.8 %all_to_all.22.got_ref = bf16[32,32,128]{2,1,0:T(8,128)(2,1)S(1)} all-to-all(bf16[32,32,128]{2,1,0:T(8,128)(2,1)S(1)} %get-tuple-element.17), channel_id=1, replica_groups=mesh['det'=4,'pix'=8] {'det','pix'}, dimensions={0} | all-to-all | bytes 524288 | tf_op jit(solution)/shard_map/all_to_all | solution.py:246
  80.4 1.8 %shard_map.71 = (f32[32,1,256]{2,1,0:T(1,128)S(1)}, f32[6,32,128]{2,1,0:T(8,128)S(1)}) custom-call(bf16[32,32,128]{2,1,0:T(8,128)(2,1)S(1)} %all_to_all.22.got_ref, bf16[64,2048]{1,0:T(8,128)(2,1)S(1)} %get-tuple-element.13.col_ref, f32[8,2048]{1,0:T(8,128)S(1)} %get-tuple-element.14.idx_ref, f32[64,64]{1,0:T(8,128)S(1)} %get-tuple-element.15.inv_ref, ...), custom_call_target="tpu_custom_call" | custom-call | tf_op jit(solution)/shard_map/pallas_call | solution.py:235
  82.2 9.4 %all_to_all.23.got_ref = f32[32,1,256]{2,1,0:T(1,128)S(1)} all-to-all(f32[32,1,256]{2,1,0:T(1,128)S(1)} %get-tuple-element.20), channel_id=1, replica_groups=mesh['det'=4,'pix'=8] {'det','pix'}, dimensions={0} | all-to-all | bytes 65536 | tf_op jit(solution)/shard_map/all_to_all | solution.py:246
  91.6 0.6 shard_map.72
Async XLA Ops:
  1.4 0.9 copy-start
  2.4 0.7 copy-start.1
  3.0 0.7 copy-start.2

commit v2 on v1

v2 whole, which is shorter than its diff:
```python
import functools

import jax
import jax.numpy as jnp
from jax import lax
from jax.experimental import pallas as pl
from jax.experimental.pallas import tpu as pltpu
from jax.sharding import PartitionSpec as P

PB_DEV = 64
NBASE_DEV = 128
CAP = 64
LANES = 128
AXES = ("det", "pix")
BF = jnp.bfloat16
F32 = jnp.float32
VMEM_LIMIT = 48 * 1024 * 1024


def dot_nn(a, b):
    return lax.dot_general(a, b, (((1,), (0,)), ((), ())), preferred_element_type=F32)


def dot_nt(a, b):
    return lax.dot_general(a, b, (((1,), (1,)), ((), ())), preferred_element_type=F32)


def split3(v):
    a = v.astype(BF)
    left = v - a.astype(F32)
    b = left.astype(BF)
    c = (left - b.astype(F32)).astype(BF)
    return a, b, c


def iota(shape, dim):
    return lax.broadcasted_iota(jnp.int32, shape, dim)


def bin_kernel(
    n_det, n_pix, group, ts_hbm, w_hbm, own_hbm, loc_hbm, base_hbm, mine_ref, give_ref, rest_ref,
    w_s, ts_s, own_s, loc_s, base_s, col_s, hit_s, dat_s, slot_lo, slot_hi, pb_lo, pb_hi, sem, small,
):
    blocks, samples, pixels = w_s.shape
    steps = blocks // group

    def weights(c):
        where = pl.ds(c * group, group)
        return pltpu.make_async_copy(w_hbm.at[0, where], w_s.at[where], sem.at[c])

    little = [
        pltpu.make_async_copy(src, dst, small.at[k])
        for k, (src, dst) in enumerate(((ts_hbm, ts_s), (own_hbm, own_s), (loc_hbm, loc_s), (base_hbm, base_s)))
    ]
    for copy in little:
        copy.start()
    for c in range(steps):
        weights(c).start()
    for copy in little:
        copy.wait()

    wide = n_pix * LANES
    loc_row = loc_s[...].astype(F32).astype(BF)
    base_row = base_s[...].astype(F32).astype(BF)
    eye = (iota((blocks, blocks), 0) == iota((blocks, blocks), 1)).astype(F32).astype(BF)
    tri = (iota((blocks, blocks), 1) < iota((blocks, blocks), 0)).astype(F32).astype(BF)
    loc = dot_nt(eye, jnp.broadcast_to(loc_row, (8, blocks)))[:, 0:1].astype(jnp.int32)
    own_row = own_s[...].astype(F32).astype(BF)
    own = dot_nt(eye, jnp.broadcast_to(own_row, (8, blocks)))[:, 0:1].astype(jnp.int32)
    own_hot = (own == iota((blocks, LANES), 1)).astype(F32)
    before = dot_nn(tri, own_hot.astype(BF))
    pos = jnp.sum(before * own_hot, axis=1, keepdims=True).astype(jnp.int32)
    lane = iota((blocks, wide), 1)

    def hot(target):
        return (lane == target).astype(F32).astype(BF)

    slot_lo[...], slot_hi[...] = hot(own * LANES + pos), hot(own * LANES + PB_DEV + pos)
    pb_lo[...], pb_hi[...] = hot(own * LANES + loc), hot(own * LANES + PB_DEV + loc)
    row = iota((8, samples), 0)
    place = iota((samples, LANES), 1)

    def row_sums(c):
        acc = jnp.zeros((samples, LANES), F32)
        for j in range(group):
            w = w_s[c * group + j].astype(F32)
            halves = w[:, 0:LANES]
            for k in range(LANES, pixels, LANES):
                halves = halves + w[:, k : k + LANES]
            acc = jnp.where(place == j, jnp.sum(halves, axis=1, keepdims=True), acc)
        return acc.T[0:group]

    def terms(c, sums):
        for j in range(group):
            r = jnp.broadcast_to(sums[j : j + 1], (8, samples))
            u = jnp.broadcast_to(ts_s[0, pl.ds(c * group + j, 1), :], (8, samples))
            lhs = jnp.where(row == 0, r, jnp.where(row == 1, u, 1.0)).astype(BF)
            t = dot_nn(lhs, w_s[c * group + j])
            where = pl.ds(c * group + j, 1)
            hit_s[where, :] = t[0:1]
            dat_s[where, :] = t[1:2]
            col_s[where, :] = t[2:3]

    def step(c, sums):
        weights(c).wait()
        after = row_sums(c)
        terms(c - 1, sums)
        return after

    weights(0).wait()
    sums = lax.fori_loop(1, steps, step, row_sums(0))
    terms(steps - 1, sums)

    pch = pixels // n_det
    half = pch // 2
    core = lax.rem(lax.axis_index("det"), 2)
    hit_s[...] = hit_s[...].T
    dat_s[...] = dat_s[...].T

    def part(of, which):
        rows = [of[pl.ds(pl.multiple_of(d * pch + which * half, half), half), :] for d in range(n_det)]
        return jnp.concatenate(rows, axis=0).astype(BF)

    def binned(which):
        return dot_nn(part(hit_s, which), pb_lo[...]) + dot_nn(part(dat_s, which), pb_hi[...])

    theirs, mine = binned(1 - core), binned(core)
    col_t = col_s[...].T.astype(BF)
    low = jnp.concatenate([col_t[d * pch : d * pch + half] for d in range(n_det)], axis=0)
    high = jnp.concatenate([col_t[d * pch + half : (d + 1) * pch] for d in range(n_det)], axis=0)
    columns = (dot_nn(low, slot_lo[...]) + dot_nn(high, slot_hi[...])).astype(BF)
    where = dot_nn(jnp.broadcast_to(loc_row, (8, blocks)), slot_lo[...])
    where = where + dot_nn(jnp.broadcast_to(base_row, (8, blocks)), slot_hi[...])

    base_hot = (iota((NBASE_DEV, blocks), 0) == base_s[...]).astype(F32).astype(BF)
    t0, t1, t2 = split3(ts_s[0])
    per_base = dot_nn(base_hot, t0) + dot_nn(base_hot, t1) + dot_nn(base_hot, t2)
    b0, b1, b2 = split3(per_base)
    one = jnp.ones((8, samples), BF)
    s0, s1, s2 = [s.astype(F32) for s in split3(dot_nt(one, b0) + dot_nt(one, b1) + dot_nt(one, b2))]
    count = dot_nt(jnp.ones((8, blocks), BF), base_hot)
    r8 = iota((8, LANES), 0)
    own_rows = jnp.where(r8 == 1, s0, jnp.where(r8 == 2, s1, jnp.where(r8 == 3, s2, count)))
    for o in range(n_pix):
        cols = slice(o * LANES, (o + 1) * LANES)
        tile = jnp.where(r8 == 0, where[:, cols], own_rows).astype(BF)
        for d in range(n_det):
            to, rows = d * n_pix + o, slice(d * half, (d + 1) * half)
            give_ref[to] = theirs[rows, cols].astype(BF)
            mine_ref[to] = mine[rows, cols]
            rest_ref[to, 0:half, :] = columns[rows, cols]
            rest_ref[to, half:, :] = tile


def add_kernel(mine_ref, took_ref, rest_ref, send_ref):
    rows, half, _ = mine_ref.shape
    for g in range(rows):
        send_ref[g, 0:half, :] = rest_ref[g, 0:half, :]
        send_ref[g, half : 2 * half, :] = (mine_ref[g] + took_ref[g].astype(F32)).astype(BF)
        send_ref[g, 2 * half :, :] = rest_ref[g, half:, :]


def project(col_t, sky_t, pb_hot, base_hot, row_hot):
    spread = dot_nn(sky_t.astype(BF), pb_hot)
    per_slot = jnp.sum(col_t.astype(F32) * spread, axis=0, keepdims=True)
    parts = [jnp.where(row_hot, p.astype(F32), 0.0).astype(BF) for p in split3(per_slot)]
    return dot_nt(parts[0], base_hot) + dot_nt(parts[1], base_hot) + dot_nt(parts[2], base_hot)


def bin_amps(amps, col_t, pb_hot, base_hot, row_hot):
    a0, a1, a2 = split3(amps)
    spread = dot_nn(a0, base_hot) + dot_nn(a1, base_hot) + dot_nn(a2, base_hot)
    per_slot = jnp.sum(jnp.where(row_hot, spread, 0.0), axis=0, keepdims=True)
    terms = col_t.astype(F32) * per_slot
    high = terms.astype(BF)
    low = (terms - high.astype(F32)).astype(BF)
    return dot_nt(high, pb_hot) + dot_nt(low, pb_hot)


def hots(idx_ref):
    slots = idx_ref.shape[1]
    pb_hot = (iota((PB_DEV, slots), 0).astype(F32) == idx_ref[0:1, :]).astype(F32).astype(BF)
    base_hot = (iota((NBASE_DEV, slots), 0).astype(F32) == idx_ref[1:2, :]).astype(F32).astype(BF)
    return pb_hot, base_hot


def row_mask(rows, slots):
    return iota((rows, slots), 1) // CAP == iota((rows, slots), 0)


def owner_kernel(pch, n_pix, got_ref, send_ref, col_ref, idx_ref, inv_ref, base_ref, count_ref):
    rows = got_ref.shape[0]
    half = pch // 2
    low = iota((half, LANES), 1) < CAP
    low8 = iota((8, LANES), 1) < CAP
    maps = [jnp.zeros((half, LANES), F32), jnp.zeros((half, LANES), F32)]
    for g in range(rows):
        core = (g // n_pix) % 2
        maps[core] = maps[core] + got_ref[g, half : 2 * half, :].astype(F32)
    for i in range(rows // 2):
        a, b = got_ref[2 * i, 0:half, :].astype(F32), got_ref[2 * i + 1, 0:half, :].astype(F32)
        cols = slice(i * LANES, (i + 1) * LANES)
        col_ref[0:half, cols] = jnp.where(low, a, pltpu.roll(b, CAP, 1)).astype(BF)
        col_ref[half:, cols] = jnp.where(low, pltpu.roll(a, CAP, 1), b).astype(BF)
        ta, tb = got_ref[2 * i, 2 * half :, :].astype(F32), got_ref[2 * i + 1, 2 * half :, :].astype(F32)
        pb = jnp.where(low8, ta, pltpu.roll(tb, CAP, 1))
        base = jnp.where(low8, pltpu.roll(ta, CAP, 1), tb)
        idx_ref[0:1, cols] = pb[0:1]
        idx_ref[1:2, cols] = base[0:1]
        for g, t in ((2 * i, ta), (2 * i + 1, tb)):
            base_ref[g : g + 1, :] = t[1:2] + t[2:3] + t[3:4]
            count_ref[g : g + 1, :] = t[4:5]
    maps = jnp.concatenate(maps, axis=0)
    inv = 1.0 / (maps[:, 0:PB_DEV] + 1.0)
    inv_ref[...] = inv
    sky = maps[:, PB_DEV:] * inv
    pb_hot, base_hot = hots(idx_ref)
    part = project(col_ref[...], sky, pb_hot, base_hot, row_mask(rows, col_ref.shape[1])).astype(BF)
    for g in range(rows):
        send_ref[g] = part


def total_of(got_ref):
    acc = got_ref[0].astype(F32)
    for g in range(1, got_ref.shape[0]):
        acc = acc + got_ref[g].astype(F32)
    return acc


def first_kernel(samples, got_ref, col_ref, idx_ref, inv_ref, base_ref, send_ref, rhs_ref):
    rhs = (base_ref[...] - total_of(got_ref)) * (1.0 / samples)
    rhs_ref[...] = rhs
    pb_hot, base_hot = hots(idx_ref)
    row_hot = row_mask(rhs.shape[0], col_ref.shape[1])
    binned = bin_amps(rhs, col_ref[...], pb_hot, base_hot, row_hot)
    part = project(col_ref[...], binned * inv_ref[...], pb_hot, base_hot, row_hot).astype(BF)
    for g in range(send_ref.shape[0]):
        send_ref[g] = part


def second_kernel(samples, got_ref, col_ref, idx_ref, inv_ref, rhs_ref, count_ref, send_ref, state_ref):
    rhs = rhs_ref[...]
    more = count_ref[...] + 1.0
    image = more * rhs - total_of(got_ref) * (1.0 / samples)
    rr = jnp.sum(rhs * rhs)
    alpha = rr / jnp.sum(rhs * image)
    levels = alpha * rhs
    error = rhs - alpha * image
    new = jnp.sum(error * error)
    heading = error + (new / rr) * rhs
    curve = jnp.sum(more * heading * heading)
    pb_hot, base_hot = hots(idx_ref)
    rows = rhs.shape[0]
    row_hot = row_mask(rows, col_ref.shape[1])
    binned = bin_amps(heading, col_ref[...], pb_hot, base_hot, row_hot)
    sky = binned * inv_ref[...]
    quad = jnp.sum(binned * sky)
    part = project(col_ref[...], sky, pb_hot, base_hot, row_hot)
    for g in range(rows):
        send_ref[g, 0:1, 0:LANES] = part[g : g + 1]
        send_ref[g, 0:1, LANES:] = jnp.full((1, LANES), quad, F32)
    state_ref[0] = levels
    state_ref[1] = error
    state_ref[2] = heading
    state_ref[3] = more * heading
    state_ref[4] = jnp.full((rows, LANES), new, F32)
    state_ref[5] = jnp.full((rows, LANES), curve, F32)


def last_kernel(samples, n_pix, got_ref, state_ref, levels_ref, error_ref):
    me = lax.axis_index("det") * n_pix + lax.axis_index("pix")
    acc = got_ref[0]
    for g in range(1, got_ref.shape[0]):
        acc = acc + got_ref[g]
    acc = acc * (1.0 / samples)
    mine = [state_ref[k, pl.ds(me, 1), :] for k in range(6)]
    levels, error, heading, scaled, new, curve = mine
    image = scaled - acc[:, 0:LANES]
    alpha = new / (curve - acc[:, LANES:])
    levels_ref[...] = levels + alpha * heading
    error_ref[...] = error - alpha * image


def call(kernel, outs, *args, **kw):
    vmem = pl.BlockSpec(memory_space=pltpu.VMEM)
    return pl.pallas_call(
        kernel,
        out_shape=outs,
        in_specs=[vmem] * len(args),
        out_specs=[vmem] * len(outs),
        compiler_params=pltpu.CompilerParams(vmem_limit_bytes=VMEM_LIMIT),
        **kw,
    )(*args)


def exchange(x):
    return lax.all_to_all(x, AXES, split_axis=0, concat_axis=0, tiled=True)


def body(timestream, weights, block_owner, block_local, baseline_of):
    n_det, n_pix = lax.axis_size("det"), lax.axis_size("pix")
    rows = n_det * n_pix
    _, blocks, samples, pixels = weights.shape
    pch = pixels // n_det
    half = pch // 2
    slots = rows * CAP
    group = 32
    shape = jax.ShapeDtypeStruct
    here = pl.BlockSpec(memory_space=pltpu.VMEM)
    wide = n_pix * LANES
    mine, give, rest = pl.pallas_call(
        functools.partial(bin_kernel, n_det, n_pix, group),
        out_shape=[shape((rows, half, LANES), F32), shape((rows, half, LANES), BF), shape((rows, half + 8, LANES), BF)],
        in_specs=[pl.BlockSpec(memory_space=pltpu.HBM)] * 5,
        out_specs=[here] * 3,
        scratch_shapes=[
            pltpu.VMEM((blocks, samples, pixels), BF),
            pltpu.VMEM((1, blocks, samples), F32),
            *[pltpu.VMEM((1, blocks), jnp.int32)] * 3,
            *[pltpu.VMEM((blocks, pixels), F32)] * 3,
            *[pltpu.VMEM((blocks, wide), BF)] * 4,
            pltpu.SemaphoreType.DMA((blocks // group,)),
            pltpu.SemaphoreType.DMA((4,)),
        ],
        compiler_params=pltpu.CompilerParams(vmem_limit_bytes=VMEM_LIMIT),
    )(timestream, weights, block_owner.reshape(1, blocks), block_local, baseline_of)
    took = lax.ppermute(give, "det", [(i, i ^ 1) for i in range(n_det)])
    sent = call(add_kernel, [shape((rows, pch + 8, LANES), BF)], mine, took, rest)[0]
    got = exchange(sent)
    everyone = shape((rows, rows, NBASE_DEV), BF)
    vector = shape((rows, NBASE_DEV), F32)
    part, col_t, idx, inv, base, count = call(
        functools.partial(owner_kernel, pch, n_pix),
        [everyone, shape((pch, slots), BF), shape((8, slots), F32), shape((pch, PB_DEV), F32), vector, vector],
        got,
    )
    part, rhs = call(
        functools.partial(first_kernel, samples), [everyone, vector], exchange(part), col_t, idx, inv, base
    )
    part, state = call(
        functools.partial(second_kernel, samples),
        [shape((rows, 1, 2 * LANES), F32), shape((6, rows, NBASE_DEV), F32)],
        exchange(part), col_t, idx, inv, rhs, count,
    )
    own = shape((1, NBASE_DEV), F32)
    return tuple(call(functools.partial(last_kernel, samples, n_pix), [own, own], exchange(part), state))


def solution(mesh):
    placed = (
        P(AXES, None, None),
        P(AXES, None, None, None),
        P(AXES, None, None),
        P(AXES, None),
        P(AXES, None),
    )
    return jax.shard_map(
        body,
        mesh=mesh,
        in_specs=placed,
        out_specs=(P(AXES, None), P(AXES, None)),
        check_vma=False,
    )
```

time: 92.7 us -> 78.8 us (0.85)
  Pallas kernels: 21.6 us -> 13.6 us
  blocking collectives: 66.8 us -> 59.7 us
  waiting for transfers between devices: 0 us -> 1.16 us
    pallas_call x1, Pallas kernels: 16.7 us -> 8.61 us  [body(): pl.pallas_call(functools.partial(bin_kernel, n_det, n_pix, group), out_sh...]
    all_to_all x4, blocking collectives: 66.8 us -> 59.7 us  [exchange(): return lax.all_to_all(x, AXES, split_axis=0, concat_axis=0, tiled=True)]
    ppermute x0 -> x1, waiting for transfers between devices: none -> 1.16 us  [body(): took = lax.ppermute(give, 'det', [(i, i ^ 1) for i in range(n_det)])]
    unnamed x7 -> x8, local copies, waits for them, and re-layouts: 3.07 us -> 2.93 us
    pallas_call x4 -> x5, Pallas kernels: 4.94 us -> 4.99 us  [call(): pl.pallas_call(kernel, out_shape=outs, in_specs=[vmem] * len(args), out_s...]
  transfers between devices with their start and end apart: 0 -> 1, of which waited for: 0 -> 1; matrix products, arithmetic and copies ran while one was open for 0% -> 0% of each run, Pallas kernels for 0% -> 0%
where the time goes in v2:
time: 78.8 us; the launch traced here: 78.6 us
  blocking collectives  59.7 us (76%)
  Pallas kernels  13.6 us (17%)
  local copies, waits for them, and re-layouts  2.93 us (4%)
  waiting for transfers between devices  1.16 us (1%)
    all_to_all x4, blocking collectives, exchange(): return lax.all_to_all(x, AXES, split_axis=0, concat_axis=0, tiled=True)  59.7 us
    pallas_call x1, Pallas kernels, body(): pl.pallas_call(functools.partial(bin_kernel, n_det, n_pix, group), out_sh...  8.61 us
    pallas_call x5, Pallas kernels, call(): pl.pallas_call(kernel, out_shape=outs, in_specs=[vmem] * len(args), out_s...  4.99 us
    unnamed x8, local copies, waits for them, and re-layouts  2.93 us
  transfers between devices with their start and end apart: 1, of which 1 were waited for; matrix products, arithmetic and copies ran while one was open for 0% of the time, Pallas kernels for 0%

profile of v2, /device:TPU:0, one launch (start us, length us, event | category | flops | bytes accessed | tf_op | source)
XLA Modules:
  0.0 78.6 jit_solution(12640456599143086408)
XLA Ops:
  0.6 0.0 copy-start
  0.6 0.9 %copy-done = f32[1,256,128]{2,1,0:T(8,128)S(1)} copy-done((f32[1,256,128]{2,1,0:T(8,128)S(1)}, f32[1,256,128]{2,1,0:T(8,128)}, u32[]{:S(2)}) %copy-start) | copy-done | bytes 131096
  1.5 0.0 copy-start.1
  1.5 0.7 copy-done.1
  2.2 0.0 copy-start.2
  2.2 0.7 copy-done.2
  2.9 0.0 copy-start.3
  2.9 0.7 copy-done.3
  3.6 8.6 %shard_map.68 = (f32[32,32,128]{2,1,0:T(8,128)S(1)}, bf16[32,32,128]{2,1,0:T(8,128)(2,1)S(1)}, bf16[32,40,128]{2,1,0:T(8,128)(2,1)S(1)}) custom-call(f32[1,256,128]{2,1,0:T(8,128)S(1)} %copy-done, bf16[1,256,128,256]{3,2,1,0:T(8,128)(2,1)} %w_hbm.1, s32[1,256]{1,0:T(1,128)S(1)} %bitcast.1, s32[1,256]{1,0:T(1,128)S(1)} %copy-done.2, s32[1,256]{1,0:T(1,128)S(1)} %copy-done.3), custom_call_target="tpu_custom_call" | custom-call | tf_op jit(solution)/shard_map/pallas_call | solution.py:311
  12.2 0.5 collective-permute-start
  12.7 1.2 %collective-permute-done.took_ref = bf16[32,32,128]{2,1,0:T(8,128)(2,1)S(1)} collective-permute-done((bf16[32,32,128]{2,1,0:T(8,128)(2,1)S(1)}, bf16[32,32,128]{2,1,0:T(8,128)(2,1)S(1)}, u32[]{:S(2)}, u32[]{:S(2)}) %collective-permute-start) | collective-permute-done | bytes 262176 | tf_op jit(solution)/shard_map/ppermute | solution.py:327
  13.9 0.1 shard_map.69
  14.0 24.8 %all_to_all.20.got_ref = bf16[32,72,128]{2,1,0:T(8,128)(2,1)S(1)} all-to-all(bf16[32,72,128]{2,1,0:T(8,128)(2,1)S(1)} %shard_map.69), channel_id=1, replica_groups=mesh['det'=4,'pix'=8] {'det','pix'}, dimensions={0} | all-to-all | bytes 1179648 | tf_op jit(solution)/shard_map/all_to_all | solution.py:297
  38.7 1.0 %shard_map.70 = (bf16[32,32,128]{2,1,0:T(8,128)(2,1)S(1)}, bf16[64,2048]{1,0:T(8,128)(2,1)S(1)}, f32[8,2048]{1,0:T(8,128)S(1)}, f32[64,64]{1,0:T(8,128)S(1)}, f3...) custom-call(bf16[32,72,128]{2,1,0:T(8,128)(2,1)S(1)} %all_to_all.20.got_ref), custom_call_target="tpu_custom_call" | custom-call | tf_op jit(solution)/shard_map/pallas_call | solution.py:286
  39.7 12.7 %all_to_all.21.got_ref = bf16[32,32,128]{2,1,0:T(8,128)(2,1)S(1)} all-to-all(bf16[32,32,128]{2,1,0:T(8,128)(2,1)S(1)} %get-tuple-element.18), channel_id=1, replica_groups=mesh['det'=4,'pix'=8] {'det','pix'}, dimensions={0} | all-to-all | bytes 524288 | tf_op jit(solution)/shard_map/all_to_all | solution.py:297
  52.4 1.5 %shard_map.71 = (bf16[32,32,128]{2,1,0:T(8,128)(2,1)S(1)}, f32[32,128]{1,0:T(8,128)S(1)}) custom-call(bf16[32,32,128]{2,1,0:T(8,128)(2,1)S(1)} %all_to_all.21.got_ref, bf16[64,2048]{1,0:T(8,128)(2,1)S(1)} %get-tuple-element.19.col_ref, f32[8,2048]{1,0:T(8,128)S(1)} %get-tuple-element.20.idx_ref, f32[64,64]{1,0:T(8,128)S(1)} %get-tuple-element.21.inv_ref, ...), custom_call_target="tpu_custom_call" | custom-call | tf_op jit(solution)/shard_map/pallas_call | solution.py:286
  54.0 12.8 %all_to_all.22.got_ref = bf16[32,32,128]{2,1,0:T(8,128)(2,1)S(1)} all-to-all(bf16[32,32,128]{2,1,0:T(8,128)(2,1)S(1)} %get-tuple-element.23), channel_id=1, replica_groups=mesh['det'=4,'pix'=8] {'det','pix'}, dimensions={0} | all-to-all | bytes 524288 | tf_op jit(solution)/shard_map/all_to_all | solution.py:297
  66.8 1.8 %shard_map.72 = (f32[32,1,256]{2,1,0:T(1,128)S(1)}, f32[6,32,128]{2,1,0:T(8,128)S(1)}) custom-call(bf16[32,32,128]{2,1,0:T(8,128)(2,1)S(1)} %all_to_all.22.got_ref, bf16[64,2048]{1,0:T(8,128)(2,1)S(1)} %get-tuple-element.19.col_ref, f32[8,2048]{1,0:T(8,128)S(1)} %get-tuple-element.20.idx_ref, f32[64,64]{1,0:T(8,128)S(1)} %get-tuple-element.21.inv_ref, ...), custom_call_target="tpu_custom_call" | custom-call | tf_op jit(solution)/shard_map/pallas_call | solution.py:286
  68.7 9.4 %all_to_all.23.got_ref = f32[32,1,256]{2,1,0:T(1,128)S(1)} all-to-all(f32[32,1,256]{2,1,0:T(1,128)S(1)} %get-tuple-element.26), channel_id=1, replica_groups=mesh['det'=4,'pix'=8] {'det','pix'}, dimensions={0} | all-to-all | bytes 65536 | tf_op jit(solution)/shard_map/all_to_all | solution.py:297
  78.0 0.6 shard_map.73
Async XLA Ops:
  0.6 0.9 %copy-start = (f32[1,256,128]{2,1,0:T(8,128)S(1)}, f32[1,256,128]{2,1,0:T(8,128)}, u32[]{:S(2)}) copy-start(f32[1,256,128]{2,1,0:T(8,128)} %ts_hbm.1) | copy-start | bytes 393220
  1.5 0.7 copy-start.1
  2.2 0.7 copy-start.2
  2.9 0.7 copy-start.3
  12.2 1.7 %collective-permute-start = (bf16[32,32,128]{2,1,0:T(8,128)(2,1)S(1)}, bf16[32,32,128]{2,1,0:T(8,128)(2,1)S(1)}, u32[]{:S(2)}, u32[]{:S(2)}) collective-permute-start(bf16[32,32,128]{2,1,0:T(8,128)(2,1)S(1)} %get-tuple-element.16), channel_id=1, source_target_pairs={{0,8},{8,0},{16,24},{24,16},{1,9},{9,1},{17,25},{25,17},{2,10},{10... | collective-permute-start | bytes 786440 | tf_op jit(solution)/shard_map/ppermute | solution.py:327

commit v3 on v2

v3 whole, which is shorter than its diff:
```python
import functools

import jax
import jax.numpy as jnp
from jax import lax
from jax.experimental import pallas as pl
from jax.experimental.pallas import tpu as pltpu
from jax.sharding import PartitionSpec as P

PB_DEV = 64
NBASE_DEV = 128
CAP = 64
LANES = 128
AXES = ("det", "pix")
BF = jnp.bfloat16
F32 = jnp.float32
VMEM_LIMIT = 48 * 1024 * 1024


def dot_nn(a, b):
    return lax.dot_general(a, b, (((1,), (0,)), ((), ())), preferred_element_type=F32)


def dot_nt(a, b):
    return lax.dot_general(a, b, (((1,), (1,)), ((), ())), preferred_element_type=F32)


def split3(v):
    a = v.astype(BF)
    left = v - a.astype(F32)
    b = left.astype(BF)
    c = (left - b.astype(F32)).astype(BF)
    return a, b, c


def iota(shape, dim):
    return lax.broadcasted_iota(jnp.int32, shape, dim)


def column(row):
    n = row.shape[1]
    eye = (iota((n, n), 0) == iota((n, n), 1)).astype(F32).astype(BF)
    return dot_nt(eye, jnp.broadcast_to(row.astype(F32).astype(BF), (8, n)))[:, 0:1].astype(jnp.int32)


def hot(target, wide):
    return (iota((target.shape[0], wide), 1) == target).astype(F32).astype(BF)


def bin_kernel(
    n_det, n_pix, group, ts_hbm, w_hbm, own_hbm, loc_hbm,
    give_ref, hit_ref, dat_ref, col_ref, pb_hot,
    w_s, ts_s, own_s, loc_s, hit_s, dat_s, col_s, sem, small,
):
    blocks, samples, pixels = w_s.shape
    steps = blocks // group

    def weights(c):
        where = pl.ds(c * group, group)
        return pltpu.make_async_copy(w_hbm.at[0, where], w_s.at[where], sem.at[c])

    def series(c):
        where = pl.ds(c * group, group)
        return pltpu.make_async_copy(ts_hbm.at[0, where], ts_s.at[0, where], small.at[c])

    indices = [
        pltpu.make_async_copy(src, dst, small.at[steps + k]) for k, (src, dst) in enumerate(((own_hbm, own_s), (loc_hbm, loc_s)))
    ]
    for copy in indices:
        copy.start()
    for c in range(steps):
        series(c).start()
        weights(c).start()
    row = iota((8, samples), 0)
    place = iota((samples, LANES), 1)

    def row_sums(c):
        acc = jnp.zeros((samples, LANES), F32)
        for j in range(group):
            w = w_s[c * group + j].astype(F32)
            halves = w[:, 0:LANES]
            for k in range(LANES, pixels, LANES):
                halves = halves + w[:, k : k + LANES]
            acc = jnp.where(place == j, jnp.sum(halves, axis=1, keepdims=True), acc)
        return acc.T[0:group]

    def terms(c, sums):
        for j in range(group):
            r = jnp.broadcast_to(sums[j : j + 1], (8, samples))
            u = jnp.broadcast_to(ts_s[0, pl.ds(c * group + j, 1), :], (8, samples))
            lhs = jnp.where(row == 0, r, jnp.where(row == 1, u, 1.0)).astype(BF)
            t = dot_nn(lhs, w_s[c * group + j])
            where = pl.ds(c * group + j, 1)
            hit_s[where, :] = t[0:1]
            dat_s[where, :] = t[1:2]
            col_s[where, :] = t[2:3]

    def step(c, sums):
        series(c - 1).wait()
        weights(c).wait()
        after = row_sums(c)
        terms(c - 1, sums)
        return after

    weights(0).wait()
    sums = lax.fori_loop(1, steps, step, row_sums(0))
    series(steps - 1).wait()
    for copy in indices:
        copy.wait()
    pb_hot[...] = hot(column(own_s[...]) * PB_DEV + column(loc_s[...]), n_pix * PB_DEV)
    terms(steps - 1, sums)
    hit_ref[...] = hit_s[...].T
    dat_ref[...] = dat_s[...].T
    col_ref[...] = col_s[...].T
    core = lax.rem(lax.axis_index("det"), 2)
    binned(n_det, n_pix, 1 - core, hit_ref, dat_ref, pb_hot, give_ref)


def pair(first, second, swap):
    low = iota(first.shape, 1) < CAP
    return jnp.where(low, first, swap(second)), jnp.where(low, swap(first), second)


def swap_halves(v):
    return pltpu.roll(v, CAP, 1)


def two_up(n_det, n_pix, first, second, ref):
    half = first.shape[0] // n_det
    for i in range(n_pix // 2):
        cols = slice(i * LANES, (i + 1) * LANES)
        for o, tile in zip((2 * i, 2 * i + 1), pair(first[:, cols], second[:, cols], swap_halves)):
            tile = tile.astype(ref.dtype)
            for d in range(n_det):
                ref[d * n_pix + o, 0:half, :] = tile[d * half : (d + 1) * half]


def binned(n_det, n_pix, which, hit_ref, dat_ref, pb_hot, ref):
    half = hit_ref.shape[0] // n_det // 2
    rows = [
        of[pl.ds(pl.multiple_of((2 * d + which) * half, half), half), :].astype(BF) for of in (hit_ref, dat_ref) for d in range(n_det)
    ]
    both = dot_nn(jnp.concatenate(rows, axis=0), pb_hot[...])
    two_up(n_det, n_pix, both[: n_det * half], both[n_det * half :], ref)


def fill_kernel(n_det, n_pix, ts_ref, own_ref, loc_ref, base_ref, hit_ref, dat_ref, col_ref, pb_hot, mine_ref, rest_ref):
    _, blocks, samples = ts_ref.shape
    own = column(own_ref[...])
    tri = (iota((blocks, blocks), 1) < iota((blocks, blocks), 0)).astype(F32).astype(BF)
    own_hot = (own == iota((blocks, LANES), 1)).astype(F32)
    before = dot_nn(tri, own_hot.astype(BF))
    slot = own * CAP + jnp.sum(before * own_hot, axis=1, keepdims=True).astype(jnp.int32)
    slot_hot = hot(slot, n_pix * CAP)
    core = lax.rem(lax.axis_index("det"), 2)
    binned(n_det, n_pix, core, hit_ref, dat_ref, pb_hot, mine_ref)
    col_t = col_ref[...].astype(BF)
    pch = col_t.shape[0] // n_det
    half = pch // 2
    rows = [col_t[(2 * d + k) * half : (2 * d + k + 1) * half] for k in (0, 1) for d in range(n_det)]
    both = dot_nn(jnp.concatenate(rows, axis=0), slot_hot)
    two_up(n_det, n_pix, both[: n_det * half], both[n_det * half :], rest_ref)

    sums = jnp.sum(ts_ref[0].T, axis=0, keepdims=True)
    w0, w1, w2 = [w.astype(F32) for w in split3(sums / jnp.sum(col_t.astype(F32), axis=0, keepdims=True))]
    r16 = iota((16, blocks), 0)
    lhs = jnp.where(r16 == 0, loc_ref[...].astype(F32), jnp.where(r16 == 8, base_ref[...].astype(F32), 0.0))
    lhs = jnp.where(r16 == 1, w0, jnp.where(r16 == 9, w1, jnp.where(r16 == 2, w2, lhs)))
    where = dot_nn(lhs.astype(BF), slot_hot)
    base_hot = (column(base_ref[...]) == iota((blocks, NBASE_DEV), 1)).astype(F32)
    count = jnp.sum(base_hot, axis=0, keepdims=True)
    r8 = iota((8, LANES), 0)
    for i in range(n_pix // 2):
        cols = slice(i * LANES, (i + 1) * LANES)
        for o, tile in zip((2 * i, 2 * i + 1), pair(where[0:8, cols], where[8:16, cols], swap_halves)):
            tile = jnp.where(r8 == 3, count, tile).astype(BF)
            for d in range(n_det):
                rest_ref[d * n_pix + o, half:, :] = tile


def join_kernel(mine_ref, took_ref, rest_ref, send_ref):
    rows, half, _ = mine_ref.shape
    for g in range(rows):
        send_ref[g, 0:half, :] = rest_ref[g, 0:half, :]
        send_ref[g, half : 2 * half, :] = (mine_ref[g] + took_ref[g].astype(F32)).astype(BF)
        send_ref[g, 2 * half :, :] = rest_ref[g, half:, :]


def split2(v):
    a = v.astype(BF)
    return a, (v - a.astype(F32)).astype(BF)


def total(v):
    return jnp.sum(jnp.sum(v, axis=0, keepdims=True), axis=1, keepdims=True)


def project(col_t, sky_t, pb_hot, base_hot, row_hot, shift=None):
    rows = row_hot.shape[0]
    spread = dot_nn(sky_t.astype(BF), pb_hot)
    spread = spread if shift is None else spread - shift
    per_slot = jnp.sum(col_t.astype(F32) * spread, axis=0, keepdims=True)
    parts = [jnp.where(row_hot, p.astype(F32), 0.0).astype(BF) for p in split2(per_slot)]
    both = dot_nt(jnp.concatenate(parts, axis=0), base_hot)
    return both[0:rows] + both[rows:]


def bin_amps(amps, col_t, pb_hot, base_hot, row_hot):
    rows = row_hot.shape[0]
    both = dot_nn(jnp.concatenate(split2(amps), axis=0), base_hot)
    per_slot = jnp.sum(jnp.where(row_hot, both[0:rows] + both[rows:], 0.0), axis=0, keepdims=True)
    pch = col_t.shape[0]
    both = dot_nt(jnp.concatenate(split2(col_t.astype(F32) * per_slot), axis=0), pb_hot)
    return both[0:pch] + both[pch:]


def row_mask(rows, slots):
    return iota((rows, slots), 1) // CAP == iota((rows, slots), 0)


def halves_out(part, keep_ref, give_ref, work):
    work[...] = part
    half = keep_ref.shape[0]
    core = lax.rem(lax.axis_index("det"), 2)
    keep_ref[...] = work[pl.ds(pl.multiple_of(core * half, half), half), :]
    give_ref[...] = work[pl.ds(pl.multiple_of((1 - core) * half, half), half), :]


def sum_kernel(keep_ref, took_ref, send_ref):
    part = (keep_ref[...] + took_ref[...]).astype(BF)
    for g in range(send_ref.shape[0]):
        send_ref[g] = part


def total_of(got_ref, n_pix):
    sums = [None, None]
    for g in range(got_ref.shape[0]):
        core = (g // n_pix) % 2
        term = got_ref[g].astype(F32)
        sums[core] = term if sums[core] is None else sums[core] + term
    return jnp.concatenate(sums, axis=0)


def columns_of(pack_ref):
    slots = pack_ref.shape[1] - LANES
    inv = pack_ref[:, slots:].astype(F32)
    return pack_ref[:, :slots], inv[:, 0:PB_DEV] + inv[:, PB_DEV:]


def owner_kernel(pch, n_pix, got_ref, keep_ref, give_ref, pack_ref, pb_ref, hot_ref, more_ref, work, mean):
    rows = got_ref.shape[0]
    half = pch // 2
    slots = rows * CAP
    pb_of = iota((PB_DEV, LANES), 0).astype(F32)
    base_of = iota((NBASE_DEV, LANES), 0).astype(F32)
    maps = [jnp.zeros((half, LANES), F32), jnp.zeros((half, LANES), F32)]
    for g in range(rows):
        core = (g // n_pix) % 2
        maps[core] = maps[core] + got_ref[g, half : 2 * half, :].astype(F32)
    for i in range(rows // 2):
        cols = slice(i * LANES, (i + 1) * LANES)
        halves = pair(got_ref[2 * i, 0:half, :].astype(F32), got_ref[2 * i + 1, 0:half, :].astype(F32), swap_halves)
        pack_ref[0:half, cols] = halves[0].astype(BF)
        pack_ref[half:, cols] = halves[1].astype(BF)
        tiles = [got_ref[2 * i + k, 2 * half :, :].astype(F32) for k in (0, 1)]
        one, two = pair(*tiles, swap_halves)
        pb_ref[:, cols] = (pb_of == one[0:1]).astype(F32).astype(BF)
        hot_ref[:, cols] = (base_of == two[0:1]).astype(F32).astype(BF)
        mean[0:1, cols] = one[1:2] + two[1:2] + one[2:3]
        for k in (0, 1):
            more_ref[2 * i + k : 2 * i + k + 1, :] = tiles[k][3:4] + 1.0
    maps = jnp.concatenate(maps, axis=0)
    inv = 1.0 / (maps[:, 0:PB_DEV] + 1.0)
    pack_ref[:, slots:] = jnp.concatenate([v.astype(F32) for v in split2(inv)], axis=1).astype(BF)
    sky = maps[:, PB_DEV:] * inv
    part = project(pack_ref[:, :slots], sky, pb_ref[...], hot_ref[...], row_mask(rows, slots), mean[0:1, :])
    halves_out(part, keep_ref, give_ref, work)


def first_kernel(samples, n_pix, got_ref, pack_ref, other_ref, pb_ref, hot_ref, send_ref, rhs_ref):
    rhs = total_of(got_ref, n_pix) * (-1.0 / samples)
    rhs_ref[...] = rhs
    rows = rhs.shape[0]
    slots = rows * CAP
    columns, inv = zip(columns_of(pack_ref), columns_of(other_ref))
    binned = bin_amps(rhs, jnp.concatenate(columns, axis=0), pb_ref[...], hot_ref[...], row_mask(rows, slots))
    sky = binned * jnp.concatenate(inv, axis=0)
    core = lax.rem(lax.axis_index("det"), 2)
    mine = pl.ds(pl.multiple_of(core * (slots // 2), slots // 2), slots // 2)
    columns = jnp.concatenate([pack_ref[:, mine], other_ref[:, mine]], axis=0)
    part = project(columns, sky, pb_ref[:, mine], hot_ref[:, mine], row_mask(rows // 2, slots // 2)).astype(BF)
    for g in range(rows):
        send_ref[g] = part


def second_kernel(samples, n_pix, got_ref, pack_ref, pb_ref, hot_ref, rhs_ref, more_ref, send_ref, state_ref):
    rhs = rhs_ref[...]
    more = more_ref[...]
    image = more * rhs - total_of(got_ref, n_pix) * (1.0 / samples)
    rr = total(rhs * rhs)
    alpha = rr / total(rhs * image)
    error = rhs - alpha * image
    new = total(error * error)
    heading = error + (new / rr) * rhs
    rows = rhs.shape[0]
    columns, inv = columns_of(pack_ref)
    row_hot = row_mask(rows, columns.shape[1])
    binned = bin_amps(heading, columns, pb_ref[...], hot_ref[...], row_hot)
    sky = binned * inv
    part = project(columns, sky, pb_ref[...], hot_ref[...], row_hot)
    quad = jnp.broadcast_to(total(binned * sky), (1, LANES))
    for g in range(rows):
        send_ref[g, 0:1, 0:LANES] = part[g : g + 1]
        send_ref[g, 0:1, LANES:] = quad
    scaled = more * heading
    state_ref[0] = alpha * rhs
    state_ref[1] = error
    state_ref[2] = heading
    state_ref[3] = scaled
    state_ref[4] = jnp.broadcast_to(new, (rows, LANES))
    state_ref[5] = jnp.broadcast_to(total(scaled * heading), (rows, LANES))


def last_kernel(samples, n_pix, got_ref, state_ref, levels_ref, error_ref):
    me = lax.axis_index("det") * n_pix + lax.axis_index("pix")
    acc = got_ref[0]
    for g in range(1, got_ref.shape[0]):
        acc = acc + got_ref[g]
    acc = acc * (1.0 / samples)
    mine = [state_ref[k, pl.ds(me, 1), :] for k in range(6)]
    levels, error, heading, scaled, new, curve = mine
    image = scaled - acc[:, 0:LANES]
    alpha = new / (curve - acc[:, LANES:])
    levels_ref[...] = levels + alpha * heading
    error_ref[...] = error - alpha * image


def call(kernel, outs, *args, scratch=()):
    vmem = pl.BlockSpec(memory_space=pltpu.VMEM)
    return pl.pallas_call(
        kernel,
        out_shape=outs,
        in_specs=[vmem] * len(args),
        out_specs=[vmem] * len(outs),
        scratch_shapes=scratch,
        compiler_params=pltpu.CompilerParams(vmem_limit_bytes=VMEM_LIMIT),
        cost_estimate=pl.CostEstimate(flops=10**8, bytes_accessed=4 * 10**6, transcendentals=0),
    )(*args)


def exchange(x):
    return lax.all_to_all(x, AXES, split_axis=0, concat_axis=0, tiled=True)


def other_core(x):
    return lax.ppermute(x, "det", [(i, i ^ 1) for i in range(lax.axis_size("det"))])


def body(timestream, weights, block_owner, block_local, baseline_of):
    n_det, n_pix = lax.axis_size("det"), lax.axis_size("pix")
    rows = n_det * n_pix
    _, blocks, samples, pixels = weights.shape
    pch = pixels // n_det
    half = pch // 2
    slots = rows * CAP
    group = 32
    shape = jax.ShapeDtypeStruct
    hbm = functools.partial(pltpu.with_memory_space_constraint, memory_space=pltpu.HBM)
    owners = block_owner.reshape(1, blocks)
    give, *filling = pl.pallas_call(
        functools.partial(bin_kernel, n_det, n_pix, group),
        out_shape=[
            shape((rows, half, LANES), BF),
            *[shape((pixels, blocks), F32)] * 3,
            shape((blocks, n_pix * PB_DEV), BF),
        ],
        in_specs=[pl.BlockSpec(memory_space=pltpu.HBM)] * 4,
        out_specs=[pl.BlockSpec(memory_space=pltpu.VMEM)] * 5,
        scratch_shapes=[
            pltpu.VMEM((blocks, samples, pixels), BF),
            pltpu.VMEM((1, blocks, samples), F32),
            *[pltpu.VMEM((1, blocks), jnp.int32)] * 2,
            *[pltpu.VMEM((blocks, pixels), F32)] * 3,
            pltpu.SemaphoreType.DMA((blocks // group,)),
            pltpu.SemaphoreType.DMA((blocks // group + 2,)),
        ],
        compiler_params=pltpu.CompilerParams(vmem_limit_bytes=VMEM_LIMIT),
        cost_estimate=pl.CostEstimate(flops=10**8, bytes_accessed=2**25, transcendentals=0),
    )(hbm(timestream), weights, hbm(owners), hbm(block_local))
    took = other_core(give)
    mine, rest = call(
        functools.partial(fill_kernel, n_det, n_pix),
        [shape((rows, half, LANES), F32), shape((rows, half + 8, LANES), BF)],
        timestream, owners, block_local, baseline_of, *filling,
    )
    got = exchange(call(join_kernel, [shape((rows, pch + 8, LANES), BF)], mine, took, rest)[0])
    vector = shape((rows, NBASE_DEV), F32)
    part = shape((rows // 2, NBASE_DEV), F32)

    everyone = shape((rows, rows // 2, NBASE_DEV), BF)
    keep, give, pack, pb_hot, base_hot, more = call(
        functools.partial(owner_kernel, pch, n_pix),
        [part, part, shape((pch, slots + LANES), BF), shape((PB_DEV, slots), BF), shape((NBASE_DEV, slots), BF), vector],
        got,
        scratch=[pltpu.VMEM((rows, NBASE_DEV), F32), pltpu.VMEM((8, slots), F32)],
    )
    took, pack = lax.optimization_barrier((other_core(give), pack))
    other = other_core(pack)
    sent = call(sum_kernel, [everyone], keep, took)[0]
    sent, rhs = call(
        functools.partial(first_kernel, samples, n_pix), [everyone, vector], exchange(sent), pack, other, pb_hot, base_hot
    )
    sent, state = call(
        functools.partial(second_kernel, samples, n_pix),
        [shape((rows, 1, 2 * LANES), F32), shape((6, rows, NBASE_DEV), F32)],
        exchange(sent), pack, pb_hot, base_hot, rhs, more,
    )
    own = shape((1, NBASE_DEV), F32)
    return tuple(call(functools.partial(last_kernel, samples, n_pix), [own, own], exchange(sent), state))


def solution(mesh):
    placed = (
        P(AXES, None, None),
        P(AXES, None, None, None),
        P(AXES, None, None),
        P(AXES, None),
        P(AXES, None),
    )
    return jax.shard_map(
        body,
        mesh=mesh,
        in_specs=placed,
        out_specs=(P(AXES, None), P(AXES, None)),
        check_vma=False,
    )
```

time: 78.8 us -> 69.8 us (0.89)
  blocking collectives: 59.7 us -> 54 us
  local copies, waits for them, and re-layouts: 2.93 us -> 0.02 us
  Pallas kernels: 13.6 us -> 12.7 us
    all_to_all x4, blocking collectives: 59.7 us -> 54 us  [exchange(): return lax.all_to_all(x, AXES, split_axis=0, concat_axis=0, tiled=True)]
    unnamed x8, local copies, waits for them, and re-layouts: 2.93 us -> 0.02 us
    pallas_call x5 -> x7, Pallas kernels: 4.99 us -> 4.71 us  [call(): pl.pallas_call(kernel, out_shape=outs, in_specs=[vmem] * len(args), out_s...]
  transfers between devices with their start and end apart: 1 -> 3, of which waited for: 1 -> 2; matrix products, arithmetic and copies ran while one was open for 0% -> 0% of each run, Pallas kernels for 0% -> 1%
where the time goes in v3:
time: 69.8 us; the launch traced here: 69.6 us
  blocking collectives  54 us (77%)
  Pallas kernels  12.7 us (18%)
  waiting for transfers between devices  1.36 us (2%)
  starting transfers between devices  0.75 us (1%)
  between operations  0.72 us (1%)
    all_to_all x4, blocking collectives, exchange(): return lax.all_to_all(x, AXES, split_axis=0, concat_axis=0, tiled=True)  54 us
    pallas_call x1, Pallas kernels, body(): pl.pallas_call(functools.partial(bin_kernel, n_det, n_pix, group), out_sh...  8.02 us
    pallas_call x7, Pallas kernels, call(): pl.pallas_call(kernel, out_shape=outs, in_specs=[vmem] * len(args), out_s...  4.71 us
  transfers between devices with their start and end apart: 3, of which 2 were waited for; matrix products, arithmetic and copies ran while one was open for 0% of the time, Pallas kernels for 1%

profile of v3, /device:TPU:0, one launch (start us, length us, event | category | flops | bytes accessed | tf_op | source)
XLA Modules:
  0.0 69.6 jit_solution(1262527012593712720)
XLA Ops:
  0.6 0.0 copy-start.2
  0.6 0.0 copy-start
  0.7 0.0 copy-start.1
  0.7 0.0 copy-start.3
  0.7 8.0 %shard_map.68 = (bf16[32,32,128]{2,1,0:T(8,128)(2,1)S(1)}, f32[256,256]{1,0:T(8,128)S(1)}, f32[256,256]{1,0:T(8,128)S(1)}, f32[256,256]{1,0:T(8,128)S(1)}, bf16[256,512]{1,0:T(8,128)(2,1)S(1)}) custom-call(f32[1,256,128]{2,1,0:T(8,128)} %ts_ref.1, bf16[1,256,128,256]{3,2,1,0:T(8,128)(2,1)} %w_hbm.1, s32[1,256]{1,0:T(1,128)} %bitcast.1, s32[1,256]{1,0:T(1,128)} %loc_ref.1), custom_call_target="tpu_custom_call" | custom-call | flops 100000000 | bytes 33554432 | tf_op jit(solution)/shard_map/pallas_call | solution.py:370
  8.7 0.5 collective-permute-start
  9.2 0.0 copy-done.2
  9.2 0.0 copy-done
  9.2 0.0 copy-done.1
  9.2 0.9 %shard_map.69 = (f32[32,32,128]{2,1,0:T(8,128)S(1)}, bf16[32,40,128]{2,1,0:T(8,128)(2,1)S(1)}) custom-call(f32[1,256,128]{2,1,0:T(8,128)S(1)} %copy-done, s32[1,256]{1,0:T(1,128)S(1)} %bitcast.2, s32[1,256]{1,0:T(1,128)S(1)} %copy-done.2, s32[1,256]{1,0:T(1,128)S(1)} %copy-done.3, f32[256,256]{1,0:T(8,128)S(1)} %get-tuple-element.21.hit_ref, ...), custom_call_target="tpu_custom_call" | custom-call | flops 100000000 | bytes 4000000 | tf_op jit(solution)/shard_map/pallas_call | solution.py:340
  10.2 0.2 collective-permute-done.took_ref
  10.4 0.1 shard_map.70
  10.5 24.8 %all_to_all.20.got_ref = bf16[32,72,128]{2,1,0:T(8,128)(2,1)S(1)} all-to-all(bf16[32,72,128]{2,1,0:T(8,128)(2,1)S(1)} %shard_map.70), channel_id=1, replica_groups=mesh['det'=4,'pix'=8] {'det','pix'}, dimensions={0} | all-to-all | bytes 1179648 | tf_op jit(solution)/shard_map/all_to_all | solution.py:352
  35.2 0.8 %shard_map.71 = (f32[16,128]{1,0:T(8,128)S(1)}, f32[16,128]{1,0:T(8,128)S(1)}, bf16[64,2176]{1,0:T(8,128)(2,1)S(1)}, bf16[64,2048]{1,0:T(8,128)(2,1)S(1)}, bf16[...) custom-call(bf16[32,72,128]{2,1,0:T(8,128)(2,1)S(1)} %all_to_all.20.got_ref), custom_call_target="tpu_custom_call" | custom-call | flops 100000000 | bytes 4000000 | tf_op jit(solution)/shard_map/pallas_call | solution.py:340
  36.1 0.1 collective-permute-start.1
  36.1 1.2 %collective-permute-done.1.took_ref = f32[16,128]{1,0:T(8,128)S(1)} collective-permute-done((f32[16,128]{1,0:T(8,128)S(1)}, f32[16,128]{1,0:T(8,128)S(1)}, u32[]{:S(2)}, u32[]{:S(2)}) %collective-permute-start.1) | collective-permute-done | bytes 8224 | tf_op jit(solution)/shard_map/ppermute | solution.py:356
  37.3 0.2 collective-permute-start.2
  37.5 9.8 %all_to_all.21.got_ref = bf16[32,16,128]{2,1,0:T(8,128)(2,1)S(1)} all-to-all(bf16[32,16,128]{2,1,0:T(8,128)(2,1)S(1)} %shard_map.72), channel_id=1, replica_groups=mesh['det'=4,'pix'=8] {'det','pix'}, dimensions={0} | all-to-all | bytes 262144 | tf_op jit(solution)/shard_map/all_to_all | solution.py:352
  47.3 0.0 collective-permute-done.2.other_ref
  47.3 1.1 %shard_map.73 = (bf16[32,16,128]{2,1,0:T(8,128)(2,1)S(1)}, f32[32,128]{1,0:T(8,128)S(1)}) custom-call(bf16[32,16,128]{2,1,0:T(8,128)(2,1)S(1)} %all_to_all.21.got_ref, bf16[64,2176]{1,0:T(8,128)(2,1)S(1)} %get-tuple-element.32.pack_ref, bf16[64,2176]{1,0:T(8,128)(2,1)S(1)} %collective-permute-done.2.other_ref, ...), custom_call_target="tpu_custom_call" | custom-call | flops 100000000 | bytes 4000000 | tf_op jit(solution)/shard_map/pallas_call | solution.py:340
  48.4 10.0 %all_to_all.22.got_ref = bf16[32,16,128]{2,1,0:T(8,128)(2,1)S(1)} all-to-all(bf16[32,16,128]{2,1,0:T(8,128)(2,1)S(1)} %get-tuple-element.35), channel_id=1, replica_groups=mesh['det'=4,'pix'=8] {'det','pix'}, dimensions={0} | all-to-all | bytes 262144 | tf_op jit(solution)/shard_map/all_to_all | solution.py:352
  58.4 1.2 %shard_map.74 = (f32[32,1,256]{2,1,0:T(1,128)S(1)}, f32[6,32,128]{2,1,0:T(8,128)S(1)}) custom-call(bf16[32,16,128]{2,1,0:T(8,128)(2,1)S(1)} %all_to_all.22.got_ref, bf16[64,2176]{1,0:T(8,128)(2,1)S(1)} %get-tuple-element.32.pack_ref, bf16[64,2048]{1,0:T(8,128)(2,1)S(1)} %get-tuple-element.33.pb_ref, bf16[128,2048]{1,0:T(8,128)(2,1)S(1)} %get-tuple-element.34.hot_ref, ...), custom_call_target="tpu_custom_call" | custom-call | flops 100000000 | bytes 4000000 | tf_op jit(solution)/shard_map/pallas_call | solution.py:340
  59.6 9.4 %all_to_all.23.got_ref = f32[32,1,256]{2,1,0:T(1,128)S(1)} all-to-all(f32[32,1,256]{2,1,0:T(1,128)S(1)} %get-tuple-element.38), channel_id=1, replica_groups=mesh['det'=4,'pix'=8] {'det','pix'}, dimensions={0} | all-to-all | bytes 65536 | tf_op jit(solution)/shard_map/all_to_all | solution.py:352
  69.1 0.6 shard_map.75
  (2 shorter events, 0.0 us)
Async XLA Ops:
  0.6 8.6 %copy-start.2 = (s32[1,256]{1,0:T(1,128)S(1)}, s32[1,256]{1,0:T(1,128)}, u32[]{:S(2)}) copy-start(s32[1,256]{1,0:T(1,128)} %loc_ref.1) | copy-start | bytes 3076
  0.6 8.6 %copy-start = (f32[1,256,128]{2,1,0:T(8,128)S(1)}, f32[1,256,128]{2,1,0:T(8,128)}, u32[]{:S(2)}) copy-start(f32[1,256,128]{2,1,0:T(8,128)} %ts_ref.1) | copy-start | bytes 393220
  0.7 8.6 %copy-start.1 = (s32[1,256,1]{1,2,0:T(1,128)S(1)}, s32[1,256,1]{1,2,0:T(1,128)}, u32[]{:S(2)}) copy-start(s32[1,256,1]{1,2,0:T(1,128)} %param.7) | copy-start | bytes 3076
  0.7 8.6 %copy-start.3 = (s32[1,256]{1,0:T(1,128)S(1)}, s32[1,256]{1,0:T(1,128)}, u32[]{:S(2)}) copy-start(s32[1,256]{1,0:T(1,128)} %base_ref.1) | copy-start | bytes 3076
  8.7 1.7 %collective-permute-start = (bf16[32,32,128]{2,1,0:T(8,128)(2,1)S(1)}, bf16[32,32,128]{2,1,0:T(8,128)(2,1)S(1)}, u32[]{:S(2)}, u32[]{:S(2)}) collective-permute-start(bf16[32,32,128]{2,1,0:T(8,128)(2,1)S(1)} %get-tuple-element.26), channel_id=1, source_target_pairs={{0,8},{8,0},{16,24},{24,16},{1,9},{9,1},{17,25},{25,17},{2,10},{10... | collective-permute-start | bytes 786440 | tf_op jit(solution)/shard_map/ppermute | solution.py:356
  36.1 1.2 %collective-permute-start.1 = (f32[16,128]{1,0:T(8,128)S(1)}, f32[16,128]{1,0:T(8,128)S(1)}, u32[]{:S(2)}, u32[]{:S(2)}) collective-permute-start(f32[16,128]{1,0:T(8,128)S(1)} %get-tuple-element.29), channel_id=1, source_target_pairs={{0,8},{8,0},{16,24},{24,16},{1,9},{9,1},{17,25},{25,17},{2,10},{10... | collective-permute-start | bytes 24584 | tf_op jit(solution)/shard_map/ppermute | solution.py:356
  37.3 10.0 %collective-permute-start.2 = (bf16[64,2176]{1,0:T(8,128)(2,1)S(1)}, bf16[64,2176]{1,0:T(8,128)(2,1)S(1)}, u32[]{:S(2)}, u32[]{:S(2)}) collective-permute-start(bf16[64,2176]{1,0:T(8,128)(2,1)S(1)} %get-tuple-element.32.pack_ref), channel_id=1, source_target_pairs={{0,8},{8,0},{16,24},{24,16},{1,9},{9,1},{17,25},{25,17},{2,10},{10... | collective-permute-start | bytes 835592 | tf_op jit(solution)/shard_map/ppermute | solution.py:356

commit v4 on v3

--- a/solution.py
+++ b/solution.py
@@ -53,62 +53,75 @@
     w_s, ts_s, own_s, loc_s, hit_s, dat_s, col_s, sem, small,
 ):
     blocks, samples, pixels = w_s.shape
-    steps = blocks // group
-
-    def weights(c):
-        where = pl.ds(c * group, group)
-        return pltpu.make_async_copy(w_hbm.at[0, where], w_s.at[where], sem.at[c])
-
-    def series(c):
-        where = pl.ds(c * group, group)
-        return pltpu.make_async_copy(ts_hbm.at[0, where], ts_s.at[0, where], small.at[c])
+    steps = blocks // group - 1
+    short = group // 2
+
+    def copies(first, many, k):
+        where = pl.ds(first, many)
+        return (
+            pltpu.make_async_copy(ts_hbm.at[0, where], ts_s.at[0, where], small.at[k]),
+            pltpu.make_async_copy(w_hbm.at[0, where], w_s.at[where], sem.at[k]),
+        )
+
+    def full(c):
+        return copies(c * group, group, c)
+
+    ends = [copies(steps * group + k * short, short, steps + k) for k in (0, 1)]
 
     indices = [
-        pltpu.make_async_copy(src, dst, small.at[steps + k]) for k, (src, dst) in enumerate(((own_hbm, own_s), (loc_hbm, loc_s)))
+        pltpu.make_async_copy(src, dst, small.at[steps + 2 + k]) for k, (src, dst) in enumerate(((own_hbm, own_s), (loc_hbm, loc_s)))
     ]
     for copy in indices:
         copy.start()
-    for c in range(steps):
-        series(c).start()
-        weights(c).start()
+    for piece in [full(c) for c in range(steps)] + ends:
+        for copy in piece:
+            copy.start()
     row = iota((8, samples), 0)
     place = iota((samples, LANES), 1)
 
-    def row_sums(c):
+    def row_sums(first, many):
         acc = jnp.zeros((samples, LANES), F32)
-        for j in range(group):
-            w = w_s[c * group + j].astype(F32)
+        for j in range(many):
+            w = w_s[first + j].astype(F32)
             halves = w[:, 0:LANES]
             for k in range(LANES, pixels, LANES):
                 halves = halves + w[:, k : k + LANES]
             acc = jnp.where(place == j, jnp.sum(halves, axis=1, keepdims=True), acc)
-        return acc.T[0:group]
-
-    def terms(c, sums):
-        for j in range(group):
+        return acc.T[0:many]
+
+    def terms(first, many, sums):
+        for j in range(many):
             r = jnp.broadcast_to(sums[j : j + 1], (8, samples))
-            u = jnp.broadcast_to(ts_s[0, pl.ds(c * group + j, 1), :], (8, samples))
+            u = jnp.broadcast_to(ts_s[0, pl.ds(first + j, 1), :], (8, samples))
             lhs = jnp.where(row == 0, r, jnp.where(row == 1, u, 1.0)).astype(BF)
-            t = dot_nn(lhs, w_s[c * group + j])
-            where = pl.ds(c * group + j, 1)
+            t = dot_nn(lhs, w_s[first + j])
+            where = pl.ds(first + j, 1)
             hit_s[where, :] = t[0:1]
             dat_s[where, :] = t[1:2]
             col_s[where, :] = t[2:3]
 
+    def wait(piece):
+        for copy in piece:
+            copy.wait()
+
     def step(c, sums):
-        series(c - 1).wait()
-        weights(c).wait()
-        after = row_sums(c)
-        terms(c - 1, sums)
+        wait(full(c))
+        after = row_sums(c * group, group)
+        terms((c - 1) * group, group, sums)
         return after
 
-    weights(0).wait()
-    sums = lax.fori_loop(1, steps, step, row_sums(0))
-    series(steps - 1).wait()
+    wait(full(0))
+    sums = lax.fori_loop(1, steps, step, row_sums(0, group))
+    wait(ends[0])
+    after = row_sums(steps * group, short)
+    terms((steps - 1) * group, group, sums)
+    wait(ends[1])
+    last = row_sums(steps * group + short, short)
+    terms(steps * group, short, after)
     for copy in indices:
         copy.wait()
     pb_hot[...] = hot(column(own_s[...]) * PB_DEV + column(loc_s[...]), n_pix * PB_DEV)
-    terms(steps - 1, sums)
+    terms(steps * group + short, short, last)
     hit_ref[...] = hit_s[...].T
     dat_ref[...] = dat_s[...].T
     col_ref[...] = col_s[...].T
@@ -209,9 +222,7 @@
     rows = row_hot.shape[0]
     both = dot_nn(jnp.concatenate(split2(amps), axis=0), base_hot)
     per_slot = jnp.sum(jnp.where(row_hot, both[0:rows] + both[rows:], 0.0), axis=0, keepdims=True)
-    pch = col_t.shape[0]
-    both = dot_nt(jnp.concatenate(split2(col_t.astype(F32) * per_slot), axis=0), pb_hot)
-    return both[0:pch] + both[pch:]
+    return dot_nt((col_t.astype(F32) * per_slot).astype(BF), pb_hot)
 
 
 def row_mask(rows, slots):
@@ -277,13 +288,14 @@
     halves_out(part, keep_ref, give_ref, work)
 
 
-def first_kernel(samples, n_pix, got_ref, pack_ref, other_ref, pb_ref, hot_ref, send_ref, rhs_ref):
+def first_kernel(samples, n_pix, got_ref, pack_ref, other_ref, pb_ref, hot_ref, send_ref, rhs_ref, map_ref):
     rhs = total_of(got_ref, n_pix) * (-1.0 / samples)
     rhs_ref[...] = rhs
     rows = rhs.shape[0]
     slots = rows * CAP
     columns, inv = zip(columns_of(pack_ref), columns_of(other_ref))
     binned = bin_amps(rhs, jnp.concatenate(columns, axis=0), pb_ref[...], hot_ref[...], row_mask(rows, slots))
+    map_ref[...] = binned[: pack_ref.shape[0]]
     sky = binned * jnp.concatenate(inv, axis=0)
     core = lax.rem(lax.axis_index("det"), 2)
     mine = pl.ds(pl.multiple_of(core * (slots // 2), slots // 2), slots // 2)
@@ -293,19 +305,21 @@
         send_ref[g] = part
 
 
-def second_kernel(samples, n_pix, got_ref, pack_ref, pb_ref, hot_ref, rhs_ref, more_ref, send_ref, state_ref):
+def second_kernel(samples, n_pix, got_ref, pack_ref, pb_ref, hot_ref, rhs_ref, map_ref, more_ref, send_ref, state_ref):
     rhs = rhs_ref[...]
     more = more_ref[...]
     image = more * rhs - total_of(got_ref, n_pix) * (1.0 / samples)
+    rows = rhs.shape[0]
+    columns, inv = columns_of(pack_ref)
+    row_hot = row_mask(rows, columns.shape[1])
+    image_map = bin_amps(image, columns, pb_ref[...], hot_ref[...], row_hot)
     rr = total(rhs * rhs)
     alpha = rr / total(rhs * image)
     error = rhs - alpha * image
     new = total(error * error)
-    heading = error + (new / rr) * rhs
-    rows = rhs.shape[0]
-    columns, inv = columns_of(pack_ref)
-    row_hot = row_mask(rows, columns.shape[1])
-    binned = bin_amps(heading, columns, pb_ref[...], hot_ref[...], row_hot)
+    beta = new / rr
+    heading = error + beta * rhs
+    binned = (1.0 + beta) * map_ref[...] - alpha * image_map
     sky = binned * inv
     part = project(columns, sky, pb_ref[...], hot_ref[...], row_hot)
     quad = jnp.broadcast_to(total(binned * sky), (1, LANES))
@@ -381,8 +395,8 @@
             pltpu.VMEM((1, blocks, samples), F32),
             *[pltpu.VMEM((1, blocks), jnp.int32)] * 2,
             *[pltpu.VMEM((blocks, pixels), F32)] * 3,
-            pltpu.SemaphoreType.DMA((blocks // group,)),
-            pltpu.SemaphoreType.DMA((blocks // group + 2,)),
+            pltpu.SemaphoreType.DMA((blocks // group + 1,)),
+            pltpu.SemaphoreType.DMA((blocks // group + 3,)),
         ],
         compiler_params=pltpu.CompilerParams(vmem_limit_bytes=VMEM_LIMIT),
         cost_estimate=pl.CostEstimate(flops=10**8, bytes_accessed=2**25, transcendentals=0),
@@ -407,13 +421,13 @@
     took, pack = lax.optimization_barrier((other_core(give), pack))
     other = other_core(pack)
     sent = call(sum_kernel, [everyone], keep, took)[0]
-    sent, rhs = call(
-        functools.partial(first_kernel, samples, n_pix), [everyone, vector], exchange(sent), pack, other, pb_hot, base_hot
+    sent, rhs, rhs_map = call(
+        functools.partial(first_kernel, samples, n_pix), [everyone, vector, shape((pch, PB_DEV), F32)], exchange(sent), pack, other, pb_hot, base_hot
     )
     sent, state = call(
         functools.partial(second_kernel, samples, n_pix),
         [shape((rows, 1, 2 * LANES), F32), shape((6, rows, NBASE_DEV), F32)],
-        exchange(sent), pack, pb_hot, base_hot, rhs, more,
+        exchange(sent), pack, pb_hot, base_hot, rhs, rhs_map, more,
     )
     own = shape((1, NBASE_DEV), F32)
     return tuple(call(functools.partial(last_kernel, samples, n_pix), [own, own], exchange(sent), state))

time: 69.8 us -> 69.3 us (level)
  no operation moved by 1% of the time
where the time goes in v4:
time: 69.3 us; the launch traced here: 69.1 us
  blocking collectives  54.1 us (78%)
  Pallas kernels  12.2 us (18%)
  waiting for transfers between devices  1.36 us (2%)
  starting transfers between devices  0.75 us (1%)
  between operations  0.72 us (1%)
    all_to_all x4, blocking collectives, exchange(): return lax.all_to_all(x, AXES, split_axis=0, concat_axis=0, tiled=True)  54.1 us
    pallas_call x1, Pallas kernels, body(): pl.pallas_call(functools.partial(bin_kernel, n_det, n_pix, group), out_sh...  8.02 us
    pallas_call x7, Pallas kernels, call(): pl.pallas_call(kernel, out_shape=outs, in_specs=[vmem] * len(args), out_s...  4.19 us
  transfers between devices with their start and end apart: 3, of which 2 were waited for; matrix products, arithmetic and copies ran while one was open for 0% of the time, Pallas kernels for 1%

profile of v4, /device:TPU:0, one launch (start us, length us, event | category | flops | bytes accessed | tf_op | source)
XLA Modules:
  0.0 69.1 jit_solution(13115199546018737536)
XLA Ops:
  0.6 0.0 copy-start.2
  0.6 0.0 copy-start
  0.7 0.0 copy-start.1
  0.7 0.0 copy-start.3
  0.7 8.0 %shard_map.68 = (bf16[32,32,128]{2,1,0:T(8,128)(2,1)S(1)}, f32[256,256]{1,0:T(8,128)S(1)}, f32[256,256]{1,0:T(8,128)S(1)}, f32[256,256]{1,0:T(8,128)S(1)}, bf16[256,512]{1,0:T(8,128)(2,1)S(1)}) custom-call(f32[1,256,128]{2,1,0:T(8,128)} %ts_ref.1, bf16[1,256,128,256]{3,2,1,0:T(8,128)(2,1)} %w_hbm.1, s32[1,256]{1,0:T(1,128)} %bitcast.1, s32[1,256]{1,0:T(1,128)} %loc_ref.1), custom_call_target="tpu_custom_call" | custom-call | flops 100000000 | bytes 33554432 | tf_op jit(solution)/shard_map/pallas_call | solution.py:384
  8.7 0.5 collective-permute-start
  9.2 0.0 copy-done.2
  9.2 0.0 copy-done
  9.2 0.0 copy-done.1
  9.2 0.9 %shard_map.69 = (f32[32,32,128]{2,1,0:T(8,128)S(1)}, bf16[32,40,128]{2,1,0:T(8,128)(2,1)S(1)}) custom-call(f32[1,256,128]{2,1,0:T(8,128)S(1)} %copy-done, s32[1,256]{1,0:T(1,128)S(1)} %bitcast.2, s32[1,256]{1,0:T(1,128)S(1)} %copy-done.2, s32[1,256]{1,0:T(1,128)S(1)} %copy-done.3, f32[256,256]{1,0:T(8,128)S(1)} %get-tuple-element.22.hit_ref, ...), custom_call_target="tpu_custom_call" | custom-call | flops 100000000 | bytes 4000000 | tf_op jit(solution)/shard_map/pallas_call | solution.py:354
  10.2 0.2 collective-permute-done.took_ref
  10.4 0.1 shard_map.70
  10.5 24.8 %all_to_all.20.got_ref = bf16[32,72,128]{2,1,0:T(8,128)(2,1)S(1)} all-to-all(bf16[32,72,128]{2,1,0:T(8,128)(2,1)S(1)} %shard_map.70), channel_id=1, replica_groups=mesh['det'=4,'pix'=8] {'det','pix'}, dimensions={0} | all-to-all | bytes 1179648 | tf_op jit(solution)/shard_map/all_to_all | solution.py:366
  35.2 0.8 %shard_map.71 = (f32[16,128]{1,0:T(8,128)S(1)}, f32[16,128]{1,0:T(8,128)S(1)}, bf16[64,2176]{1,0:T(8,128)(2,1)S(1)}, bf16[64,2048]{1,0:T(8,128)(2,1)S(1)}, bf16[...) custom-call(bf16[32,72,128]{2,1,0:T(8,128)(2,1)S(1)} %all_to_all.20.got_ref), custom_call_target="tpu_custom_call" | custom-call | flops 100000000 | bytes 4000000 | tf_op jit(solution)/shard_map/pallas_call | solution.py:354
  36.1 0.1 collective-permute-start.1
  36.1 1.2 %collective-permute-done.1.took_ref = f32[16,128]{1,0:T(8,128)S(1)} collective-permute-done((f32[16,128]{1,0:T(8,128)S(1)}, f32[16,128]{1,0:T(8,128)S(1)}, u32[]{:S(2)}, u32[]{:S(2)}) %collective-permute-start.1) | collective-permute-done | bytes 8224 | tf_op jit(solution)/shard_map/ppermute | solution.py:370
  37.3 0.2 collective-permute-start.2
  37.5 9.8 %all_to_all.21.got_ref = bf16[32,16,128]{2,1,0:T(8,128)(2,1)S(1)} all-to-all(bf16[32,16,128]{2,1,0:T(8,128)(2,1)S(1)} %shard_map.72), channel_id=1, replica_groups=mesh['det'=4,'pix'=8] {'det','pix'}, dimensions={0} | all-to-all | bytes 262144 | tf_op jit(solution)/shard_map/all_to_all | solution.py:366
  47.3 0.0 collective-permute-done.2.other_ref
  47.3 0.9 %shard_map.73 = (bf16[32,16,128]{2,1,0:T(8,128)(2,1)S(1)}, f32[32,128]{1,0:T(8,128)S(1)}, f32[64,64]{1,0:T(8,128)S(1)}) custom-call(bf16[32,16,128]{2,1,0:T(8,128)(2,1)S(1)} %all_to_all.21.got_ref, bf16[64,2176]{1,0:T(8,128)(2,1)S(1)} %get-tuple-element.33.pack_ref, bf16[64,2176]{1,0:T(8,128)(2,1)S(1)} %collective-permute-done.2.other_ref, ...), custom_call_target="tpu_custom_call" | custom-call | flops 100000000 | bytes 4000000 | tf_op jit(solution)/shard_map/pallas_call | solution.py:354
  48.2 10.0 %all_to_all.22.got_ref = bf16[32,16,128]{2,1,0:T(8,128)(2,1)S(1)} all-to-all(bf16[32,16,128]{2,1,0:T(8,128)(2,1)S(1)} %get-tuple-element.36), channel_id=1, replica_groups=mesh['det'=4,'pix'=8] {'det','pix'}, dimensions={0} | all-to-all | bytes 262144 | tf_op jit(solution)/shard_map/all_to_all | solution.py:366
  58.2 0.9 %shard_map.74 = (f32[32,1,256]{2,1,0:T(1,128)S(1)}, f32[6,32,128]{2,1,0:T(8,128)S(1)}) custom-call(bf16[32,16,128]{2,1,0:T(8,128)(2,1)S(1)} %all_to_all.22.got_ref, bf16[64,2176]{1,0:T(8,128)(2,1)S(1)} %get-tuple-element.33.pack_ref, bf16[64,2048]{1,0:T(8,128)(2,1)S(1)} %get-tuple-element.34.pb_ref, bf16[128,2048]{1,0:T(8,128)(2,1)S(1)} %get-tuple-element.35.hot_ref, ...), custom_call_target="tpu_custom_call" | custom-call | flops 100000000 | bytes 4000000 | tf_op jit(solution)/shard_map/pallas_call | solution.py:354
  59.1 9.4 %all_to_all.23.got_ref = f32[32,1,256]{2,1,0:T(1,128)S(1)} all-to-all(f32[32,1,256]{2,1,0:T(1,128)S(1)} %get-tuple-element.40), channel_id=1, replica_groups=mesh['det'=4,'pix'=8] {'det','pix'}, dimensions={0} | all-to-all | bytes 65536 | tf_op jit(solution)/shard_map/all_to_all | solution.py:366
  68.5 0.6 shard_map.75
  (2 shorter events, 0.0 us)
Async XLA Ops:
  0.6 8.6 %copy-start.2 = (s32[1,256]{1,0:T(1,128)S(1)}, s32[1,256]{1,0:T(1,128)}, u32[]{:S(2)}) copy-start(s32[1,256]{1,0:T(1,128)} %loc_ref.1) | copy-start | bytes 3076
  0.6 8.6 %copy-start = (f32[1,256,128]{2,1,0:T(8,128)S(1)}, f32[1,256,128]{2,1,0:T(8,128)}, u32[]{:S(2)}) copy-start(f32[1,256,128]{2,1,0:T(8,128)} %ts_ref.1) | copy-start | bytes 393220
  0.7 8.6 %copy-start.1 = (s32[1,256,1]{1,2,0:T(1,128)S(1)}, s32[1,256,1]{1,2,0:T(1,128)}, u32[]{:S(2)}) copy-start(s32[1,256,1]{1,2,0:T(1,128)} %param.7) | copy-start | bytes 3076
  0.7 8.6 %copy-start.3 = (s32[1,256]{1,0:T(1,128)S(1)}, s32[1,256]{1,0:T(1,128)}, u32[]{:S(2)}) copy-start(s32[1,256]{1,0:T(1,128)} %base_ref.1) | copy-start | bytes 3076
  8.7 1.7 %collective-permute-start = (bf16[32,32,128]{2,1,0:T(8,128)(2,1)S(1)}, bf16[32,32,128]{2,1,0:T(8,128)(2,1)S(1)}, u32[]{:S(2)}, u32[]{:S(2)}) collective-permute-start(bf16[32,32,128]{2,1,0:T(8,128)(2,1)S(1)} %get-tuple-element.27), channel_id=1, source_target_pairs={{0,8},{8,0},{16,24},{24,16},{1,9},{9,1},{17,25},{25,17},{2,10},{10... | collective-permute-start | bytes 786440 | tf_op jit(solution)/shard_map/ppermute | solution.py:370
  36.1 1.2 %collective-permute-start.1 = (f32[16,128]{1,0:T(8,128)S(1)}, f32[16,128]{1,0:T(8,128)S(1)}, u32[]{:S(2)}, u32[]{:S(2)}) collective-permute-start(f32[16,128]{1,0:T(8,128)S(1)} %get-tuple-element.30), channel_id=1, source_target_pairs={{0,8},{8,0},{16,24},{24,16},{1,9},{9,1},{17,25},{25,17},{2,10},{10... | collective-permute-start | bytes 24584 | tf_op jit(solution)/shard_map/ppermute | solution.py:370
  37.3 10.0 %collective-permute-start.2 = (bf16[64,2176]{1,0:T(8,128)(2,1)S(1)}, bf16[64,2176]{1,0:T(8,128)(2,1)S(1)}, u32[]{:S(2)}, u32[]{:S(2)}) collective-permute-start(bf16[64,2176]{1,0:T(8,128)(2,1)S(1)} %get-tuple-element.33.pack_ref), channel_id=1, source_target_pairs={{0,8},{8,0},{16,24},{24,16},{1,9},{9,1},{17,25},{25,17},{2,10},{10... | collective-permute-start | bytes 835592 | tf_op jit(solution)/shard_map/ppermute | solution.py:370

commit v5 on v4

--- a/solution.py
+++ b/solution.py
@@ -50,23 +50,23 @@
 def bin_kernel(
     n_det, n_pix, group, ts_hbm, w_hbm, own_hbm, loc_hbm,
     give_ref, hit_ref, dat_ref, col_ref, pb_hot,
-    w_s, ts_s, own_s, loc_s, hit_s, dat_s, col_s, sem, small,
+    w_s, ts_s, own_s, loc_s, hit_s, dat_s, sem, small,
 ):
-    blocks, samples, pixels = w_s.shape
+    blocks, samples, pixels = ts_s.shape[0], ts_s.shape[1], w_s.shape[2]
     steps = blocks // group - 1
     short = group // 2
 
     def copies(first, many, k):
-        where = pl.ds(first, many)
+        where, pairs = pl.ds(2 * first, 2 * many), pl.ds(first, many)
         return (
-            pltpu.make_async_copy(ts_hbm.at[0, where], ts_s.at[0, where], small.at[k]),
-            pltpu.make_async_copy(w_hbm.at[0, where], w_s.at[where], sem.at[k]),
+            pltpu.make_async_copy(ts_hbm.at[0, where], ts_s.at[where], small.at[k]),
+            pltpu.make_async_copy(w_hbm.at[pairs], w_s.at[pairs], sem.at[k]),
         )
 
     def full(c):
-        return copies(c * group, group, c)
-
-    ends = [copies(steps * group + k * short, short, steps + k) for k in (0, 1)]
+        return copies(c * short, short, c)
+
+    ends = [copies(steps * short + k * short // 2, short // 2, steps + k) for k in (0, 1)]
 
     indices = [
         pltpu.make_async_copy(src, dst, small.at[steps + 2 + k]) for k, (src, dst) in enumerate(((own_hbm, own_s), (loc_hbm, loc_s)))
@@ -76,29 +76,40 @@
     for piece in [full(c) for c in range(steps)] + ends:
         for copy in piece:
             copy.start()
-    row = iota((8, samples), 0)
     place = iota((samples, LANES), 1)
+    ones = jnp.ones((pixels, LANES), BF)
+    row = iota((8, 2 * samples), 0) - jnp.where(iota((8, 2 * samples), 1) < samples, 0, 3)
 
     def row_sums(first, many):
         acc = jnp.zeros((samples, LANES), F32)
-        for j in range(many):
-            w = w_s[first + j].astype(F32)
-            halves = w[:, 0:LANES]
-            for k in range(LANES, pixels, LANES):
-                halves = halves + w[:, k : k + LANES]
-            acc = jnp.where(place == j, jnp.sum(halves, axis=1, keepdims=True), acc)
-        return acc.T[0:many]
+        for j in range(2 * many):
+            w = w_s[first + j // 2, (j % 2) * samples : (j % 2 + 1) * samples, :]
+            if j % 4 == 3:
+                sums = dot_nn(w, ones)
+            else:
+                w = w.astype(F32)
+                halves = w[:, 0:LANES]
+                for k in range(LANES, pixels, LANES):
+                    halves = halves + w[:, k : k + LANES]
+                sums = jnp.sum(halves, axis=1, keepdims=True)
+            acc = jnp.where(place == j, sums, acc)
+        return acc.T[0 : 2 * many]
+
+    def beside(one, two):
+        return jnp.concatenate([jnp.broadcast_to(v, (8, samples)) for v in (one, two)], axis=1)
 
     def terms(first, many, sums):
         for j in range(many):
-            r = jnp.broadcast_to(sums[j : j + 1], (8, samples))
-            u = jnp.broadcast_to(ts_s[0, pl.ds(first + j, 1), :], (8, samples))
-            lhs = jnp.where(row == 0, r, jnp.where(row == 1, u, 1.0)).astype(BF)
+            r = beside(sums[2 * j : 2 * j + 1], sums[2 * j + 1 : 2 * j + 2])
+            at = 2 * (first + j)
+            u = beside(ts_s[pl.ds(at, 1), :], ts_s[pl.ds(at + 1, 1), :])
+            lhs = jnp.where(row == 0, r, jnp.where(row == 1, u, jnp.where(row == 2, 1.0, 0.0))).astype(BF)
             t = dot_nn(lhs, w_s[first + j])
-            where = pl.ds(first + j, 1)
-            hit_s[where, :] = t[0:1]
-            dat_s[where, :] = t[1:2]
-            col_s[where, :] = t[2:3]
+            for k in (0, 1):
+                where = pl.ds(at + k, 1)
+                hit_s[where, :] = t[3 * k : 3 * k + 1]
+                dat_s[where, :] = t[3 * k + 1 : 3 * k + 2]
+                col_ref[where, :] = t[3 * k + 2 : 3 * k + 3]
 
     def wait(piece):
         for copy in piece:
@@ -106,25 +117,25 @@
 
     def step(c, sums):
         wait(full(c))
-        after = row_sums(c * group, group)
-        terms((c - 1) * group, group, sums)
+        after = row_sums(c * short, short)
+        terms((c - 1) * short, short, sums)
         return after
 
     wait(full(0))
-    sums = lax.fori_loop(1, steps, step, row_sums(0, group))
+    sums = lax.fori_loop(1, steps, step, row_sums(0, short))
+    begin, quarter = steps * short, short // 2
     wait(ends[0])
-    after = row_sums(steps * group, short)
-    terms((steps - 1) * group, group, sums)
+    after = row_sums(begin, quarter)
+    terms(begin - short, short, sums)
     wait(ends[1])
-    last = row_sums(steps * group + short, short)
-    terms(steps * group, short, after)
+    last = row_sums(begin + quarter, quarter)
+    terms(begin, quarter, after)
     for copy in indices:
         copy.wait()
     pb_hot[...] = hot(column(own_s[...]) * PB_DEV + column(loc_s[...]), n_pix * PB_DEV)
-    terms(steps * group + short, short, last)
+    terms(begin + quarter, quarter, last)
     hit_ref[...] = hit_s[...].T
     dat_ref[...] = dat_s[...].T
-    col_ref[...] = col_s[...].T
     core = lax.rem(lax.axis_index("det"), 2)
     binned(n_det, n_pix, 1 - core, hit_ref, dat_ref, pb_hot, give_ref)
 
@@ -167,7 +178,7 @@
     slot_hot = hot(slot, n_pix * CAP)
     core = lax.rem(lax.axis_index("det"), 2)
     binned(n_det, n_pix, core, hit_ref, dat_ref, pb_hot, mine_ref)
-    col_t = col_ref[...].astype(BF)
+    col_t = col_ref[...].T.astype(BF)
     pch = col_t.shape[0] // n_det
     half = pch // 2
     rows = [col_t[(2 * d + k) * half : (2 * d + k + 1) * half] for k in (0, 1) for d in range(n_det)]
@@ -262,8 +273,9 @@
     rows = got_ref.shape[0]
     half = pch // 2
     slots = rows * CAP
-    pb_of = iota((PB_DEV, LANES), 0).astype(F32)
-    base_of = iota((NBASE_DEV, LANES), 0).astype(F32)
+    pb_of = iota((PB_DEV, LANES), 0).astype(F32).astype(BF)
+    base_of = iota((NBASE_DEV, LANES), 0).astype(F32).astype(BF)
+    yes, no = jnp.ones((1, LANES), BF), jnp.zeros((1, LANES), BF)
     maps = [jnp.zeros((half, LANES), F32), jnp.zeros((half, LANES), F32)]
     for g in range(rows):
         core = (g // n_pix) % 2
@@ -275,8 +287,8 @@
         pack_ref[half:, cols] = halves[1].astype(BF)
         tiles = [got_ref[2 * i + k, 2 * half :, :].astype(F32) for k in (0, 1)]
         one, two = pair(*tiles, swap_halves)
-        pb_ref[:, cols] = (pb_of == one[0:1]).astype(F32).astype(BF)
-        hot_ref[:, cols] = (base_of == two[0:1]).astype(F32).astype(BF)
+        pb_ref[:, cols] = jnp.where(pb_of == one[0:1].astype(BF), yes, no)
+        hot_ref[:, cols] = jnp.where(base_of == two[0:1].astype(BF), yes, no)
         mean[0:1, cols] = one[1:2] + two[1:2] + one[2:3]
         for k in (0, 1):
             more_ref[2 * i + k : 2 * i + k + 1, :] = tiles[k][3:4] + 1.0
@@ -385,22 +397,23 @@
         functools.partial(bin_kernel, n_det, n_pix, group),
         out_shape=[
             shape((rows, half, LANES), BF),
-            *[shape((pixels, blocks), F32)] * 3,
+            *[shape((pixels, blocks), F32)] * 2,
+            shape((blocks, pixels), F32),
             shape((blocks, n_pix * PB_DEV), BF),
         ],
         in_specs=[pl.BlockSpec(memory_space=pltpu.HBM)] * 4,
         out_specs=[pl.BlockSpec(memory_space=pltpu.VMEM)] * 5,
         scratch_shapes=[
-            pltpu.VMEM((blocks, samples, pixels), BF),
-            pltpu.VMEM((1, blocks, samples), F32),
+            pltpu.VMEM((blocks // 2, 2 * samples, pixels), BF),
+            pltpu.VMEM((blocks, samples), F32),
             *[pltpu.VMEM((1, blocks), jnp.int32)] * 2,
-            *[pltpu.VMEM((blocks, pixels), F32)] * 3,
+            *[pltpu.VMEM((blocks, pixels), F32)] * 2,
             pltpu.SemaphoreType.DMA((blocks // group + 1,)),
             pltpu.SemaphoreType.DMA((blocks // group + 3,)),
         ],
         compiler_params=pltpu.CompilerParams(vmem_limit_bytes=VMEM_LIMIT),
         cost_estimate=pl.CostEstimate(flops=10**8, bytes_accessed=2**25, transcendentals=0),
-    )(hbm(timestream), weights, hbm(owners), hbm(block_local))
+    )(hbm(timestream), weights.reshape(blocks // 2, 2 * samples, pixels), hbm(owners), hbm(block_local))
     took = other_core(give)
     mine, rest = call(
         functools.partial(fill_kernel, n_det, n_pix),

time: 69.3 us -> 68.9 us (level)
  no operation moved by 1% of the time
where the time goes in v5:
time: 68.9 us; the launch traced here: 68.7 us
  blocking collectives  54.1 us (79%)
  Pallas kernels  11.8 us (17%)
  waiting for transfers between devices  1.35 us (2%)
  starting transfers between devices  0.76 us (1%)
  between operations  0.72 us (1%)
    all_to_all x4, blocking collectives, exchange(): return lax.all_to_all(x, AXES, split_axis=0, concat_axis=0, tiled=True)  54.1 us
    pallas_call x1, Pallas kernels, body(): pl.pallas_call(functools.partial(bin_kernel, n_det, n_pix, group), out_sh...  7.66 us
    pallas_call x7, Pallas kernels, call(): pl.pallas_call(kernel, out_shape=outs, in_specs=[vmem] * len(args), out_s...  4.13 us
  transfers between devices with their start and end apart: 3, of which 2 were waited for; matrix products, arithmetic and copies ran while one was open for 0% of the time, Pallas kernels for 1%

profile of v5, /device:TPU:0, one launch (start us, length us, event | category | flops | bytes accessed | tf_op | source)
XLA Modules:
  0.0 68.7 jit_solution(3643961200887573829)
XLA Ops:
  0.6 0.0 copy-start.2
  0.6 0.0 copy-start
  0.7 0.0 copy-start.1
  0.7 0.0 copy-start.3
  0.7 7.7 %shard_map.68 = (bf16[32,32,128]{2,1,0:T(8,128)(2,1)S(1)}, f32[256,256]{1,0:T(8,128)S(1)}, f32[256,256]{1,0:T(8,128)S(1)}, f32[256,256]{1,0:T(8,128)S(1)}, bf16[256,512]{1,0:T(8,128)(2,1)S(1)}) custom-call(f32[1,256,128]{2,1,0:T(8,128)} %ts_ref.1, bf16[128,256,256]{2,1,0:T(8,128)(2,1)} %bitcast.4, s32[1,256]{1,0:T(1,128)} %bitcast.2, s32[1,256]{1,0:T(1,128)} %loc_ref.1), custom_call_target="tpu_custom_call" | custom-call | flops 100000000 | bytes 33554432 | tf_op jit(solution)/shard_map/pallas_call | solution.py:396
  8.3 0.5 collective-permute-start
  8.9 0.0 copy-done.2
  8.9 0.0 copy-done
  8.9 0.0 copy-done.3
  8.9 1.0 %shard_map.69 = (f32[32,32,128]{2,1,0:T(8,128)S(1)}, bf16[32,40,128]{2,1,0:T(8,128)(2,1)S(1)}) custom-call(f32[1,256,128]{2,1,0:T(8,128)S(1)} %copy-done, s32[1,256]{1,0:T(1,128)S(1)} %bitcast.3, s32[1,256]{1,0:T(1,128)S(1)} %copy-done.2, s32[1,256]{1,0:T(1,128)S(1)} %copy-done.3, f32[256,256]{1,0:T(8,128)S(1)} %get-tuple-element.22.hit_ref, ...), custom_call_target="tpu_custom_call" | custom-call | flops 100000000 | bytes 4000000 | tf_op jit(solution)/shard_map/pallas_call | solution.py:366
  9.8 0.2 collective-permute-done.took_ref
  10.0 0.1 shard_map.70
  10.1 24.8 %all_to_all.20.got_ref = bf16[32,72,128]{2,1,0:T(8,128)(2,1)S(1)} all-to-all(bf16[32,72,128]{2,1,0:T(8,128)(2,1)S(1)} %shard_map.70), channel_id=1, replica_groups=mesh['det'=4,'pix'=8] {'det','pix'}, dimensions={0} | all-to-all | bytes 1179648 | tf_op jit(solution)/shard_map/all_to_all | solution.py:378
  34.9 0.7 %shard_map.71 = (f32[16,128]{1,0:T(8,128)S(1)}, f32[16,128]{1,0:T(8,128)S(1)}, bf16[64,2176]{1,0:T(8,128)(2,1)S(1)}, bf16[64,2048]{1,0:T(8,128)(2,1)S(1)}, bf16[...) custom-call(bf16[32,72,128]{2,1,0:T(8,128)(2,1)S(1)} %all_to_all.20.got_ref), custom_call_target="tpu_custom_call" | custom-call | flops 100000000 | bytes 4000000 | tf_op jit(solution)/shard_map/pallas_call | solution.py:366
  35.6 0.1 collective-permute-start.1
  35.7 1.2 %collective-permute-done.1.took_ref = f32[16,128]{1,0:T(8,128)S(1)} collective-permute-done((f32[16,128]{1,0:T(8,128)S(1)}, f32[16,128]{1,0:T(8,128)S(1)}, u32[]{:S(2)}, u32[]{:S(2)}) %collective-permute-start.1) | collective-permute-done | bytes 8224 | tf_op jit(solution)/shard_map/ppermute | solution.py:382
  36.9 0.2 collective-permute-start.2
  37.0 9.8 %all_to_all.21.got_ref = bf16[32,16,128]{2,1,0:T(8,128)(2,1)S(1)} all-to-all(bf16[32,16,128]{2,1,0:T(8,128)(2,1)S(1)} %shard_map.72), channel_id=1, replica_groups=mesh['det'=4,'pix'=8] {'det','pix'}, dimensions={0} | all-to-all | bytes 262144 | tf_op jit(solution)/shard_map/all_to_all | solution.py:378
  46.9 0.0 collective-permute-done.2.other_ref
  46.9 0.9 %shard_map.73 = (bf16[32,16,128]{2,1,0:T(8,128)(2,1)S(1)}, f32[32,128]{1,0:T(8,128)S(1)}, f32[64,64]{1,0:T(8,128)S(1)}) custom-call(bf16[32,16,128]{2,1,0:T(8,128)(2,1)S(1)} %all_to_all.21.got_ref, bf16[64,2176]{1,0:T(8,128)(2,1)S(1)} %get-tuple-element.33.pack_ref, bf16[64,2176]{1,0:T(8,128)(2,1)S(1)} %collective-permute-done.2.other_ref, ...), custom_call_target="tpu_custom_call" | custom-call | flops 100000000 | bytes 4000000 | tf_op jit(solution)/shard_map/pallas_call | solution.py:366
  47.8 10.0 %all_to_all.22.got_ref = bf16[32,16,128]{2,1,0:T(8,128)(2,1)S(1)} all-to-all(bf16[32,16,128]{2,1,0:T(8,128)(2,1)S(1)} %get-tuple-element.36), channel_id=1, replica_groups=mesh['det'=4,'pix'=8] {'det','pix'}, dimensions={0} | all-to-all | bytes 262144 | tf_op jit(solution)/shard_map/all_to_all | solution.py:378
  57.8 0.9 %shard_map.74 = (f32[32,1,256]{2,1,0:T(1,128)S(1)}, f32[6,32,128]{2,1,0:T(8,128)S(1)}) custom-call(bf16[32,16,128]{2,1,0:T(8,128)(2,1)S(1)} %all_to_all.22.got_ref, bf16[64,2176]{1,0:T(8,128)(2,1)S(1)} %get-tuple-element.33.pack_ref, bf16[64,2048]{1,0:T(8,128)(2,1)S(1)} %get-tuple-element.34.pb_ref, bf16[128,2048]{1,0:T(8,128)(2,1)S(1)} %get-tuple-element.35.hot_ref, ...), custom_call_target="tpu_custom_call" | custom-call | flops 100000000 | bytes 4000000 | tf_op jit(solution)/shard_map/pallas_call | solution.py:366
  58.7 9.4 %all_to_all.23.got_ref = f32[32,1,256]{2,1,0:T(1,128)S(1)} all-to-all(f32[32,1,256]{2,1,0:T(1,128)S(1)} %get-tuple-element.40), channel_id=1, replica_groups=mesh['det'=4,'pix'=8] {'det','pix'}, dimensions={0} | all-to-all | bytes 65536 | tf_op jit(solution)/shard_map/all_to_all | solution.py:378
  68.1 0.6 shard_map.75
  (2 shorter events, 0.0 us)
Async XLA Ops:
  0.6 8.2 %copy-start.2 = (s32[1,256]{1,0:T(1,128)S(1)}, s32[1,256]{1,0:T(1,128)}, u32[]{:S(2)}) copy-start(s32[1,256]{1,0:T(1,128)} %loc_ref.1) | copy-start | bytes 3076
  0.6 8.2 %copy-start = (f32[1,256,128]{2,1,0:T(8,128)S(1)}, f32[1,256,128]{2,1,0:T(8,128)}, u32[]{:S(2)}) copy-start(f32[1,256,128]{2,1,0:T(8,128)} %ts_ref.1) | copy-start | bytes 393220
  0.7 8.2 %copy-start.1 = (s32[1,256,1]{1,2,0:T(1,128)S(1)}, s32[1,256,1]{1,2,0:T(1,128)}, u32[]{:S(2)}) copy-start(s32[1,256,1]{1,2,0:T(1,128)} %param.7) | copy-start | bytes 3076
  0.7 8.2 %copy-start.3 = (s32[1,256]{1,0:T(1,128)S(1)}, s32[1,256]{1,0:T(1,128)}, u32[]{:S(2)}) copy-start(s32[1,256]{1,0:T(1,128)} %base_ref.1) | copy-start | bytes 3076
  8.3 1.7 %collective-permute-start = (bf16[32,32,128]{2,1,0:T(8,128)(2,1)S(1)}, bf16[32,32,128]{2,1,0:T(8,128)(2,1)S(1)}, u32[]{:S(2)}, u32[]{:S(2)}) collective-permute-start(bf16[32,32,128]{2,1,0:T(8,128)(2,1)S(1)} %get-tuple-element.27), channel_id=1, source_target_pairs={{0,8},{8,0},{16,24},{24,16},{1,9},{9,1},{17,25},{25,17},{2,10},{10... | collective-permute-start | bytes 786440 | tf_op jit(solution)/shard_map/ppermute | solution.py:382
  35.6 1.2 %collective-permute-start.1 = (f32[16,128]{1,0:T(8,128)S(1)}, f32[16,128]{1,0:T(8,128)S(1)}, u32[]{:S(2)}, u32[]{:S(2)}) collective-permute-start(f32[16,128]{1,0:T(8,128)S(1)} %get-tuple-element.30), channel_id=1, source_target_pairs={{0,8},{8,0},{16,24},{24,16},{1,9},{9,1},{17,25},{25,17},{2,10},{10... | collective-permute-start | bytes 24584 | tf_op jit(solution)/shard_map/ppermute | solution.py:382
  36.9 10.0 %collective-permute-start.2 = (bf16[64,2176]{1,0:T(8,128)(2,1)S(1)}, bf16[64,2176]{1,0:T(8,128)(2,1)S(1)}, u32[]{:S(2)}, u32[]{:S(2)}) collective-permute-start(bf16[64,2176]{1,0:T(8,128)(2,1)S(1)} %get-tuple-element.33.pack_ref), channel_id=1, source_target_pairs={{0,8},{8,0},{16,24},{24,16},{1,9},{9,1},{17,25},{25,17},{2,10},{10... | collective-permute-start | bytes 835592 | tf_op jit(solution)/shard_map/ppermute | solution.py:382

commit v6 on v5

--- a/solution.py
+++ b/solution.py
@@ -219,21 +219,21 @@
     return jnp.sum(jnp.sum(v, axis=0, keepdims=True), axis=1, keepdims=True)
 
 
-def project(col_t, sky_t, pb_hot, base_hot, row_hot, shift=None):
+def project(col_t, sky_t, pb_hot, collapse, row_hot, shift=None):
     rows = row_hot.shape[0]
     spread = dot_nn(sky_t.astype(BF), pb_hot)
     spread = spread if shift is None else spread - shift
     per_slot = jnp.sum(col_t.astype(F32) * spread, axis=0, keepdims=True)
     parts = [jnp.where(row_hot, p.astype(F32), 0.0).astype(BF) for p in split2(per_slot)]
-    both = dot_nt(jnp.concatenate(parts, axis=0), base_hot)
+    both = collapse(jnp.concatenate(parts, axis=0))
     return both[0:rows] + both[rows:]
 
 
-def bin_amps(amps, col_t, pb_hot, base_hot, row_hot):
+def bin_amps(amps, col_t, pb_back, base_hot, row_hot):
     rows = row_hot.shape[0]
     both = dot_nn(jnp.concatenate(split2(amps), axis=0), base_hot)
     per_slot = jnp.sum(jnp.where(row_hot, both[0:rows] + both[rows:], 0.0), axis=0, keepdims=True)
-    return dot_nt((col_t.astype(F32) * per_slot).astype(BF), pb_hot)
+    return dot_nn((col_t.astype(F32) * per_slot).astype(BF), pb_back)
 
 
 def row_mask(rows, slots):
@@ -296,35 +296,45 @@
     inv = 1.0 / (maps[:, 0:PB_DEV] + 1.0)
     pack_ref[:, slots:] = jnp.concatenate([v.astype(F32) for v in split2(inv)], axis=1).astype(BF)
     sky = maps[:, PB_DEV:] * inv
-    part = project(pack_ref[:, :slots], sky, pb_ref[...], hot_ref[...], row_mask(rows, slots), mean[0:1, :])
+    collapse = lambda v: dot_nt(v, hot_ref[...])
+    part = project(pack_ref[:, :slots], sky, pb_ref[...], collapse, row_mask(rows, slots), mean[0:1, :])
     halves_out(part, keep_ref, give_ref, work)
 
 
-def first_kernel(samples, n_pix, got_ref, pack_ref, other_ref, pb_ref, hot_ref, send_ref, rhs_ref, map_ref):
+def turn_kernel(pb_ref, hot_ref, pb_back_ref, hot_back_ref):
+    for k in range(0, pb_ref.shape[1], LANES):
+        for ref, back in ((pb_ref, pb_back_ref), (hot_ref, hot_back_ref)):
+            back[k : k + LANES, :] = ref[:, k : k + LANES].astype(F32).T.astype(BF)
+
+
+def first_kernel(samples, n_pix, got_ref, pack_ref, other_ref, pb_ref, hot_ref, pb_back, hot_back, send_ref, rhs_ref, map_ref):
     rhs = total_of(got_ref, n_pix) * (-1.0 / samples)
     rhs_ref[...] = rhs
     rows = rhs.shape[0]
     slots = rows * CAP
     columns, inv = zip(columns_of(pack_ref), columns_of(other_ref))
-    binned = bin_amps(rhs, jnp.concatenate(columns, axis=0), pb_ref[...], hot_ref[...], row_mask(rows, slots))
+    binned = bin_amps(rhs, jnp.concatenate(columns, axis=0), pb_back[...], hot_ref[...], row_mask(rows, slots))
     map_ref[...] = binned[: pack_ref.shape[0]]
     sky = binned * jnp.concatenate(inv, axis=0)
     core = lax.rem(lax.axis_index("det"), 2)
     mine = pl.ds(pl.multiple_of(core * (slots // 2), slots // 2), slots // 2)
     columns = jnp.concatenate([pack_ref[:, mine], other_ref[:, mine]], axis=0)
-    part = project(columns, sky, pb_ref[:, mine], hot_ref[:, mine], row_mask(rows // 2, slots // 2)).astype(BF)
+    collapse = lambda v: dot_nn(v, hot_back[mine, :])
+    part = project(columns, sky, pb_ref[:, mine], collapse, row_mask(rows // 2, slots // 2)).astype(BF)
     for g in range(rows):
         send_ref[g] = part
 
 
-def second_kernel(samples, n_pix, got_ref, pack_ref, pb_ref, hot_ref, rhs_ref, map_ref, more_ref, send_ref, state_ref):
+def second_kernel(
+    samples, n_pix, got_ref, pack_ref, pb_ref, hot_ref, pb_back, hot_back, rhs_ref, map_ref, more_ref, send_ref, state_ref
+):
     rhs = rhs_ref[...]
     more = more_ref[...]
     image = more * rhs - total_of(got_ref, n_pix) * (1.0 / samples)
     rows = rhs.shape[0]
     columns, inv = columns_of(pack_ref)
     row_hot = row_mask(rows, columns.shape[1])
-    image_map = bin_amps(image, columns, pb_ref[...], hot_ref[...], row_hot)
+    image_map = bin_amps(image, columns, pb_back[...], hot_ref[...], row_hot)
     rr = total(rhs * rhs)
     alpha = rr / total(rhs * image)
     error = rhs - alpha * image
@@ -333,7 +343,7 @@
     heading = error + beta * rhs
     binned = (1.0 + beta) * map_ref[...] - alpha * image_map
     sky = binned * inv
-    part = project(columns, sky, pb_ref[...], hot_ref[...], row_hot)
+    part = project(columns, sky, pb_ref[...], lambda v: dot_nn(v, hot_back[...]), row_hot)
     quad = jnp.broadcast_to(total(binned * sky), (1, LANES))
     for g in range(rows):
         send_ref[g, 0:1, 0:LANES] = part[g : g + 1]
@@ -431,16 +441,17 @@
         got,
         scratch=[pltpu.VMEM((rows, NBASE_DEV), F32), pltpu.VMEM((8, slots), F32)],
     )
-    took, pack = lax.optimization_barrier((other_core(give), pack))
+    backs = call(turn_kernel, [shape((slots, PB_DEV), BF), shape((slots, NBASE_DEV), BF)], pb_hot, base_hot)
+    took, pack, *backs = lax.optimization_barrier((other_core(give), pack, *backs))
     other = other_core(pack)
     sent = call(sum_kernel, [everyone], keep, took)[0]
     sent, rhs, rhs_map = call(
-        functools.partial(first_kernel, samples, n_pix), [everyone, vector, shape((pch, PB_DEV), F32)], exchange(sent), pack, other, pb_hot, base_hot
+        functools.partial(first_kernel, samples, n_pix), [everyone, vector, shape((pch, PB_DEV), F32)], exchange(sent), pack, other, pb_hot, base_hot, *backs
     )
     sent, state = call(
         functools.partial(second_kernel, samples, n_pix),
         [shape((rows, 1, 2 * LANES), F32), shape((6, rows, NBASE_DEV), F32)],
-        exchange(sent), pack, pb_hot, base_hot, rhs, rhs_map, more,
+        exchange(sent), pack, pb_hot, base_hot, *backs, rhs, rhs_map, more,
     )
     own = shape((1, NBASE_DEV), F32)
     return tuple(call(functools.partial(last_kernel, samples, n_pix), [own, own], exchange(sent), state))

time: 68.9 us -> 68.6 us (level)
    pallas_call x7 -> x8, Pallas kernels: 4.13 us -> 4.2 us  [call(): pl.pallas_call(kernel, out_shape=outs, in_specs=[vmem] * len(args), out_s...]
  transfers between devices with their start and end apart: 3 -> 3, of which waited for: 2 -> 2; matrix products, arithmetic and copies ran while one was open for 0% -> 0% of each run, Pallas kernels for 1% -> 2%
where the time goes in v6:
time: 68.6 us; the launch traced here: 68.4 us
  blocking collectives  54 us (79%)
  Pallas kernels  11.9 us (17%)
  waiting for transfers between devices  1 us (1%)
  starting transfers between devices  0.76 us (1%)
  between operations  0.73 us (1%)
    all_to_all x4, blocking collectives, exchange(): return lax.all_to_all(x, AXES, split_axis=0, concat_axis=0, tiled=True)  54 us
    pallas_call x1, Pallas kernels, body(): pl.pallas_call(functools.partial(bin_kernel, n_det, n_pix, group), out_sh...  7.66 us
    pallas_call x8, Pallas kernels, call(): pl.pallas_call(kernel, out_shape=outs, in_specs=[vmem] * len(args), out_s...  4.2 us
  transfers between devices with their start and end apart: 3, of which 2 were waited for; matrix products, arithmetic and copies ran while one was open for 0% of the time, Pallas kernels for 2%

profile of v6, /device:TPU:0, one launch (start us, length us, event | category | flops | bytes accessed | tf_op | source)
XLA Modules:
  0.0 68.4 jit_solution(1597226474927293200)
XLA Ops:
  0.6 0.0 copy-start.2
  0.6 0.0 copy-start
  0.7 0.0 copy-start.1
  0.7 0.0 copy-start.3
  0.7 7.7 %shard_map.68 = (bf16[32,32,128]{2,1,0:T(8,128)(2,1)S(1)}, f32[256,256]{1,0:T(8,128)S(1)}, f32[256,256]{1,0:T(8,128)S(1)}, f32[256,256]{1,0:T(8,128)S(1)}, bf16[256,512]{1,0:T(8,128)(2,1)S(1)}) custom-call(f32[1,256,128]{2,1,0:T(8,128)} %ts_ref.1, bf16[128,256,256]{2,1,0:T(8,128)(2,1)} %bitcast.4, s32[1,256]{1,0:T(1,128)} %bitcast.2, s32[1,256]{1,0:T(1,128)} %loc_ref.1), custom_call_target="tpu_custom_call" | custom-call | flops 100000000 | bytes 33554432 | tf_op jit(solution)/shard_map/pallas_call | solution.py:406
  8.3 0.5 collective-permute-start
  8.9 0.0 copy-done.2
  8.9 0.0 copy-done.3
  8.9 1.0 %shard_map.69 = (f32[32,32,128]{2,1,0:T(8,128)S(1)}, bf16[32,40,128]{2,1,0:T(8,128)(2,1)S(1)}) custom-call(f32[1,256,128]{2,1,0:T(8,128)S(1)} %copy-done, s32[1,256]{1,0:T(1,128)S(1)} %bitcast.3, s32[1,256]{1,0:T(1,128)S(1)} %copy-done.2, s32[1,256]{1,0:T(1,128)S(1)} %copy-done.3, f32[256,256]{1,0:T(8,128)S(1)} %get-tuple-element.26.hit_ref, ...), custom_call_target="tpu_custom_call" | custom-call | flops 100000000 | bytes 4000000 | tf_op jit(solution)/shard_map/pallas_call | solution.py:376
  9.8 0.2 collective-permute-done.took_ref
  10.0 0.1 shard_map.70
  10.1 24.8 %all_to_all.20.got_ref = bf16[32,72,128]{2,1,0:T(8,128)(2,1)S(1)} all-to-all(bf16[32,72,128]{2,1,0:T(8,128)(2,1)S(1)} %shard_map.70), channel_id=1, replica_groups=mesh['det'=4,'pix'=8] {'det','pix'}, dimensions={0} | all-to-all | bytes 1179648 | tf_op jit(solution)/shard_map/all_to_all | solution.py:388
  34.9 0.7 %shard_map.71 = (f32[16,128]{1,0:T(8,128)S(1)}, f32[16,128]{1,0:T(8,128)S(1)}, bf16[64,2176]{1,0:T(8,128)(2,1)S(1)}, bf16[64,2048]{1,0:T(8,128)(2,1)S(1)}, bf16[...) custom-call(bf16[32,72,128]{2,1,0:T(8,128)(2,1)S(1)} %all_to_all.20.got_ref), custom_call_target="tpu_custom_call" | custom-call | flops 100000000 | bytes 4000000 | tf_op jit(solution)/shard_map/pallas_call | solution.py:376
  35.6 0.1 collective-permute-start.1
  35.7 0.3 shard_map.72
  36.1 0.8 %collective-permute-done.1.took_ref = f32[16,128]{1,0:T(8,128)S(1)} collective-permute-done((f32[16,128]{1,0:T(8,128)S(1)}, f32[16,128]{1,0:T(8,128)S(1)}, u32[]{:S(2)}, u32[]{:S(2)}) %collective-permute-start.1) | collective-permute-done | bytes 8224 | tf_op jit(solution)/shard_map/ppermute | solution.py:392
  36.9 0.2 collective-permute-start.2
  37.0 9.8 %all_to_all.21.got_ref = bf16[32,16,128]{2,1,0:T(8,128)(2,1)S(1)} all-to-all(bf16[32,16,128]{2,1,0:T(8,128)(2,1)S(1)} %shard_map.73), channel_id=1, replica_groups=mesh['det'=4,'pix'=8] {'det','pix'}, dimensions={0} | all-to-all | bytes 262144 | tf_op jit(solution)/shard_map/all_to_all | solution.py:388
  46.9 0.0 collective-permute-done.2.other_ref
  46.9 0.8 %shard_map.74 = (bf16[32,16,128]{2,1,0:T(8,128)(2,1)S(1)}, f32[32,128]{1,0:T(8,128)S(1)}, f32[64,64]{1,0:T(8,128)S(1)}) custom-call(bf16[32,16,128]{2,1,0:T(8,128)(2,1)S(1)} %all_to_all.21.got_ref, bf16[64,2176]{1,0:T(8,128)(2,1)S(1)} %get-tuple-element.41.pack_ref, bf16[64,2176]{1,0:T(8,128)(2,1)S(1)} %collective-permute-done.2.other_ref, ...), custom_call_target="tpu_custom_call" | custom-call | flops 100000000 | bytes 4000000 | tf_op jit(solution)/shard_map/pallas_call | solution.py:376
  47.7 10.0 %all_to_all.22.got_ref = bf16[32,16,128]{2,1,0:T(8,128)(2,1)S(1)} all-to-all(bf16[32,16,128]{2,1,0:T(8,128)(2,1)S(1)} %get-tuple-element.44), channel_id=1, replica_groups=mesh['det'=4,'pix'=8] {'det','pix'}, dimensions={0} | all-to-all | bytes 262144 | tf_op jit(solution)/shard_map/all_to_all | solution.py:388
  57.6 0.7 %shard_map.75 = (f32[32,1,256]{2,1,0:T(1,128)S(1)}, f32[6,32,128]{2,1,0:T(8,128)S(1)}) custom-call(bf16[32,16,128]{2,1,0:T(8,128)(2,1)S(1)} %all_to_all.22.got_ref, bf16[64,2176]{1,0:T(8,128)(2,1)S(1)} %get-tuple-element.41.pack_ref, bf16[64,2048]{1,0:T(8,128)(2,1)S(1)} %get-tuple-element.36.pb_ref, bf16[128,2048]{1,0:T(8,128)(2,1)S(1)} %get-tuple-element.37.hot_ref, ...), custom_call_target="tpu_custom_call" | custom-call | flops 100000000 | bytes 4000000 | tf_op jit(solution)/shard_map/pallas_call | solution.py:376
  58.4 9.4 %all_to_all.23.got_ref = f32[32,1,256]{2,1,0:T(1,128)S(1)} all-to-all(f32[32,1,256]{2,1,0:T(1,128)S(1)} %get-tuple-element.48), channel_id=1, replica_groups=mesh['det'=4,'pix'=8] {'det','pix'}, dimensions={0} | all-to-all | bytes 65536 | tf_op jit(solution)/shard_map/all_to_all | solution.py:388
  67.9 0.6 shard_map.76
  (3 shorter events, 0.0 us)
Async XLA Ops:
  0.6 8.2 %copy-start.2 = (s32[1,256]{1,0:T(1,128)S(1)}, s32[1,256]{1,0:T(1,128)}, u32[]{:S(2)}) copy-start(s32[1,256]{1,0:T(1,128)} %loc_ref.1) | copy-start | bytes 3076
  0.6 8.2 %copy-start = (f32[1,256,128]{2,1,0:T(8,128)S(1)}, f32[1,256,128]{2,1,0:T(8,128)}, u32[]{:S(2)}) copy-start(f32[1,256,128]{2,1,0:T(8,128)} %ts_ref.1) | copy-start | bytes 393220
  0.7 8.2 %copy-start.1 = (s32[1,256,1]{1,2,0:T(1,128)S(1)}, s32[1,256,1]{1,2,0:T(1,128)}, u32[]{:S(2)}) copy-start(s32[1,256,1]{1,2,0:T(1,128)} %param.7) | copy-start | bytes 3076
  0.7 8.2 %copy-start.3 = (s32[1,256]{1,0:T(1,128)S(1)}, s32[1,256]{1,0:T(1,128)}, u32[]{:S(2)}) copy-start(s32[1,256]{1,0:T(1,128)} %base_ref.1) | copy-start | bytes 3076
  8.3 1.7 %collective-permute-start = (bf16[32,32,128]{2,1,0:T(8,128)(2,1)S(1)}, bf16[32,32,128]{2,1,0:T(8,128)(2,1)S(1)}, u32[]{:S(2)}, u32[]{:S(2)}) collective-permute-start(bf16[32,32,128]{2,1,0:T(8,128)(2,1)S(1)} %get-tuple-element.31), channel_id=1, source_target_pairs={{0,8},{8,0},{16,24},{24,16},{1,9},{9,1},{17,25},{25,17},{2,10},{10... | collective-permute-start | bytes 786440 | tf_op jit(solution)/shard_map/ppermute | solution.py:392
  35.6 1.2 %collective-permute-start.1 = (f32[16,128]{1,0:T(8,128)S(1)}, f32[16,128]{1,0:T(8,128)S(1)}, u32[]{:S(2)}, u32[]{:S(2)}) collective-permute-start(f32[16,128]{1,0:T(8,128)S(1)} %get-tuple-element.34), channel_id=1, source_target_pairs={{0,8},{8,0},{16,24},{24,16},{1,9},{9,1},{17,25},{25,17},{2,10},{10... | collective-permute-start | bytes 24584 | tf_op jit(solution)/shard_map/ppermute | solution.py:392
  36.9 10.0 %collective-permute-start.2 = (bf16[64,2176]{1,0:T(8,128)(2,1)S(1)}, bf16[64,2176]{1,0:T(8,128)(2,1)S(1)}, u32[]{:S(2)}, u32[]{:S(2)}) collective-permute-start(bf16[64,2176]{1,0:T(8,128)(2,1)S(1)} %get-tuple-element.41.pack_ref), channel_id=1, source_target_pairs={{0,8},{8,0},{16,24},{24,16},{1,9},{9,1},{17,25},{25,17},{2,10},{10... | collective-permute-start | bytes 835592 | tf_op jit(solution)/shard_map/ppermute | solution.py:392

commit v7 on v6

--- a/solution.py
+++ b/solution.py
@@ -80,11 +80,11 @@
     ones = jnp.ones((pixels, LANES), BF)
     row = iota((8, 2 * samples), 0) - jnp.where(iota((8, 2 * samples), 1) < samples, 0, 3)
 
-    def row_sums(first, many):
+    def row_sums(first, many, every=4):
         acc = jnp.zeros((samples, LANES), F32)
         for j in range(2 * many):
             w = w_s[first + j // 2, (j % 2) * samples : (j % 2 + 1) * samples, :]
-            if j % 4 == 3:
+            if j % every == every - 1:
                 sums = dot_nn(w, ones)
             else:
                 w = w.astype(F32)
@@ -125,10 +125,10 @@
     sums = lax.fori_loop(1, steps, step, row_sums(0, short))
     begin, quarter = steps * short, short // 2
     wait(ends[0])
-    after = row_sums(begin, quarter)
+    after = row_sums(begin, quarter, 3)
     terms(begin - short, short, sums)
     wait(ends[1])
-    last = row_sums(begin + quarter, quarter)
+    last = row_sums(begin + quarter, quarter, 2)
     terms(begin, quarter, after)
     for copy in indices:
         copy.wait()
@@ -269,7 +269,7 @@
     return pack_ref[:, :slots], inv[:, 0:PB_DEV] + inv[:, PB_DEV:]
 
 
-def owner_kernel(pch, n_pix, got_ref, keep_ref, give_ref, pack_ref, pb_ref, hot_ref, more_ref, work, mean):
+def owner_kernel(pch, n_pix, got_ref, keep_ref, give_ref, col_ref, inv_ref, pb_ref, hot_ref, work, mean):
     rows = got_ref.shape[0]
     half = pch // 2
     slots = rows * CAP
@@ -283,28 +283,31 @@
     for i in range(rows // 2):
         cols = slice(i * LANES, (i + 1) * LANES)
         halves = pair(got_ref[2 * i, 0:half, :].astype(F32), got_ref[2 * i + 1, 0:half, :].astype(F32), swap_halves)
-        pack_ref[0:half, cols] = halves[0].astype(BF)
-        pack_ref[half:, cols] = halves[1].astype(BF)
+        col_ref[0:half, cols] = halves[0].astype(BF)
+        col_ref[half:, cols] = halves[1].astype(BF)
         tiles = [got_ref[2 * i + k, 2 * half :, :].astype(F32) for k in (0, 1)]
         one, two = pair(*tiles, swap_halves)
         pb_ref[:, cols] = jnp.where(pb_of == one[0:1].astype(BF), yes, no)
         hot_ref[:, cols] = jnp.where(base_of == two[0:1].astype(BF), yes, no)
         mean[0:1, cols] = one[1:2] + two[1:2] + one[2:3]
-        for k in (0, 1):
-            more_ref[2 * i + k : 2 * i + k + 1, :] = tiles[k][3:4] + 1.0
     maps = jnp.concatenate(maps, axis=0)
     inv = 1.0 / (maps[:, 0:PB_DEV] + 1.0)
-    pack_ref[:, slots:] = jnp.concatenate([v.astype(F32) for v in split2(inv)], axis=1).astype(BF)
+    inv_ref[...] = inv
     sky = maps[:, PB_DEV:] * inv
     collapse = lambda v: dot_nt(v, hot_ref[...])
-    part = project(pack_ref[:, :slots], sky, pb_ref[...], collapse, row_mask(rows, slots), mean[0:1, :])
+    part = project(col_ref[...], sky, pb_ref[...], collapse, row_mask(rows, slots), mean[0:1, :])
     halves_out(part, keep_ref, give_ref, work)
 
 
-def turn_kernel(pb_ref, hot_ref, pb_back_ref, hot_back_ref):
-    for k in range(0, pb_ref.shape[1], LANES):
+def turn_kernel(got_ref, col_ref, inv_ref, pb_ref, hot_ref, pack_ref, pb_back_ref, hot_back_ref, more_ref):
+    pch, slots = col_ref.shape
+    pack_ref[:, :slots] = col_ref[...]
+    pack_ref[:, slots:] = jnp.concatenate([v.astype(F32) for v in split2(inv_ref[...])], axis=1).astype(BF)
+    for k in range(0, slots, LANES):
         for ref, back in ((pb_ref, pb_back_ref), (hot_ref, hot_back_ref)):
             back[k : k + LANES, :] = ref[:, k : k + LANES].astype(F32).T.astype(BF)
+    for g in range(got_ref.shape[0]):
+        more_ref[g : g + 1, :] = got_ref[g, pch:, :].astype(F32)[3:4] + 1.0
 
 
 def first_kernel(samples, n_pix, got_ref, pack_ref, other_ref, pb_ref, hot_ref, pb_back, hot_back, send_ref, rhs_ref, map_ref):
@@ -435,14 +438,21 @@
     part = shape((rows // 2, NBASE_DEV), F32)
 
     everyone = shape((rows, rows // 2, NBASE_DEV), BF)
-    keep, give, pack, pb_hot, base_hot, more = call(
+    keep, give, col_t, inv, pb_hot, base_hot = call(
         functools.partial(owner_kernel, pch, n_pix),
-        [part, part, shape((pch, slots + LANES), BF), shape((PB_DEV, slots), BF), shape((NBASE_DEV, slots), BF), vector],
+        [
+            part, part, shape((pch, slots), BF), shape((pch, PB_DEV), F32),
+            shape((PB_DEV, slots), BF), shape((NBASE_DEV, slots), BF),
+        ],
         got,
         scratch=[pltpu.VMEM((rows, NBASE_DEV), F32), pltpu.VMEM((8, slots), F32)],
     )
-    backs = call(turn_kernel, [shape((slots, PB_DEV), BF), shape((slots, NBASE_DEV), BF)], pb_hot, base_hot)
-    took, pack, *backs = lax.optimization_barrier((other_core(give), pack, *backs))
+    turned = call(
+        turn_kernel,
+        [shape((pch, slots + LANES), BF), shape((slots, PB_DEV), BF), shape((slots, NBASE_DEV), BF), vector],
+        got, col_t, inv, pb_hot, base_hot,
+    )
+    took, pack, *backs, more = lax.optimization_barrier((other_core(give), *turned))
     other = other_core(pack)
     sent = call(sum_kernel, [everyone], keep, took)[0]
     sent, rhs, rhs_map = call(

time: 68.6 us -> 68.7 us (level)
  no operation moved by 1% of the time
where the time goes in v7:
time: 68.7 us; the launch traced here: 68.5 us
  blocking collectives  54 us (79%)
  Pallas kernels  12 us (17%)
  waiting for transfers between devices  0.95 us (1%)
  starting transfers between devices  0.75 us (1%)
  between operations  0.73 us (1%)
    all_to_all x4, blocking collectives, exchange(): return lax.all_to_all(x, AXES, split_axis=0, concat_axis=0, tiled=True)  54 us
    pallas_call x1, Pallas kernels, body(): pl.pallas_call(functools.partial(bin_kernel, n_det, n_pix, group), out_sh...  7.74 us
    pallas_call x8, Pallas kernels, call(): pl.pallas_call(kernel, out_shape=outs, in_specs=[vmem] * len(args), out_s...  4.26 us
  transfers between devices with their start and end apart: 3, of which 2 were waited for; matrix products, arithmetic and copies ran while one was open for 0% of the time, Pallas kernels for 2%

profile of v7, /device:TPU:0, one launch (start us, length us, event | category | flops | bytes accessed | tf_op | source)
XLA Modules:
  0.0 68.5 jit_solution(2457940846979161820)
XLA Ops:
  0.6 0.0 copy-start.2
  0.6 0.0 copy-start
  0.7 0.0 copy-start.1
  0.7 0.0 copy-start.3
  0.7 7.7 %shard_map.68 = (bf16[32,32,128]{2,1,0:T(8,128)(2,1)S(1)}, f32[256,256]{1,0:T(8,128)S(1)}, f32[256,256]{1,0:T(8,128)S(1)}, f32[256,256]{1,0:T(8,128)S(1)}, bf16[256,512]{1,0:T(8,128)(2,1)S(1)}) custom-call(f32[1,256,128]{2,1,0:T(8,128)} %ts_ref.1, bf16[128,256,256]{2,1,0:T(8,128)(2,1)} %bitcast.4, s32[1,256]{1,0:T(1,128)} %bitcast.2, s32[1,256]{1,0:T(1,128)} %loc_ref.1), custom_call_target="tpu_custom_call" | custom-call | flops 100000000 | bytes 33554432 | tf_op jit(solution)/shard_map/pallas_call | solution.py:409
  8.4 0.5 collective-permute-start
  8.9 0.0 copy-done.2
  8.9 0.0 copy-done
  8.9 1.0 %shard_map.69 = (f32[32,32,128]{2,1,0:T(8,128)S(1)}, bf16[32,40,128]{2,1,0:T(8,128)(2,1)S(1)}) custom-call(f32[1,256,128]{2,1,0:T(8,128)S(1)} %copy-done, s32[1,256]{1,0:T(1,128)S(1)} %bitcast.3, s32[1,256]{1,0:T(1,128)S(1)} %copy-done.2, s32[1,256]{1,0:T(1,128)S(1)} %copy-done.3, f32[256,256]{1,0:T(8,128)S(1)} %get-tuple-element.29.hit_ref, ...), custom_call_target="tpu_custom_call" | custom-call | flops 100000000 | bytes 4000000 | tf_op jit(solution)/shard_map/pallas_call | solution.py:379
  9.9 0.2 collective-permute-done.took_ref
  10.1 0.1 shard_map.70
  10.2 24.8 %all_to_all.20.got_ref = bf16[32,72,128]{2,1,0:T(8,128)(2,1)S(1)} all-to-all(bf16[32,72,128]{2,1,0:T(8,128)(2,1)S(1)} %shard_map.70), channel_id=1, replica_groups=mesh['det'=4,'pix'=8] {'det','pix'}, dimensions={0} | all-to-all | bytes 1179648 | tf_op jit(solution)/shard_map/all_to_all | solution.py:391
  35.0 0.7 %shard_map.71 = (f32[16,128]{1,0:T(8,128)S(1)}, f32[16,128]{1,0:T(8,128)S(1)}, bf16[64,2048]{1,0:T(8,128)(2,1)S(1)}, f32[64,64]{1,0:T(8,128)S(1)}, bf16[64,2048]...) custom-call(bf16[32,72,128]{2,1,0:T(8,128)(2,1)S(1)} %all_to_all.20.got_ref), custom_call_target="tpu_custom_call" | custom-call | flops 100000000 | bytes 4000000 | tf_op jit(solution)/shard_map/pallas_call | solution.py:379
  35.7 0.1 collective-permute-start.1
  35.8 0.4 shard_map.72
  36.2 0.8 %collective-permute-done.1.took_ref = f32[16,128]{1,0:T(8,128)S(1)} collective-permute-done((f32[16,128]{1,0:T(8,128)S(1)}, f32[16,128]{1,0:T(8,128)S(1)}, u32[]{:S(2)}, u32[]{:S(2)}) %collective-permute-start.1) | collective-permute-done | bytes 8224 | tf_op jit(solution)/shard_map/ppermute | solution.py:395
  37.0 0.2 collective-permute-start.2
  37.1 9.8 %all_to_all.21.got_ref = bf16[32,16,128]{2,1,0:T(8,128)(2,1)S(1)} all-to-all(bf16[32,16,128]{2,1,0:T(8,128)(2,1)S(1)} %shard_map.73), channel_id=1, replica_groups=mesh['det'=4,'pix'=8] {'det','pix'}, dimensions={0} | all-to-all | bytes 262144 | tf_op jit(solution)/shard_map/all_to_all | solution.py:391
  46.9 0.0 collective-permute-done.2.other_ref
  47.0 0.8 %shard_map.74 = (bf16[32,16,128]{2,1,0:T(8,128)(2,1)S(1)}, f32[32,128]{1,0:T(8,128)S(1)}, f32[64,64]{1,0:T(8,128)S(1)}) custom-call(bf16[32,16,128]{2,1,0:T(8,128)(2,1)S(1)} %all_to_all.21.got_ref, bf16[64,2176]{1,0:T(8,128)(2,1)S(1)} %get-tuple-element.47.pack_ref, bf16[64,2176]{1,0:T(8,128)(2,1)S(1)} %collective-permute-done.2.other_ref, ...), custom_call_target="tpu_custom_call" | custom-call | flops 100000000 | bytes 4000000 | tf_op jit(solution)/shard_map/pallas_call | solution.py:379
  47.7 10.0 %all_to_all.22.got_ref = bf16[32,16,128]{2,1,0:T(8,128)(2,1)S(1)} all-to-all(bf16[32,16,128]{2,1,0:T(8,128)(2,1)S(1)} %get-tuple-element.50), channel_id=1, replica_groups=mesh['det'=4,'pix'=8] {'det','pix'}, dimensions={0} | all-to-all | bytes 262144 | tf_op jit(solution)/shard_map/all_to_all | solution.py:391
  57.7 0.7 %shard_map.75 = (f32[32,1,256]{2,1,0:T(1,128)S(1)}, f32[6,32,128]{2,1,0:T(8,128)S(1)}) custom-call(bf16[32,16,128]{2,1,0:T(8,128)(2,1)S(1)} %all_to_all.22.got_ref, bf16[64,2176]{1,0:T(8,128)(2,1)S(1)} %get-tuple-element.47.pack_ref, bf16[64,2048]{1,0:T(8,128)(2,1)S(1)} %get-tuple-element.40.pb_ref, bf16[128,2048]{1,0:T(8,128)(2,1)S(1)} %get-tuple-element.41.hot_ref, ...), custom_call_target="tpu_custom_call" | custom-call | flops 100000000 | bytes 4000000 | tf_op jit(solution)/shard_map/pallas_call | solution.py:379
  58.5 9.4 %all_to_all.23.got_ref = f32[32,1,256]{2,1,0:T(1,128)S(1)} all-to-all(f32[32,1,256]{2,1,0:T(1,128)S(1)} %get-tuple-element.54), channel_id=1, replica_groups=mesh['det'=4,'pix'=8] {'det','pix'}, dimensions={0} | all-to-all | bytes 65536 | tf_op jit(solution)/shard_map/all_to_all | solution.py:391
  67.9 0.6 shard_map.76
  (3 shorter events, 0.0 us)
Async XLA Ops:
  0.6 8.3 %copy-start.2 = (s32[1,256]{1,0:T(1,128)S(1)}, s32[1,256]{1,0:T(1,128)}, u32[]{:S(2)}) copy-start(s32[1,256]{1,0:T(1,128)} %loc_ref.1) | copy-start | bytes 3076
  0.6 8.3 %copy-start = (f32[1,256,128]{2,1,0:T(8,128)S(1)}, f32[1,256,128]{2,1,0:T(8,128)}, u32[]{:S(2)}) copy-start(f32[1,256,128]{2,1,0:T(8,128)} %ts_ref.1) | copy-start | bytes 393220
  0.7 8.3 %copy-start.1 = (s32[1,256,1]{1,2,0:T(1,128)S(1)}, s32[1,256,1]{1,2,0:T(1,128)}, u32[]{:S(2)}) copy-start(s32[1,256,1]{1,2,0:T(1,128)} %param.7) | copy-start | bytes 3076
  0.7 8.3 %copy-start.3 = (s32[1,256]{1,0:T(1,128)S(1)}, s32[1,256]{1,0:T(1,128)}, u32[]{:S(2)}) copy-start(s32[1,256]{1,0:T(1,128)} %base_ref.1) | copy-start | bytes 3076
  8.4 1.7 %collective-permute-start = (bf16[32,32,128]{2,1,0:T(8,128)(2,1)S(1)}, bf16[32,32,128]{2,1,0:T(8,128)(2,1)S(1)}, u32[]{:S(2)}, u32[]{:S(2)}) collective-permute-start(bf16[32,32,128]{2,1,0:T(8,128)(2,1)S(1)} %get-tuple-element.34), channel_id=1, source_target_pairs={{0,8},{8,0},{16,24},{24,16},{1,9},{9,1},{17,25},{25,17},{2,10},{10... | collective-permute-start | bytes 786440 | tf_op jit(solution)/shard_map/ppermute | solution.py:395
  35.7 1.2 %collective-permute-start.1 = (f32[16,128]{1,0:T(8,128)S(1)}, f32[16,128]{1,0:T(8,128)S(1)}, u32[]{:S(2)}, u32[]{:S(2)}) collective-permute-start(f32[16,128]{1,0:T(8,128)S(1)} %get-tuple-element.37), channel_id=1, source_target_pairs={{0,8},{8,0},{16,24},{24,16},{1,9},{9,1},{17,25},{25,17},{2,10},{10... | collective-permute-start | bytes 24584 | tf_op jit(solution)/shard_map/ppermute | solution.py:395
  37.0 10.0 %collective-permute-start.2 = (bf16[64,2176]{1,0:T(8,128)(2,1)S(1)}, bf16[64,2176]{1,0:T(8,128)(2,1)S(1)}, u32[]{:S(2)}, u32[]{:S(2)}) collective-permute-start(bf16[64,2176]{1,0:T(8,128)(2,1)S(1)} %get-tuple-element.47.pack_ref), channel_id=1, source_target_pairs={{0,8},{8,0},{16,24},{24,16},{1,9},{9,1},{17,25},{25,17},{2,10},{10... | collective-permute-start | bytes 835592 | tf_op jit(solution)/shard_map/ppermute | solution.py:395

commit v8 on v7

--- a/solution.py
+++ b/solution.py
@@ -156,7 +156,7 @@
         for o, tile in zip((2 * i, 2 * i + 1), pair(first[:, cols], second[:, cols], swap_halves)):
             tile = tile.astype(ref.dtype)
             for d in range(n_det):
-                ref[d * n_pix + o, 0:half, :] = tile[d * half : (d + 1) * half]
+                ref[o * n_det + d, 0:half, :] = tile[d * half : (d + 1) * half]
 
 
 def binned(n_det, n_pix, which, hit_ref, dat_ref, pb_hot, ref):
@@ -199,7 +199,7 @@
         for o, tile in zip((2 * i, 2 * i + 1), pair(where[0:8, cols], where[8:16, cols], swap_halves)):
             tile = jnp.where(r8 == 3, count, tile).astype(BF)
             for d in range(n_det):
-                rest_ref[d * n_pix + o, half:, :] = tile
+                rest_ref[o * n_det + d, half:, :] = tile
 
 
 def join_kernel(mine_ref, took_ref, rest_ref, send_ref):
@@ -254,10 +254,10 @@
         send_ref[g] = part
 
 
-def total_of(got_ref, n_pix):
+def total_of(got_ref):
     sums = [None, None]
     for g in range(got_ref.shape[0]):
-        core = (g // n_pix) % 2
+        core = g % 2
         term = got_ref[g].astype(F32)
         sums[core] = term if sums[core] is None else sums[core] + term
     return jnp.concatenate(sums, axis=0)
@@ -269,7 +269,7 @@
     return pack_ref[:, :slots], inv[:, 0:PB_DEV] + inv[:, PB_DEV:]
 
 
-def owner_kernel(pch, n_pix, got_ref, keep_ref, give_ref, col_ref, inv_ref, pb_ref, hot_ref, work, mean):
+def owner_kernel(pch, got_ref, keep_ref, give_ref, col_ref, inv_ref, pb_ref, hot_ref, work, mean):
     rows = got_ref.shape[0]
     half = pch // 2
     slots = rows * CAP
@@ -278,7 +278,7 @@
     yes, no = jnp.ones((1, LANES), BF), jnp.zeros((1, LANES), BF)
     maps = [jnp.zeros((half, LANES), F32), jnp.zeros((half, LANES), F32)]
     for g in range(rows):
-        core = (g // n_pix) % 2
+        core = g % 2
         maps[core] = maps[core] + got_ref[g, half : 2 * half, :].astype(F32)
     for i in range(rows // 2):
         cols = slice(i * LANES, (i + 1) * LANES)
@@ -310,8 +310,8 @@
         more_ref[g : g + 1, :] = got_ref[g, pch:, :].astype(F32)[3:4] + 1.0
 
 
-def first_kernel(samples, n_pix, got_ref, pack_ref, other_ref, pb_ref, hot_ref, pb_back, hot_back, send_ref, rhs_ref, map_ref):
-    rhs = total_of(got_ref, n_pix) * (-1.0 / samples)
+def first_kernel(samples, got_ref, pack_ref, other_ref, pb_ref, hot_ref, pb_back, hot_back, send_ref, rhs_ref, map_ref):
+    rhs = total_of(got_ref) * (-1.0 / samples)
     rhs_ref[...] = rhs
     rows = rhs.shape[0]
     slots = rows * CAP
@@ -329,11 +329,11 @@
 
 
 def second_kernel(
-    samples, n_pix, got_ref, pack_ref, pb_ref, hot_ref, pb_back, hot_back, rhs_ref, map_ref, more_ref, send_ref, state_ref
+    samples, got_ref, pack_ref, pb_ref, hot_ref, pb_back, hot_back, rhs_ref, map_ref, more_ref, send_ref, state_ref
 ):
     rhs = rhs_ref[...]
     more = more_ref[...]
-    image = more * rhs - total_of(got_ref, n_pix) * (1.0 / samples)
+    image = more * rhs - total_of(got_ref) * (1.0 / samples)
     rows = rhs.shape[0]
     columns, inv = columns_of(pack_ref)
     row_hot = row_mask(rows, columns.shape[1])
@@ -360,8 +360,8 @@
     state_ref[5] = jnp.broadcast_to(total(scaled * heading), (rows, LANES))
 
 
-def last_kernel(samples, n_pix, got_ref, state_ref, levels_ref, error_ref):
-    me = lax.axis_index("det") * n_pix + lax.axis_index("pix")
+def last_kernel(samples, n_det, got_ref, state_ref, levels_ref, error_ref):
+    me = lax.axis_index("pix") * n_det + lax.axis_index("det")
     acc = got_ref[0]
     for g in range(1, got_ref.shape[0]):
         acc = acc + got_ref[g]
@@ -388,7 +388,7 @@
 
 
 def exchange(x):
-    return lax.all_to_all(x, AXES, split_axis=0, concat_axis=0, tiled=True)
+    return lax.all_to_all(x, ("pix", "det"), split_axis=0, concat_axis=0, tiled=True)
 
 
 def other_core(x):
@@ -439,7 +439,7 @@
 
     everyone = shape((rows, rows // 2, NBASE_DEV), BF)
     keep, give, col_t, inv, pb_hot, base_hot = call(
-        functools.partial(owner_kernel, pch, n_pix),
+        functools.partial(owner_kernel, pch),
         [
             part, part, shape((pch, slots), BF), shape((pch, PB_DEV), F32),
             shape((PB_DEV, slots), BF), shape((NBASE_DEV, slots), BF),
@@ -456,15 +456,15 @@
     other = other_core(pack)
     sent = call(sum_kernel, [everyone], keep, took)[0]
     sent, rhs, rhs_map = call(
-        functools.partial(first_kernel, samples, n_pix), [everyone, vector, shape((pch, PB_DEV), F32)], exchange(sent), pack, other, pb_hot, base_hot, *backs
+        functools.partial(first_kernel, samples), [everyone, vector, shape((pch, PB_DEV), F32)], exchange(sent), pack, other, pb_hot, base_hot, *backs
     )
     sent, state = call(
-        functools.partial(second_kernel, samples, n_pix),
+        functools.partial(second_kernel, samples),
         [shape((rows, 1, 2 * LANES), F32), shape((6, rows, NBASE_DEV), F32)],
         exchange(sent), pack, pb_hot, base_hot, *backs, rhs, rhs_map, more,
     )
     own = shape((1, NBASE_DEV), F32)
-    return tuple(call(functools.partial(last_kernel, samples, n_pix), [own, own], exchange(sent), state))
+    return tuple(call(functools.partial(last_kernel, samples, n_det), [own, own], exchange(sent), state))
 
 
 def solution(mesh):

time: 68.7 us -> 68.8 us (level)
  no operation moved by 1% of the time
where the time goes in v8:
time: 68.8 us; the launch traced here: 68.6 us
  blocking collectives  54.1 us (79%)
  Pallas kernels  12 us (17%)
  waiting for transfers between devices  0.95 us (1%)
  starting transfers between devices  0.75 us (1%)
  between operations  0.73 us (1%)
    all_to_all x4, blocking collectives, exchange(): lax.all_to_all(x, ('pix', 'det'), split_axis=0, concat_axis=0, tiled=True)  54.1 us
    pallas_call x1, Pallas kernels, body(): pl.pallas_call(functools.partial(bin_kernel, n_det, n_pix, group), out_sh...  7.74 us
    pallas_call x8, Pallas kernels, call(): pl.pallas_call(kernel, out_shape=outs, in_specs=[vmem] * len(args), out_s...  4.27 us
  transfers between devices with their start and end apart: 3, of which 2 were waited for; matrix products, arithmetic and copies ran while one was open for 0% of the time, Pallas kernels for 2%

profile of v8, /device:TPU:0, one launch (start us, length us, event | category | flops | bytes accessed | tf_op | source)
XLA Modules:
  0.0 68.6 jit_solution(6112233312192228620)
XLA Ops:
  0.6 0.0 copy-start.2
  0.6 0.0 copy-start
  0.7 0.0 copy-start.1
  0.7 0.0 copy-start.3
  0.7 7.7 %shard_map.68 = (bf16[32,32,128]{2,1,0:T(8,128)(2,1)S(1)}, f32[256,256]{1,0:T(8,128)S(1)}, f32[256,256]{1,0:T(8,128)S(1)}, f32[256,256]{1,0:T(8,128)S(1)}, bf16[256,512]{1,0:T(8,128)(2,1)S(1)}) custom-call(f32[1,256,128]{2,1,0:T(8,128)} %ts_ref.1, bf16[128,256,256]{2,1,0:T(8,128)(2,1)} %bitcast.4, s32[1,256]{1,0:T(1,128)} %bitcast.2, s32[1,256]{1,0:T(1,128)} %loc_ref.1), custom_call_target="tpu_custom_call" | custom-call | flops 100000000 | bytes 33554432 | tf_op jit(solution)/shard_map/pallas_call | solution.py:409
  8.4 0.5 collective-permute-start
  8.9 0.0 copy-done.2
  8.9 0.0 copy-done
  8.9 1.0 %shard_map.69 = (f32[32,32,128]{2,1,0:T(8,128)S(1)}, bf16[32,40,128]{2,1,0:T(8,128)(2,1)S(1)}) custom-call(f32[1,256,128]{2,1,0:T(8,128)S(1)} %copy-done, s32[1,256]{1,0:T(1,128)S(1)} %bitcast.3, s32[1,256]{1,0:T(1,128)S(1)} %copy-done.2, s32[1,256]{1,0:T(1,128)S(1)} %copy-done.3, f32[256,256]{1,0:T(8,128)S(1)} %get-tuple-element.29.hit_ref, ...), custom_call_target="tpu_custom_call" | custom-call | flops 100000000 | bytes 4000000 | tf_op jit(solution)/shard_map/pallas_call | solution.py:379
  9.9 0.2 collective-permute-done.took_ref
  10.1 0.1 shard_map.70
  10.2 23.8 %all_to_all.20.got_ref = bf16[32,72,128]{2,1,0:T(8,128)(2,1)S(1)} all-to-all(bf16[32,72,128]{2,1,0:T(8,128)(2,1)S(1)} %shard_map.70), channel_id=1, replica_groups=mesh['det'=4,'pix'=8] {'pix','det'}, dimensions={0} | all-to-all | bytes 1179648 | tf_op jit(solution)/shard_map/all_to_all | solution.py:391
  33.9 0.7 %shard_map.71 = (f32[16,128]{1,0:T(8,128)S(1)}, f32[16,128]{1,0:T(8,128)S(1)}, bf16[64,2048]{1,0:T(8,128)(2,1)S(1)}, f32[64,64]{1,0:T(8,128)S(1)}, bf16[64,2048]...) custom-call(bf16[32,72,128]{2,1,0:T(8,128)(2,1)S(1)} %all_to_all.20.got_ref), custom_call_target="tpu_custom_call" | custom-call | flops 100000000 | bytes 4000000 | tf_op jit(solution)/shard_map/pallas_call | solution.py:379
  34.7 0.1 collective-permute-start.1
  34.8 0.4 shard_map.72
  35.2 0.8 %collective-permute-done.1.took_ref = f32[16,128]{1,0:T(8,128)S(1)} collective-permute-done((f32[16,128]{1,0:T(8,128)S(1)}, f32[16,128]{1,0:T(8,128)S(1)}, u32[]{:S(2)}, u32[]{:S(2)}) %collective-permute-start.1) | collective-permute-done | bytes 8224 | tf_op jit(solution)/shard_map/ppermute | solution.py:395
  35.9 0.2 collective-permute-start.2
  36.1 11.3 %all_to_all.21.got_ref = bf16[32,16,128]{2,1,0:T(8,128)(2,1)S(1)} all-to-all(bf16[32,16,128]{2,1,0:T(8,128)(2,1)S(1)} %shard_map.73), channel_id=1, replica_groups=mesh['det'=4,'pix'=8] {'pix','det'}, dimensions={0} | all-to-all | bytes 262144 | tf_op jit(solution)/shard_map/all_to_all | solution.py:391
  47.4 0.0 collective-permute-done.2.other_ref
  47.4 0.8 %shard_map.74 = (bf16[32,16,128]{2,1,0:T(8,128)(2,1)S(1)}, f32[32,128]{1,0:T(8,128)S(1)}, f32[64,64]{1,0:T(8,128)S(1)}) custom-call(bf16[32,16,128]{2,1,0:T(8,128)(2,1)S(1)} %all_to_all.21.got_ref, bf16[64,2176]{1,0:T(8,128)(2,1)S(1)} %get-tuple-element.47.pack_ref, bf16[64,2176]{1,0:T(8,128)(2,1)S(1)} %collective-permute-done.2.other_ref, ...), custom_call_target="tpu_custom_call" | custom-call | flops 100000000 | bytes 4000000 | tf_op jit(solution)/shard_map/pallas_call | solution.py:379
  48.2 10.0 %all_to_all.22.got_ref = bf16[32,16,128]{2,1,0:T(8,128)(2,1)S(1)} all-to-all(bf16[32,16,128]{2,1,0:T(8,128)(2,1)S(1)} %get-tuple-element.50), channel_id=1, replica_groups=mesh['det'=4,'pix'=8] {'pix','det'}, dimensions={0} | all-to-all | bytes 262144 | tf_op jit(solution)/shard_map/all_to_all | solution.py:391
  58.2 0.7 %shard_map.75 = (f32[32,1,256]{2,1,0:T(1,128)S(1)}, f32[6,32,128]{2,1,0:T(8,128)S(1)}) custom-call(bf16[32,16,128]{2,1,0:T(8,128)(2,1)S(1)} %all_to_all.22.got_ref, bf16[64,2176]{1,0:T(8,128)(2,1)S(1)} %get-tuple-element.47.pack_ref, bf16[64,2048]{1,0:T(8,128)(2,1)S(1)} %get-tuple-element.40.pb_ref, bf16[128,2048]{1,0:T(8,128)(2,1)S(1)} %get-tuple-element.41.hot_ref, ...), custom_call_target="tpu_custom_call" | custom-call | flops 100000000 | bytes 4000000 | tf_op jit(solution)/shard_map/pallas_call | solution.py:379
  59.0 9.0 %all_to_all.23.got_ref = f32[32,1,256]{2,1,0:T(1,128)S(1)} all-to-all(f32[32,1,256]{2,1,0:T(1,128)S(1)} %get-tuple-element.54), channel_id=1, replica_groups=mesh['det'=4,'pix'=8] {'pix','det'}, dimensions={0} | all-to-all | bytes 65536 | tf_op jit(solution)/shard_map/all_to_all | solution.py:391
  68.0 0.6 shard_map.76
  (3 shorter events, 0.0 us)
Async XLA Ops:
  0.6 8.3 %copy-start.2 = (s32[1,256]{1,0:T(1,128)S(1)}, s32[1,256]{1,0:T(1,128)}, u32[]{:S(2)}) copy-start(s32[1,256]{1,0:T(1,128)} %loc_ref.1) | copy-start | bytes 3076
  0.6 8.3 %copy-start = (f32[1,256,128]{2,1,0:T(8,128)S(1)}, f32[1,256,128]{2,1,0:T(8,128)}, u32[]{:S(2)}) copy-start(f32[1,256,128]{2,1,0:T(8,128)} %ts_ref.1) | copy-start | bytes 393220
  0.7 8.3 %copy-start.1 = (s32[1,256,1]{1,2,0:T(1,128)S(1)}, s32[1,256,1]{1,2,0:T(1,128)}, u32[]{:S(2)}) copy-start(s32[1,256,1]{1,2,0:T(1,128)} %param.7) | copy-start | bytes 3076
  0.7 8.3 %copy-start.3 = (s32[1,256]{1,0:T(1,128)S(1)}, s32[1,256]{1,0:T(1,128)}, u32[]{:S(2)}) copy-start(s32[1,256]{1,0:T(1,128)} %base_ref.1) | copy-start | bytes 3076
  8.4 1.7 %collective-permute-start = (bf16[32,32,128]{2,1,0:T(8,128)(2,1)S(1)}, bf16[32,32,128]{2,1,0:T(8,128)(2,1)S(1)}, u32[]{:S(2)}, u32[]{:S(2)}) collective-permute-start(bf16[32,32,128]{2,1,0:T(8,128)(2,1)S(1)} %get-tuple-element.34), channel_id=1, source_target_pairs={{0,8},{8,0},{16,24},{24,16},{1,9},{9,1},{17,25},{25,17},{2,10},{10... | collective-permute-start | bytes 786440 | tf_op jit(solution)/shard_map/ppermute | solution.py:395
  34.7 1.2 %collective-permute-start.1 = (f32[16,128]{1,0:T(8,128)S(1)}, f32[16,128]{1,0:T(8,128)S(1)}, u32[]{:S(2)}, u32[]{:S(2)}) collective-permute-start(f32[16,128]{1,0:T(8,128)S(1)} %get-tuple-element.37), channel_id=1, source_target_pairs={{0,8},{8,0},{16,24},{24,16},{1,9},{9,1},{17,25},{25,17},{2,10},{10... | collective-permute-start | bytes 24584 | tf_op jit(solution)/shard_map/ppermute | solution.py:395
  35.9 11.5 %collective-permute-start.2 = (bf16[64,2176]{1,0:T(8,128)(2,1)S(1)}, bf16[64,2176]{1,0:T(8,128)(2,1)S(1)}, u32[]{:S(2)}, u32[]{:S(2)}) collective-permute-start(bf16[64,2176]{1,0:T(8,128)(2,1)S(1)} %get-tuple-element.47.pack_ref), channel_id=1, source_target_pairs={{0,8},{8,0},{16,24},{24,16},{1,9},{9,1},{17,25},{25,17},{2,10},{10... | collective-permute-start | bytes 835592 | tf_op jit(solution)/shard_map/ppermute | solution.py:395

commit v9 on v6

--- a/solution.py
+++ b/solution.py
@@ -84,7 +84,7 @@
         acc = jnp.zeros((samples, LANES), F32)
         for j in range(2 * many):
             w = w_s[first + j // 2, (j % 2) * samples : (j % 2 + 1) * samples, :]
-            if j % 4 == 3:
+            if j % 3 == 2:
                 sums = dot_nn(w, ones)
             else:
                 w = w.astype(F32)

time: 68.6 us -> 68.7 us (level)
  no operation moved by 1% of the time
where the time goes in v9:
time: 68.7 us; the launch traced here: 68.5 us
  blocking collectives  54.1 us (79%)
  Pallas kernels  11.9 us (17%)
  waiting for transfers between devices  1 us (1%)
  starting transfers between devices  0.75 us (1%)
  between operations  0.73 us (1%)
    all_to_all x4, blocking collectives, exchange(): return lax.all_to_all(x, AXES, split_axis=0, concat_axis=0, tiled=True)  54.1 us
    pallas_call x1, Pallas kernels, body(): pl.pallas_call(functools.partial(bin_kernel, n_det, n_pix, group), out_sh...  7.73 us
    pallas_call x8, Pallas kernels, call(): pl.pallas_call(kernel, out_shape=outs, in_specs=[vmem] * len(args), out_s...  4.19 us
  transfers between devices with their start and end apart: 3, of which 2 were waited for; matrix products, arithmetic and copies ran while one was open for 0% of the time, Pallas kernels for 2%

profile of v9, /device:TPU:0, one launch (start us, length us, event | category | flops | bytes accessed | tf_op | source)
XLA Modules:
  0.0 68.5 jit_solution(17305557321494453100)
XLA Ops:
  0.6 0.0 copy-start.2
  0.6 0.0 copy-start
  0.7 0.0 copy-start.1
  0.7 0.0 copy-start.3
  0.7 7.7 %shard_map.68 = (bf16[32,32,128]{2,1,0:T(8,128)(2,1)S(1)}, f32[256,256]{1,0:T(8,128)S(1)}, f32[256,256]{1,0:T(8,128)S(1)}, f32[256,256]{1,0:T(8,128)S(1)}, bf16[256,512]{1,0:T(8,128)(2,1)S(1)}) custom-call(f32[1,256,128]{2,1,0:T(8,128)} %ts_ref.1, bf16[128,256,256]{2,1,0:T(8,128)(2,1)} %bitcast.4, s32[1,256]{1,0:T(1,128)} %bitcast.2, s32[1,256]{1,0:T(1,128)} %loc_ref.1), custom_call_target="tpu_custom_call" | custom-call | flops 100000000 | bytes 33554432 | tf_op jit(solution)/shard_map/pallas_call | solution.py:406
  8.4 0.5 collective-permute-start
  8.9 0.0 copy-done.2
  8.9 0.0 copy-done.1
  8.9 0.9 %shard_map.69 = (f32[32,32,128]{2,1,0:T(8,128)S(1)}, bf16[32,40,128]{2,1,0:T(8,128)(2,1)S(1)}) custom-call(f32[1,256,128]{2,1,0:T(8,128)S(1)} %copy-done, s32[1,256]{1,0:T(1,128)S(1)} %bitcast.3, s32[1,256]{1,0:T(1,128)S(1)} %copy-done.2, s32[1,256]{1,0:T(1,128)S(1)} %copy-done.3, f32[256,256]{1,0:T(8,128)S(1)} %get-tuple-element.26.hit_ref, ...), custom_call_target="tpu_custom_call" | custom-call | flops 100000000 | bytes 4000000 | tf_op jit(solution)/shard_map/pallas_call | solution.py:376
  9.9 0.2 collective-permute-done.took_ref
  10.1 0.1 shard_map.70
  10.2 24.8 %all_to_all.20.got_ref = bf16[32,72,128]{2,1,0:T(8,128)(2,1)S(1)} all-to-all(bf16[32,72,128]{2,1,0:T(8,128)(2,1)S(1)} %shard_map.70), channel_id=1, replica_groups=mesh['det'=4,'pix'=8] {'det','pix'}, dimensions={0} | all-to-all | bytes 1179648 | tf_op jit(solution)/shard_map/all_to_all | solution.py:388
  35.0 0.7 %shard_map.71 = (f32[16,128]{1,0:T(8,128)S(1)}, f32[16,128]{1,0:T(8,128)S(1)}, bf16[64,2176]{1,0:T(8,128)(2,1)S(1)}, bf16[64,2048]{1,0:T(8,128)(2,1)S(1)}, bf16[...) custom-call(bf16[32,72,128]{2,1,0:T(8,128)(2,1)S(1)} %all_to_all.20.got_ref), custom_call_target="tpu_custom_call" | custom-call | flops 100000000 | bytes 4000000 | tf_op jit(solution)/shard_map/pallas_call | solution.py:376
  35.7 0.1 collective-permute-start.1
  35.8 0.3 shard_map.72
  36.1 0.8 %collective-permute-done.1.took_ref = f32[16,128]{1,0:T(8,128)S(1)} collective-permute-done((f32[16,128]{1,0:T(8,128)S(1)}, f32[16,128]{1,0:T(8,128)S(1)}, u32[]{:S(2)}, u32[]{:S(2)}) %collective-permute-start.1) | collective-permute-done | bytes 8224 | tf_op jit(solution)/shard_map/ppermute | solution.py:392
  36.9 0.2 collective-permute-start.2
  37.1 9.8 %all_to_all.21.got_ref = bf16[32,16,128]{2,1,0:T(8,128)(2,1)S(1)} all-to-all(bf16[32,16,128]{2,1,0:T(8,128)(2,1)S(1)} %shard_map.73), channel_id=1, replica_groups=mesh['det'=4,'pix'=8] {'det','pix'}, dimensions={0} | all-to-all | bytes 262144 | tf_op jit(solution)/shard_map/all_to_all | solution.py:388
  46.9 0.0 collective-permute-done.2.other_ref
  46.9 0.8 %shard_map.74 = (bf16[32,16,128]{2,1,0:T(8,128)(2,1)S(1)}, f32[32,128]{1,0:T(8,128)S(1)}, f32[64,64]{1,0:T(8,128)S(1)}) custom-call(bf16[32,16,128]{2,1,0:T(8,128)(2,1)S(1)} %all_to_all.21.got_ref, bf16[64,2176]{1,0:T(8,128)(2,1)S(1)} %get-tuple-element.41.pack_ref, bf16[64,2176]{1,0:T(8,128)(2,1)S(1)} %collective-permute-done.2.other_ref, ...), custom_call_target="tpu_custom_call" | custom-call | flops 100000000 | bytes 4000000 | tf_op jit(solution)/shard_map/pallas_call | solution.py:376
  47.7 10.0 %all_to_all.22.got_ref = bf16[32,16,128]{2,1,0:T(8,128)(2,1)S(1)} all-to-all(bf16[32,16,128]{2,1,0:T(8,128)(2,1)S(1)} %get-tuple-element.44), channel_id=1, replica_groups=mesh['det'=4,'pix'=8] {'det','pix'}, dimensions={0} | all-to-all | bytes 262144 | tf_op jit(solution)/shard_map/all_to_all | solution.py:388
  57.7 0.7 %shard_map.75 = (f32[32,1,256]{2,1,0:T(1,128)S(1)}, f32[6,32,128]{2,1,0:T(8,128)S(1)}) custom-call(bf16[32,16,128]{2,1,0:T(8,128)(2,1)S(1)} %all_to_all.22.got_ref, bf16[64,2176]{1,0:T(8,128)(2,1)S(1)} %get-tuple-element.41.pack_ref, bf16[64,2048]{1,0:T(8,128)(2,1)S(1)} %get-tuple-element.36.pb_ref, bf16[128,2048]{1,0:T(8,128)(2,1)S(1)} %get-tuple-element.37.hot_ref, ...), custom_call_target="tpu_custom_call" | custom-call | flops 100000000 | bytes 4000000 | tf_op jit(solution)/shard_map/pallas_call | solution.py:376
  58.5 9.4 %all_to_all.23.got_ref = f32[32,1,256]{2,1,0:T(1,128)S(1)} all-to-all(f32[32,1,256]{2,1,0:T(1,128)S(1)} %get-tuple-element.48), channel_id=1, replica_groups=mesh['det'=4,'pix'=8] {'det','pix'}, dimensions={0} | all-to-all | bytes 65536 | tf_op jit(solution)/shard_map/all_to_all | solution.py:388
  67.9 0.6 shard_map.76
  (3 shorter events, 0.0 us)
Async XLA Ops:
  0.6 8.3 %copy-start.2 = (s32[1,256]{1,0:T(1,128)S(1)}, s32[1,256]{1,0:T(1,128)}, u32[]{:S(2)}) copy-start(s32[1,256]{1,0:T(1,128)} %loc_ref.1) | copy-start | bytes 3076
  0.6 8.3 %copy-start = (f32[1,256,128]{2,1,0:T(8,128)S(1)}, f32[1,256,128]{2,1,0:T(8,128)}, u32[]{:S(2)}) copy-start(f32[1,256,128]{2,1,0:T(8,128)} %ts_ref.1) | copy-start | bytes 393220
  0.7 8.3 %copy-start.1 = (s32[1,256,1]{1,2,0:T(1,128)S(1)}, s32[1,256,1]{1,2,0:T(1,128)}, u32[]{:S(2)}) copy-start(s32[1,256,1]{1,2,0:T(1,128)} %param.7) | copy-start | bytes 3076
  0.7 8.3 %copy-start.3 = (s32[1,256]{1,0:T(1,128)S(1)}, s32[1,256]{1,0:T(1,128)}, u32[]{:S(2)}) copy-start(s32[1,256]{1,0:T(1,128)} %base_ref.1) | copy-start | bytes 3076
  8.4 1.7 %collective-permute-start = (bf16[32,32,128]{2,1,0:T(8,128)(2,1)S(1)}, bf16[32,32,128]{2,1,0:T(8,128)(2,1)S(1)}, u32[]{:S(2)}, u32[]{:S(2)}) collective-permute-start(bf16[32,32,128]{2,1,0:T(8,128)(2,1)S(1)} %get-tuple-element.31), channel_id=1, source_target_pairs={{0,8},{8,0},{16,24},{24,16},{1,9},{9,1},{17,25},{25,17},{2,10},{10... | collective-permute-start | bytes 786440 | tf_op jit(solution)/shard_map/ppermute | solution.py:392
  35.7 1.2 %collective-permute-start.1 = (f32[16,128]{1,0:T(8,128)S(1)}, f32[16,128]{1,0:T(8,128)S(1)}, u32[]{:S(2)}, u32[]{:S(2)}) collective-permute-start(f32[16,128]{1,0:T(8,128)S(1)} %get-tuple-element.34), channel_id=1, source_target_pairs={{0,8},{8,0},{16,24},{24,16},{1,9},{9,1},{17,25},{25,17},{2,10},{10... | collective-permute-start | bytes 24584 | tf_op jit(solution)/shard_map/ppermute | solution.py:392
  36.9 10.0 %collective-permute-start.2 = (bf16[64,2176]{1,0:T(8,128)(2,1)S(1)}, bf16[64,2176]{1,0:T(8,128)(2,1)S(1)}, u32[]{:S(2)}, u32[]{:S(2)}) collective-permute-start(bf16[64,2176]{1,0:T(8,128)(2,1)S(1)} %get-tuple-element.41.pack_ref), channel_id=1, source_target_pairs={{0,8},{8,0},{16,24},{24,16},{1,9},{9,1},{17,25},{25,17},{2,10},{10... | collective-permute-start | bytes 835592 | tf_op jit(solution)/shard_map/ppermute | solution.py:392
